TPU v7x, 32 devices: a whole 2x2x4 slice. The times are simulated.
32 devices in a mesh: cd: 8 (over y, x, core), ab: 4 (over z).
Axes of the slice: x: 2, y: 2, z: 4, core: 2. Of those that a mesh axis runs over, the one named last changes fastest.
Arguments:
- amplitudes: float32 [1024, 16384], P('ab', 'cd'), may hold values from -6 to 6
- integrals: float32 [16384, 4096], P('cd', 'ab'), may hold values from -0.046875 to 0.046875
- live_tiles: int32 [64], P('cd'), may hold values from 0 to 1, as said below
- residual_in: float32 [1024, 4096], P(('ab', 'cd')), may hold values from -6 to 6
Outputs:
- residual_out: float32 [1024, 4096], P(('ab', 'cd'))
Inputs may be any that keep to these rules, and one draw needn't show every extreme that they name: live_tiles[t] is 1 where tile t of 256 contracted pairs carries integrals and 0 where it is screened out; the 8 tiles of each index of cd hold at least one live tile.
All inputs are finite; a program needn't handle non-finite values.
Results may differ from a plain program's by a relative error of at most 0.0001.
Values sent between devices are 32-bit elements; how exact they have to be, the bound alone decides.
No kernel may reach another device: no remote copies, remote signals or barrier semaphores. Data moves between devices by JAX's collectives and lax.ppermute only.
A program may use at most 128 MiB of HBM per device.

v0:
```python
import jax
import jax.numpy as jnp
from jax import lax
from jax.sharding import PartitionSpec as P

TILE = 256


def dense_product(left_part, right_part, live_tiles, tile_size):
    weights = jnp.repeat(
        live_tiles.astype(jnp.float32), tile_size, total_repeat_length=right_part.shape[0]
    )
    return jnp.dot(
        left_part,
        right_part * weights[:, None],
        preferred_element_type=jnp.float32,
        precision=lax.Precision.HIGHEST,
    )


def per_device(amplitudes, integrals, live_tiles, residual_in):
    tile_size = TILE
    count_ab = lax.axis_size("ab")
    count_cd = lax.axis_size("cd")
    out_rows = residual_in.shape[0]
    partial_sum = dense_product(
        lax.all_gather(amplitudes, "ab", axis=0, tiled=True), integrals, live_tiles, tile_size
    )
    columns_dev = partial_sum.shape[1]
    ordered = partial_sum.reshape(count_ab, count_cd, out_rows, columns_dev).transpose(1, 0, 2, 3)
    ordered = ordered.reshape(count_cd * count_ab * out_rows, columns_dev)
    reduced = lax.psum_scatter(ordered, "cd", scatter_dimension=0, tiled=True)
    placed = lax.all_to_all(
        reduced.reshape(count_ab, out_rows, columns_dev),
        "ab",
        split_axis=0,
        concat_axis=2,
        tiled=True,
    )
    ladder = placed.reshape(out_rows, count_ab * columns_dev)
    return residual_in + ladder


def solution(mesh):
    return jax.shard_map(
        per_device,
        mesh=mesh,
        in_specs=(P("ab", "cd"), P("cd", "ab"), P("cd"), P(("ab", "cd"), None)),
        out_specs=P(("ab", "cd"), None),
        check_vma=False,
    )
```

profile of v0, /device:TPU:0, one launch (start us, length us, event | category | flops | bytes accessed | tf_op | source)
XLA Modules:
  0.0 273.9 jit_solution(9227287666794944699)
XLA Ops:
  6.5 0.0 all-gather.2.cloned.1.call-start
  6.5 0.7 all-gather.2.cloned.1.call-update
  7.3 0.0 reduce-scatter.2.cloned.1.call-start
  7.3 0.7 convert_element_type.3
  8.0 0.7 fusion.3
  8.6 5.9 %select_select_fusion = f32[2048]{0:T(1024)S(1)} fusion(pred[2048]{0:T(1024)(128)(4,1)} %constant.107, pred[2048]{0:T(1024)(128)(4,1)} %constant.108, pred[2048]{0:T(1024)(128)(4,1)} %constant.109, pred[2048]{0:T(1024)(128)(4,1)} %constant.110, pred[2048]{0:T(1024)(128)(4,1)} %constant.111, pred[2048]{0:T(1024)(128)(4,1)} %constant.112, ...), kind=kLoop, calls=%fused_computation.3 | loop fusion | flops 14336 | bytes 22560 | tf_op jit(solution)/shard_map/jit(_take)/gather | solution.py:10
  14.5 146.8 %all-gather.2.cloned.1.call-done = f32[1024,2048]{1,0:T(8,128)} async-done(((f32[256,2048]{1,0:T(8,128)}), f32[1024,2048]{1,0:T(8,128)}) %all-gather.2.cloned.1.call-update) | async-done | bytes 8388624 | tf_op jit(solution)/shard_map/all_gather | solution.py:27
  161.3 33.1 %fusion = f32[1024,1024]{0,1:T(8,128)S(1)} fusion(f32[1024,2048]{1,0:T(8,128)} %all-gather.2.cloned.1.call-done, f32[2048,1024]{1,0:T(8,128)} %param.7, f32[2048]{0:T(1024)S(1)} %select_select_fusion), kind=kOutput, calls=%fused_computation | convolution fusion | flops 25771900928 | bytes 20979712 | tf_op jit(solution)/shard_map/dot_general | solution.py:13
  194.4 0.0 copy-start
  194.5 2.2 copy.6
  196.7 0.0 reduce-scatter.2.cloned.1.call-update
  196.7 49.7 %reduce-scatter.2.cloned.1.call-done = f32[128,1024]{1,0:T(8,128)} async-done(((f32[1024,1024]{1,0:T(8,128)}), f32[128,1024]{1,0:T(8,128)}) %reduce-scatter.2.cloned.1.call-update) | async-done | bytes 524304 | tf_op jit(solution)/shard_map/reduce_scatter | solution.py:32
  246.4 19.1 %all_to_all.15 = f32[4,32,1024]{2,1,0:T(8,128)S(1)} all-to-all(f32[4,32,1024]{2,1,0:T(8,128)} %bitcast.27), channel_id=1, replica_groups=mesh['cd'=8,'ab'=4] {'ab'}, dimensions={0} | all-to-all | bytes 1048576 | tf_op jit(solution)/shard_map/all_to_all | solution.py:33
  265.5 0.3 copy.7
  265.9 0.3 copy.8
  266.2 0.0 copy-done
  266.2 0.9 add.42
Async XLA Ops:
  6.5 154.8 %all-gather.2.cloned.1.call-start = ((), (), s32[]{:S(2)}) async-start(), calls=%async_computation.2 | async-start | bytes 10485760 | tf_op jit(solution)/shard_map/all_gather | solution.py:27
  7.3 239.2 %reduce-scatter.2.cloned.1.call-start = ((), (), s32[]{:S(2)}) async-start(), calls=%async_computation.3 | async-start | bytes 4718592 | tf_op jit(solution)/shard_map/reduce_scatter | solution.py:32
  194.4 71.8 %copy-start = (f32[32,4096]{1,0:T(8,128)S(1)}, f32[32,4096]{1,0:T(8,128)}, u32[]{:S(2)}) copy-start(f32[32,4096]{1,0:T(8,128)} %param.9) | copy-start | bytes 1572868
Sparse Core Ops, SparseCore 0:
  8.9 152.3 all-gather.1
  196.8 49.5 reduce-scatter.1
where the time goes:
time: 274 us
  waiting for transfers between devices  197 us (72%)
  matrix products  33.1 us (12%)
  blocking collectives  19.1 us (7%)
  between operations  13.4 us (5%)
  other arithmetic  7.39 us (3%)
  local copies, waits for them, and re-layouts  3.55 us (1%)
    all_gather x1, waiting for transfers between devices, per_device(): lax.all_gather(amplitudes, 'ab', axis=0, tiled=True)  147 us
    reduce_scatter x1, waiting for transfers between devices, per_device(): reduced = lax.psum_scatter(ordered, 'cd', scatter_dimension=0, tiled=True)  49.7 us
    dot_general x1, matrix products, dense_product(): jnp.dot(left_part, right_part * weights[:, None], preferred_element_type=...  33.1 us
    all_to_all x1, blocking collectives, per_device(): lax.all_to_all(reduced.reshape(count_ab, out_rows, columns_dev), 'ab', sp...  19.1 us
    gather x1, other arithmetic, dense_product(): jnp.repeat(live_tiles.astype(jnp.float32), tile_size, total_repeat_length...  5.85 us
  transfers between devices with their start and end apart: 2, of which 2 were waited for; matrix products, arithmetic and copies ran while one was open for 3% of the time, Pallas kernels for 0%

commit v1 on v0

v1 whole, which is shorter than its diff:
```python
import functools

import jax
import jax.numpy as jnp
from jax import lax
from jax.experimental import pallas as pl
from jax.experimental.pallas import tpu as pltpu
from jax.sharding import PartitionSpec as P

TILE = 256
MIB = 1 << 20


def split(x):
    high = x.astype(jnp.bfloat16)
    return high, (x - high.astype(jnp.float32)).astype(jnp.bfloat16)


def multiply_add(out_ref, left, high, low):
    left_high, left_low = split(left)
    dot = functools.partial(jnp.dot, preferred_element_type=jnp.float32)
    both = dot(jnp.concatenate([left_high, left_low]), high)
    rows = left.shape[0]
    out_ref[...] += both[:rows] + (both[rows:] + dot(left_high, low))


def first_kernel(live, left_ref, right_ref, out_ref, high_ref, low_ref):
    step = pl.program_id(0)

    @pl.when(step == 0)
    def _():
        out_ref[...] = jnp.zeros_like(out_ref)

    @pl.when(live[step] > 0)
    def _():
        high_ref[0], low_ref[0] = split(right_ref[0])
        multiply_add(out_ref, left_ref[...], high_ref[0], low_ref[0])


def first_product(left, right, live):
    rows = left.shape[0]
    steps, _, columns = right.shape
    tile = pl.BlockSpec((1, TILE, columns), lambda step, live: (step, 0, 0))
    halved = jax.ShapeDtypeStruct(right.shape, jnp.bfloat16)
    return pl.pallas_call(
        first_kernel,
        out_shape=(jax.ShapeDtypeStruct((rows, columns), jnp.float32), halved, halved),
        grid_spec=pltpu.PrefetchScalarGridSpec(
            num_scalar_prefetch=1,
            grid=(steps,),
            in_specs=[pl.BlockSpec((rows, TILE), lambda step, live: (0, step)), tile],
            out_specs=(pl.BlockSpec((rows, columns), lambda step, live: (0, 0)), tile, tile),
        ),
        compiler_params=pltpu.CompilerParams(vmem_limit_bytes=16 * MIB),
        cost_estimate=pl.CostEstimate(
            flops=2 * rows * TILE * columns * steps,
            bytes_accessed=4 * rows * (steps * TILE + columns),
            transcendentals=0,
        ),
    )(live, left, right)


def product_kernel(layout, first, scalars, *refs):
    count = len(layout)
    left_refs, (high_ref, low_ref, out_ref, *lefts) = refs[: sum(layout)], refs[sum(layout) :]
    lefts, (high, low, left_sems, sems) = lefts[:count], lefts[count:]
    steps = high.shape[0]

    left_copies = []
    for i, candidates in enumerate(layout):
        here, left_refs = left_refs[:candidates], left_refs[candidates:]
        copies = [pltpu.make_async_copy(ref, lefts[i], left_sems.at[i]) for ref in here]
        if candidates == 1:
            copies[0].start()
        else:
            for which, copy in enumerate(copies):
                pl.when(scalars[0] == which)(copy.start)
        left_copies.append(copies[0])
    right_copies = []
    for step in range(steps):
        pairs = (high_ref, high), (low_ref, low)
        right_copies.append(
            [
                pltpu.make_async_copy(source.at[first + step], target.at[step], sems.at[i, step])
                for i, (source, target) in enumerate(pairs)
            ]
        )
        for copy in right_copies[-1]:
            copy.start()
    out_ref[...] = jnp.zeros_like(out_ref)

    step = 0
    for i, left in enumerate(lefts):
        left_copies[i].wait()
        for tile in range(left.shape[1] // TILE):
            for copy in right_copies[step]:
                copy.wait()

            @pl.when(scalars[1 + step] > 0)
            def _():
                left_tile = left[:, tile * TILE : (tile + 1) * TILE]
                multiply_add(out_ref, left_tile, high[step], low[step])

            step += 1


def product(lists, which, right, live, first=0):
    rows, columns = lists[0][0].shape[0], right[0].shape[2]
    widths = [candidates[0].shape[1] for candidates in lists]
    steps = sum(widths) // TILE
    lefts = [x for candidates in lists for x in candidates]
    anywhere, hbm = (pl.BlockSpec(memory_space=space) for space in (pl.ANY, pltpu.HBM))
    return pl.pallas_call(
        functools.partial(product_kernel, [len(candidates) for candidates in lists], first),
        out_shape=jax.ShapeDtypeStruct((rows, columns), jnp.float32),
        in_specs=[pl.BlockSpec(memory_space=pltpu.SMEM)] + [anywhere] * len(lefts) + [hbm] * 2,
        out_specs=pl.BlockSpec(memory_space=pltpu.VMEM),
        scratch_shapes=[pltpu.VMEM((rows, width), jnp.float32) for width in widths]
        + [
            pltpu.VMEM((steps, TILE, columns), jnp.bfloat16),
            pltpu.VMEM((steps, TILE, columns), jnp.bfloat16),
            pltpu.SemaphoreType.DMA((len(lists),)),
            pltpu.SemaphoreType.DMA((2, steps)),
        ],
        compiler_params=pltpu.CompilerParams(vmem_limit_bytes=52 * MIB),
        cost_estimate=pl.CostEstimate(
            flops=2 * rows * TILE * columns * steps,
            bytes_accessed=4 * rows * (steps * TILE + columns),
            transcendentals=0,
        ),
    )(jnp.concatenate([jnp.int32(which)[None], live[first : first + steps]]), *lefts, *right)


def cut(left, tiles):
    kept = (tiles - tiles // 4) * TILE
    return [left[:, :kept], left[:, kept:]]


def take(blocks, at, axis):
    return lax.dynamic_index_in_dim(blocks, at, axis, keepdims=False)


def halve(blocks, axis, bit):
    mine = (lax.axis_index("cd") >> bit) & 1
    pairs = [(i, i ^ (1 << bit)) for i in range(lax.axis_size("cd"))]
    return take(blocks, mine, axis) + lax.ppermute(take(blocks, 1 - mine, axis), "cd", pairs)


def core_sum(partial_rows):
    count = lax.axis_size("cd")
    rows, columns = partial_rows.shape
    return halve(partial_rows.reshape(count // 2, 2, rows // count, columns), 1, 0)


def chip_sum(blocks):
    bit = 1
    while blocks.shape[0] > 1:
        chips, rows, columns = blocks.shape
        blocks = halve(blocks.reshape(chips // 2, 2, rows, columns), 1, bit)
        bit += 1
    return blocks[0]


def chip_sum_direct(blocks):
    chip, count = lax.axis_index("cd") // 2, lax.axis_size("cd")
    total = take(blocks, chip, 0)
    for flip in range(1, blocks.shape[0]):
        pairs = [(i, i ^ (2 * flip)) for i in range(count)]
        total += lax.ppermute(take(blocks, chip ^ flip, 0), "cd", pairs)
    return total


def send(x, pairs):
    return lax.ppermute(x, "ab", pairs)


def after(*values):
    return lax.optimization_barrier(values)


def ladder_any(amplitudes, live, right):
    count = lax.axis_size("ab")
    first, *split_right = first_product(amplitudes, right, live)
    home = [chip_sum(core_sum(first))]
    for flip in range(1, count):
        pairs = [(i, i ^ flip) for i in range(count)]
        lists = [[send(x, pairs)] for x in cut(amplitudes, live.shape[0])]
        partial_rows = product(lists, 0, split_right, live)
        home.append(send(chip_sum(core_sum(partial_rows)), pairs))
    return [take(jnp.stack(home), lax.axis_index("ab") ^ i, 0) for i in range(count)]


def ladder_line(amplitudes, live, right):
    at = lax.axis_index("ab")
    inner = ((at == 1) | (at == 2)).astype(jnp.int32)
    swap_1 = [(0, 1), (1, 0), (2, 3), (3, 2)]
    swap_2 = [(0, 2), (2, 0), (1, 3), (3, 1)]
    swap_3 = [(0, 3), (3, 0), (1, 2), (2, 1)]
    swap_inner, to_end = [(1, 2), (2, 1)], [(1, 0), (2, 3)]
    lists = cut(amplitudes, live.shape[0])
    kept = lists[0].shape[1] // TILE

    one = [send(x, swap_1) for x in lists]
    three_inner = [send(x, swap_inner) for x in lists]
    two_inner = [send(x, swap_inner) for x in one]
    two_end = [send(x, to_end) for x in three_inner]
    three_end = [send(x, to_end) for x in two_inner]

    first, *split_right = first_product(amplitudes, right, live)
    sum_0 = core_sum(first)

    one[0], three_inner[0], sum_0 = after(one[0], three_inner[0], sum_0)
    one[1], three_inner[1], sum_0 = after(one[1], three_inner[1], sum_0)
    sum_1 = core_sum(product([[x] for x in one], 0, split_right, live))
    home_0 = chip_sum(sum_0)

    two_end[0], two_inner[0], home_0, sum_1 = after(two_end[0], two_inner[0], home_0, sum_1)
    two_end[1], two_inner[1], sum_1 = after(two_end[1], two_inner[1], sum_1)
    candidates = [list(pair) for pair in zip(two_end, two_inner)]
    sum_2 = core_sum(product(candidates, inner, split_right, live))
    sum_1 = chip_sum(sum_1)

    three_end[0], sum_1, sum_2 = after(three_end[0], sum_1, sum_2)
    candidates = [[three_end[0], three_inner[0]]]
    partial_3 = product(candidates, inner, split_right, live)
    sum_2 = chip_sum_direct(sum_2)
    home_1 = send(sum_1, swap_1)

    three_end[1], partial_3, sum_2, home_1 = after(three_end[1], partial_3, sum_2, home_1)
    candidates = [[three_end[1], three_inner[1]]]
    partial_3 += product(candidates, inner, split_right, live, kept)
    sum_3 = chip_sum_direct(core_sum(partial_3))
    home_2 = send(sum_2, swap_2)

    home_2, sum_3 = after(home_2, sum_3)
    home = jnp.stack([home_0, home_1, home_2, send(sum_3, swap_3)])
    return [take(home, at ^ i, 0) for i in range(4)]


def per_device(amplitudes, integrals, live_tiles, residual_in):
    right = integrals.reshape(live_tiles.shape[0], TILE, integrals.shape[1])
    ladder = ladder_line if lax.axis_size("ab") == 4 else ladder_any
    return residual_in + jnp.concatenate(ladder(amplitudes, live_tiles, right), axis=1)


def solution(mesh):
    return jax.shard_map(
        per_device,
        mesh=mesh,
        in_specs=(P("ab", "cd"), P("cd", "ab"), P("cd"), P(("ab", "cd"), None)),
        out_specs=P(("ab", "cd"), None),
        check_vma=False,
    )
```

time: 274 us -> 172 us (0.63)
  waiting for transfers between devices: 197 us -> 86.7 us
  starting transfers between devices: 0.04 us -> 37.9 us
  matrix products: 33.1 us -> 0 us
  Pallas kernels: 0 us -> 24 us
  blocking collectives: 19.1 us -> 0 us
  between operations: 13.4 us -> 0.33 us
  local copies, waits for them, and re-layouts: 3.55 us -> 15 us
    all_gather x1 -> x0, waiting for transfers between devices: 147 us -> none  [per_device(): lax.all_gather(amplitudes, 'ab', axis=0, tiled=True)]
    ppermute x0 -> x27, waiting for transfers between devices: none -> 86.7 us  [the longest x13 74.2 us: send(): return lax.ppermute(x, 'ab', pairs)]
    reduce_scatter x1 -> x0, waiting for transfers between devices: 49.7 us -> none  [per_device(): reduced = lax.psum_scatter(ordered, 'cd', scatter_dimension=0, tiled=True)]
    ppermute x0 -> x27, starting transfers between devices: none -> 37.9 us  [the longest x13 22.1 us: send(): return lax.ppermute(x, 'ab', pairs)]
    dot_general x1 -> x0, matrix products: 33.1 us -> none  [dense_product(): jnp.dot(left_part, right_part * weights[:, None], preferred_element_type=...]
    pallas_call x0 -> x5, Pallas kernels: none -> 24 us  [the longest x4 20.7 us: product(): pl.pallas_call(functools.partial(product_kernel, [len(candidates) for can...]
    all_to_all x1 -> x0, blocking collectives: 19.1 us -> none  [per_device(): lax.all_to_all(reduced.reshape(count_ab, out_rows, columns_dev), 'ab', sp...]
    unnamed x3 -> x18, local copies, waits for them, and re-layouts: 0.31 us -> 7.41 us
  transfers between devices with their start and end apart: 2 -> 27, of which waited for: 2 -> 14; matrix products, arithmetic and copies ran while one was open for 3% -> 6% of each run, Pallas kernels for 0% -> 12%
where the time goes in v1:
time: 172 us
  waiting for transfers between devices  86.7 us (50%)
  starting transfers between devices  37.9 us (22%)
  Pallas kernels  24 us (14%)
  local copies, waits for them, and re-layouts  15 us (9%)
  other arithmetic  7.93 us (5%)
    ppermute x13, waiting for transfers between devices, send(): return lax.ppermute(x, 'ab', pairs)  74.2 us
    ppermute x13, starting transfers between devices, send(): return lax.ppermute(x, 'ab', pairs)  22.1 us
    pallas_call x4, Pallas kernels, product(): pl.pallas_call(functools.partial(product_kernel, [len(candidates) for can...  20.7 us
    ppermute x8, starting transfers between devices, halve(): lax.ppermute(take(blocks, 1 - mine, axis), 'cd', pairs)  8.33 us
    ppermute x8, waiting for transfers between devices, halve(): lax.ppermute(take(blocks, 1 - mine, axis), 'cd', pairs)  8.22 us
    ppermute x6, starting transfers between devices, chip_sum_direct(): total += lax.ppermute(take(blocks, chip ^ flip, 0), 'cd', pairs)  7.42 us
    unnamed x18, local copies, waits for them, and re-layouts  7.41 us
    add x6, other arithmetic, halve(): take(blocks, mine, axis)  4.43 us
  transfers between devices with their start and end apart: 27, of which 14 were waited for; matrix products, arithmetic and copies ran while one was open for 6% of the time, Pallas kernels for 12%

profile of v1, /device:TPU:0, one launch (start us, length us, event | category | flops | bytes accessed | tf_op | source)
XLA Modules:
  0.0 171.9 jit_solution(3051622022812870785)
XLA Ops:
  0.0 2.8 %slice.12 = f32[256,1536]{1,0:T(8,128)} slice(f32[256,2048]{1,0:T(8,128)} %left_ref.1), slice={[0:256], [0:1536]} | slice | bytes 3145728 | tf_op jit(solution)/shard_map/slice | solution.py:136
  2.8 3.0 %collective-permute-start.2 = (f32[256,1536]{1,0:T(8,128)}, f32[256,1536]{1,0:T(8,128)}, u32[]{:S(2)}, u32[]{:S(2)}) collective-permute-start(f32[256,1536]{1,0:T(8,128)} %slice.12), channel_id=1, source_target_pairs={{0,1},{1,0},{2,3},{3,2},{4,5},{5,4},{6,7},{7,6},{8,9},{9,8},{10,11... | collective-permute-start | bytes 4718600 | tf_op jit(solution)/shard_map/ppermute | solution.py:174
  5.9 1.8 %collective-permute-start = (f32[256,1536]{1,0:T(8,128)}, f32[256,1536]{1,0:T(8,128)}, u32[]{:S(2)}, u32[]{:S(2)}) collective-permute-start(f32[256,1536]{1,0:T(8,128)} %slice.12), channel_id=1, source_target_pairs={{1,2},{2,1},{5,6},{6,5},{9,10},{10,9},{13,14},{14,13},{17,18},{18,... | collective-permute-start | bytes 4718600 | tf_op jit(solution)/shard_map/ppermute | solution.py:174
  7.7 3.4 %copy-done.2 = f32[2048,1024]{1,0:T(8,128)S(1)} copy-done((f32[2048,1024]{1,0:T(8,128)S(1)}, f32[2048,1024]{1,0:T(8,128)}, u32[]{:S(2)}) %copy-start.2) | copy-done | bytes 8388632
  11.1 3.3 %shard_map.46 = (f32[256,1024]{1,0:T(8,128)S(1)}, bf16[8,256,1024]{2,1,0:T(8,128)(2,1)S(1)}, bf16[8,256,1024]{2,1,0:T(8,128)(2,1)S(1)}) custom-call(s32[8]{0:T(128)S(1)} %copy-done.4, f32[256,2048]{1,0:T(8,128)S(1)} %copy-done.3, f32[8,256,1024]{2,1,0:T(8,128)S(1)} %bitcast.73), custom_call_target="tpu_custom_call" | custom-call | flops 1073741824 | bytes 3145728 | tf_op jit(solution)/shard_map/pallas_call | solution.py:45
  14.4 2.0 %copy-done = bf16[8,256,1024]{2,1,0:T(8,128)(2,1)} copy-done((bf16[8,256,1024]{2,1,0:T(8,128)(2,1)}, bf16[8,256,1024]{2,1,0:T(8,128)(2,1)S(1)}, u32[]{:S(2)}) %copy-start) | copy-done | bytes 4194328
  16.4 2.0 %copy-done.1 = bf16[8,256,1024]{2,1,0:T(8,128)(2,1)} copy-done((bf16[8,256,1024]{2,1,0:T(8,128)(2,1)}, bf16[8,256,1024]{2,1,0:T(8,128)(2,1)S(1)}, u32[]{:S(2)}) %copy-start.1) | copy-done | bytes 4194328
  20.1 3.2 %collective-permute-start.4 = (f32[256,512]{1,0:T(8,128)}, f32[256,512]{1,0:T(8,128)S(1)}, u32[]{:S(2)}, u32[]{:S(2)}) collective-permute-start(f32[256,512]{1,0:T(8,128)} %slice.13), channel_id=1, source_target_pairs={{0,1},{1,0},{2,3},{3,2},{4,5},{5,4},{6,7},{7,6},{8,9},{9,8},{10,11... | collective-permute-start | bytes 1572872 | tf_op jit(solution)/shard_map/ppermute | solution.py:174
  24.0 17.3 %collective-permute-done.2.refs_0_ = f32[256,1536]{1,0:T(8,128)} collective-permute-done((f32[256,1536]{1,0:T(8,128)}, f32[256,1536]{1,0:T(8,128)}, u32[]{:S(2)}, u32[]{:S(2)}) %collective-permute-start.2) | collective-permute-done | bytes 1572896 | tf_op jit(solution)/shard_map/ppermute | solution.py:174
  41.4 1.8 %collective-permute-start.3 = (f32[256,1536]{1,0:T(8,128)}, f32[256,1536]{1,0:T(8,128)}, u32[]{:S(2)}, u32[]{:S(2)}) collective-permute-start(f32[256,1536]{1,0:T(8,128)} %collective-permute-done.2.refs_0_), channel_id=1, source_target_pairs={{1,2},{2,1},{5,6},{6,5},{9,10},{10,9},{13,14},{14,13},{17,18},{18,... | collective-permute-start | bytes 4718600 | tf_op jit(solution)/shard_map/ppermute | solution.py:174
  43.2 1.3 collective-permute-start.1
  44.5 1.1 bitcast_add_fusion.3
  45.6 6.9 %collective-permute-done.4.refs_1_ = f32[256,512]{1,0:T(8,128)S(1)} collective-permute-done((f32[256,512]{1,0:T(8,128)}, f32[256,512]{1,0:T(8,128)S(1)}, u32[]{:S(2)}, u32[]{:S(2)}) %collective-permute-start.4) | collective-permute-done | bytes 524320 | tf_op jit(solution)/shard_map/ppermute | solution.py:174
  52.5 2.0 %collective-permute-start.7 = (f32[2,32,1024]{2,1,0:T(8,128)S(1)}, f32[2,32,1024]{2,1,0:T(8,128)}, u32[]{:S(2)}, u32[]{:S(2)}) collective-permute-start(f32[2,32,1024]{2,1,0:T(8,128)S(1)} %dynamic-slice_bitcast_fusion.5), channel_id=1, source_target_pairs={{0,8},{4,12},{8,0},{12,4},{16,24},{20,28},{24,16},{28,20},{1,9},{5... | collective-permute-start | bytes 786440 | tf_op jit(solution)/shard_map/ppermute | solution.py:146
  54.7 5.4 %shard_map.47 = f32[256,1024]{1,0:T(8,128)S(1)} custom-call(s32[9]{0:T(128)S(1)} %get-tuple-element.66.scalars, f32[256,1536]{1,0:T(8,128)} %collective-permute-done.2.refs_0_, f32[256,512]{1,0:T(8,128)S(1)} %collective-permute-done.4.refs_1_, bf16[8,256,1024]{2,1,0:T(8,128)(2,1)} %copy-done, bf16[8,256,1024]{2,1,0:T(8,128)(2,1)} %copy-done.1), custom_call_target="tpu_custom_call" | custom-call | flops 1073741824 | bytes 3145728 | tf_op jit(solution)/shard_map/pallas_call | solution.py:113
  60.9 1.0 bitcast_add_fusion.5
  61.9 2.1 %collective-permute-start.8 = (f32[1,32,1024]{2,1,0:T(8,128)S(1)}, f32[1,32,1024]{2,1,0:T(8,128)}, u32[]{:S(2)}, u32[]{:S(2)}) collective-permute-start(f32[1,32,1024]{2,1,0:T(8,128)S(1)} %constant_dynamic-slice_fusion.1), channel_id=1, source_target_pairs={{0,16},{4,20},{8,24},{12,28},{16,0},{20,4},{24,8},{28,12},{1,17},{... | collective-permute-start | bytes 393224 | tf_op jit(solution)/shard_map/ppermute | solution.py:146
  64.7 3.6 %collective-permute-done.8 = f32[1,32,1024]{2,1,0:T(8,128)} collective-permute-done((f32[1,32,1024]{2,1,0:T(8,128)S(1)}, f32[1,32,1024]{2,1,0:T(8,128)}, u32[]{:S(2)}, u32[]{:S(2)}) %collective-permute-start.8) | collective-permute-done | bytes 131104 | tf_op jit(solution)/shard_map/ppermute | solution.py:146
  68.3 1.3 collective-permute-start.13
  69.5 0.9 add_bitcast_fusion.1
  70.5 1.3 collective-permute-start.12
  71.8 1.1 bitcast_add_fusion.2
  72.9 13.4 %collective-permute-done.1.refs_0_ = f32[256,1536]{1,0:T(8,128)} collective-permute-done((f32[256,1536]{1,0:T(8,128)}, f32[256,1536]{1,0:T(8,128)}, u32[]{:S(2)}, u32[]{:S(2)}) %collective-permute-start.1) | collective-permute-done | bytes 1572896 | tf_op jit(solution)/shard_map/ppermute | solution.py:174
  86.3 11.1 %collective-permute-done.13.refs_2_ = f32[256,512]{1,0:T(8,128)S(1)} collective-permute-done((f32[256,512]{1,0:T(8,128)S(1)}, f32[256,512]{1,0:T(8,128)S(1)}, u32[]{:S(2)}, u32[]{:S(2)}) %collective-permute-start.13) | collective-permute-done | bytes 524320 | tf_op jit(solution)/shard_map/ppermute | solution.py:174
  97.5 2.0 %collective-permute-start.14 = (f32[2,32,1024]{2,1,0:T(8,128)S(1)}, f32[2,32,1024]{2,1,0:T(8,128)S(1)}, u32[]{:S(2)}, u32[]{:S(2)}) collective-permute-start(f32[2,32,1024]{2,1,0:T(8,128)S(1)} %dynamic-slice_bitcast_fusion.4), channel_id=1, source_target_pairs={{0,8},{4,12},{8,0},{12,4},{16,24},{20,28},{24,16},{28,20},{1,9},{5... | collective-permute-start | bytes 786440 | tf_op jit(solution)/shard_map/ppermute | solution.py:146
  99.5 6.3 %shard_map.48 = f32[256,1024]{1,0:T(8,128)} custom-call(s32[9]{0:T(128)S(1)} %get-tuple-element.65.scalars, f32[256,1536]{1,0:T(8,128)} %collective-permute-done.1.refs_0_, f32[256,1536]{1,0:T(8,128)} %collective-permute-done.3.refs_1_, f32[256,512]{1,0:T(8,128)S(1)} %collective-permute-done.13.refs_2_, f32[256,512]{1,0:T(8,128)S(1)} %collective-permute-done.10.refs_3_, ...), custom_call_target="tpu_custom_call" | custom-call | flops 1073741824 | bytes 3145728 | tf_op jit(solution)/shard_map/pallas_call | solution.py:113
  105.9 2.0 %dynamic-slice_bitcast_fusion.1 = f32[4,32,1024]{2,1,0:T(8,128)} fusion(f32[4,2,32,1024]{3,2,1,0:T(8,128)} %bitcast.81, s32[]{:T(128)S(6)} %select_n.67), kind=kLoop, calls=%fused_computation.7 | loop fusion | bytes 1048580 | tf_op jit(solution)/shard_map/jit(dynamic_index_in_dim)/squeeze | solution.py:140
  107.9 2.1 %collective-permute-start.15 = (f32[1,32,1024]{2,1,0:T(8,128)S(1)}, f32[1,32,1024]{2,1,0:T(8,128)S(1)}, u32[]{:S(2)}, u32[]{:S(2)}) collective-permute-start(f32[1,32,1024]{2,1,0:T(8,128)S(1)} %constant_dynamic-slice_fusion), channel_id=1, source_target_pairs={{0,16},{4,20},{8,24},{12,28},{16,0},{20,4},{24,8},{28,12},{1,17},{... | collective-permute-start | bytes 393224 | tf_op jit(solution)/shard_map/ppermute | solution.py:146
  110.2 1.3 collective-permute-start.11
  111.5 2.7 %collective-permute-done.15 = f32[1,32,1024]{2,1,0:T(8,128)S(1)} collective-permute-done((f32[1,32,1024]{2,1,0:T(8,128)S(1)}, f32[1,32,1024]{2,1,0:T(8,128)S(1)}, u32[]{:S(2)}, u32[]{:S(2)}) %collective-permute-start.15) | collective-permute-done | bytes 131104 | tf_op jit(solution)/shard_map/ppermute | solution.py:146
  114.2 1.1 bitcast_add_fusion.1
  115.3 15.9 %collective-permute-done.12.refs_0_ = f32[256,1536]{1,0:T(8,128)} collective-permute-done((f32[256,1536]{1,0:T(8,128)}, f32[256,1536]{1,0:T(8,128)}, u32[]{:S(2)}, u32[]{:S(2)}) %collective-permute-start.12) | collective-permute-done | bytes 1572896 | tf_op jit(solution)/shard_map/ppermute | solution.py:174
  131.3 2.0 %collective-permute-start.17 = (f32[32,1024]{1,0:T(8,128)S(1)}, f32[32,1024]{1,0:T(8,128)S(1)}, u32[]{:S(2)}, u32[]{:S(2)}) collective-permute-start(f32[32,1024]{1,0:T(8,128)S(1)} %get-tuple-element.62), channel_id=1, source_target_pairs={{0,8},{4,12},{8,0},{12,4},{16,24},{20,28},{24,16},{28,20},{1,9},{5... | collective-permute-start | bytes 393224 | tf_op jit(solution)/shard_map/ppermute | solution.py:169
  133.3 1.5 collective-permute-start.18
  135.0 5.6 %shard_map.49 = f32[256,1024]{1,0:T(8,128)S(1)} custom-call(s32[7]{0:T(128)S(1)} %pad_add_fusion.1.scalars, f32[256,1536]{1,0:T(8,128)} %collective-permute-done.12.refs_0_, f32[256,1536]{1,0:T(8,128)} %collective-permute-done.refs_1_, bf16[8,256,1024]{2,1,0:T(8,128)(2,1)} %copy-done, bf16[8,256,1024]{2,1,0:T(8,128)(2,1)} %copy-done.1), custom_call_target="tpu_custom_call" | custom-call | flops 805306368 | bytes 2621440 | tf_op jit(solution)/shard_map/pallas_call | solution.py:113
  140.8 1.6 collective-permute-done.11.refs_0_
  142.4 2.0 %collective-permute-done.20 = f32[32,1024]{1,0:T(8,128)S(1)} collective-permute-done((f32[32,1024]{1,0:T(8,128)S(1)}, f32[32,1024]{1,0:T(8,128)S(1)}, u32[]{:S(2)}, u32[]{:S(2)}) %collective-permute-start.20) | collective-permute-done | bytes 131104 | tf_op jit(solution)/shard_map/ppermute | solution.py:174
  144.4 3.4 %shard_map.50 = f32[256,1024]{1,0:T(8,128)} custom-call(s32[3]{0:T(128)S(1)} %pad_add_fusion.3.scalars, f32[256,512]{1,0:T(8,128)S(1)} %collective-permute-done.11.refs_0_, f32[256,512]{1,0:T(8,128)S(1)} %collective-permute-done.5.refs_1_, bf16[8,256,1024]{2,1,0:T(8,128)(2,1)} %copy-done, bf16[8,256,1024]{2,1,0:T(8,128)(2,1)} %copy-done.1), custom_call_target="tpu_custom_call" | custom-call | flops 268435456 | bytes 1572864 | tf_op jit(solution)/shard_map/pallas_call | solution.py:113
  147.8 1.4 add.132
  149.3 1.9 %collective-permute-done.22 = f32[4,32,1024]{2,1,0:T(8,128)S(1)} collective-permute-done((f32[4,32,1024]{2,1,0:T(8,128)S(1)}, f32[4,32,1024]{2,1,0:T(8,128)S(1)}, u32[]{:S(2)}, u32[]{:S(2)}) %collective-permute-start.22) | collective-permute-done | bytes 524320 | tf_op jit(solution)/shard_map/ppermute | solution.py:146
  151.4 2.3 %collective-permute-start.23 = (f32[32,1024]{1,0:T(8,128)S(1)}, f32[32,1024]{1,0:T(8,128)S(1)}, u32[]{:S(2)}, u32[]{:S(2)}) collective-permute-start(f32[32,1024]{1,0:T(8,128)S(1)} %get-tuple-element.59), channel_id=1, source_target_pairs={{0,8},{4,12},{8,0},{12,4},{16,24},{20,28},{24,16},{28,20},{1,9},{5... | collective-permute-start | bytes 393224 | tf_op jit(solution)/shard_map/ppermute | solution.py:169
  153.7 1.5 collective-permute-start.24
  155.2 2.4 %collective-permute-start.21 = (f32[32,1024]{1,0:T(8,128)S(1)}, f32[32,1024]{1,0:T(8,128)S(1)}, u32[]{:S(2)}, u32[]{:S(2)}) collective-permute-start(f32[32,1024]{1,0:T(8,128)S(1)} %fusion.3), channel_id=1, source_target_pairs={{0,2},{2,0},{1,3},{3,1},{4,6},{6,4},{5,7},{7,5},{8,10},{10,8},{9,1... | collective-permute-start | bytes 393224 | tf_op jit(solution)/shard_map/ppermute | solution.py:174
  157.6 4.1 %collective-permute-done.24 = f32[32,1024]{1,0:T(8,128)S(1)} collective-permute-done((f32[32,1024]{1,0:T(8,128)S(1)}, f32[32,1024]{1,0:T(8,128)S(1)}, u32[]{:S(2)}, u32[]{:S(2)}) %collective-permute-start.24) | collective-permute-done | bytes 131104 | tf_op jit(solution)/shard_map/ppermute | solution.py:169
  161.8 2.1 %collective-permute-done.21 = f32[32,1024]{1,0:T(8,128)S(1)} collective-permute-done((f32[32,1024]{1,0:T(8,128)S(1)}, f32[32,1024]{1,0:T(8,128)S(1)}, u32[]{:S(2)}, u32[]{:S(2)}) %collective-permute-start.21) | collective-permute-done | bytes 131104 | tf_op jit(solution)/shard_map/ppermute | solution.py:174
  163.9 3.3 %collective-permute-start.26 = (f32[32,1024]{1,0:T(8,128)S(1)}, f32[32,1024]{1,0:T(8,128)S(1)}, u32[]{:S(2)}, u32[]{:S(2)}) collective-permute-start(f32[32,1024]{1,0:T(8,128)S(1)} %fusion.1), channel_id=1, source_target_pairs={{0,3},{3,0},{1,2},{2,1},{4,7},{7,4},{5,6},{6,5},{8,11},{11,8},{9,1... | collective-permute-start | bytes 393224 | tf_op jit(solution)/shard_map/ppermute | solution.py:174
  167.2 3.8 %collective-permute-done.26 = f32[32,1024]{1,0:T(8,128)S(1)} collective-permute-done((f32[32,1024]{1,0:T(8,128)S(1)}, f32[32,1024]{1,0:T(8,128)S(1)}, u32[]{:S(2)}, u32[]{:S(2)}) %collective-permute-start.26) | collective-permute-done | bytes 131104 | tf_op jit(solution)/shard_map/ppermute | solution.py:174
  171.1 0.8 maximum_add_fusion
  (59 shorter events, 5.0 us)
Async XLA Ops:
  0.0 7.7 %copy-start.3 = (f32[256,2048]{1,0:T(8,128)S(1)}, f32[256,2048]{1,0:T(8,128)}, u32[]{:S(2)}) copy-start(f32[256,2048]{1,0:T(8,128)} %left_ref.1) | copy-start | bytes 6291460
  0.0 7.7 %copy-start.4 = (s32[8]{0:T(128)S(1)}, s32[8]{0:T(128)}, u32[]{:S(2)}) copy-start(s32[8]{0:T(128)} %live.1) | copy-start | bytes 100
  2.8 38.6 %collective-permute-start.2 = (f32[256,1536]{1,0:T(8,128)}, f32[256,1536]{1,0:T(8,128)}, u32[]{:S(2)}, u32[]{:S(2)}) collective-permute-start(f32[256,1536]{1,0:T(8,128)} %slice.12), channel_id=1, source_target_pairs={{0,1},{1,0},{2,3},{3,2},{4,5},{5,4},{6,7},{7,6},{8,9},{9,8},{10,11... | collective-permute-start | bytes 4718600 | tf_op jit(solution)/shard_map/ppermute | solution.py:174
  5.9 37.4 %collective-permute-start = (f32[256,1536]{1,0:T(8,128)}, f32[256,1536]{1,0:T(8,128)}, u32[]{:S(2)}, u32[]{:S(2)}) collective-permute-start(f32[256,1536]{1,0:T(8,128)} %slice.12), channel_id=1, source_target_pairs={{1,2},{2,1},{5,6},{6,5},{9,10},{10,9},{13,14},{14,13},{17,18},{18,... | collective-permute-start | bytes 4718600 | tf_op jit(solution)/shard_map/ppermute | solution.py:174
  7.7 3.4 %copy-start.2 = (f32[2048,1024]{1,0:T(8,128)S(1)}, f32[2048,1024]{1,0:T(8,128)}, u32[]{:S(2)}) copy-start(f32[2048,1024]{1,0:T(8,128)} %param.5) | copy-start | bytes 25165828
  14.4 2.0 %copy-start = (bf16[8,256,1024]{2,1,0:T(8,128)(2,1)}, bf16[8,256,1024]{2,1,0:T(8,128)(2,1)S(1)}, u32[]{:S(2)}) copy-start(bf16[8,256,1024]{2,1,0:T(8,128)(2,1)S(1)} %get-tuple-element.35.refs_2_.refs_4_) | copy-start | bytes 12582916
  16.4 2.0 %copy-start.1 = (bf16[8,256,1024]{2,1,0:T(8,128)(2,1)}, bf16[8,256,1024]{2,1,0:T(8,128)(2,1)S(1)}, u32[]{:S(2)}) copy-start(bf16[8,256,1024]{2,1,0:T(8,128)(2,1)S(1)} %get-tuple-element.36.refs_3_.refs_5_) | copy-start | bytes 12582916
  19.3 25.2 %collective-permute-start.6 = (f32[4,32,1024]{2,1,0:T(8,128)}, f32[4,32,1024]{2,1,0:T(8,128)}, u32[]{:S(2)}, u32[]{:S(2)}) collective-permute-start(f32[4,32,1024]{2,1,0:T(8,128)} %dynamic-slice_bitcast_fusion.3), channel_id=1, source_target_pairs={{0,4},{4,0},{8,12},{12,8},{16,20},{20,16},{24,28},{28,24},{1,5},{5... | collective-permute-start | bytes 1572872 | tf_op jit(solution)/shard_map/ppermute | solution.py:146
  20.1 32.4 %collective-permute-start.4 = (f32[256,512]{1,0:T(8,128)}, f32[256,512]{1,0:T(8,128)S(1)}, u32[]{:S(2)}, u32[]{:S(2)}) collective-permute-start(f32[256,512]{1,0:T(8,128)} %slice.13), channel_id=1, source_target_pairs={{0,1},{1,0},{2,3},{3,2},{4,5},{5,4},{6,7},{7,6},{8,9},{9,8},{10,11... | collective-permute-start | bytes 1572872 | tf_op jit(solution)/shard_map/ppermute | solution.py:174
  23.4 29.2 %collective-permute-start.5 = (f32[256,512]{1,0:T(8,128)}, f32[256,512]{1,0:T(8,128)S(1)}, u32[]{:S(2)}, u32[]{:S(2)}) collective-permute-start(f32[256,512]{1,0:T(8,128)} %slice.13), channel_id=1, source_target_pairs={{1,2},{2,1},{5,6},{6,5},{9,10},{10,9},{13,14},{14,13},{17,18},{18,... | collective-permute-start | bytes 1572872 | tf_op jit(solution)/shard_map/ppermute | solution.py:174
  41.4 29.1 %collective-permute-start.3 = (f32[256,1536]{1,0:T(8,128)}, f32[256,1536]{1,0:T(8,128)}, u32[]{:S(2)}, u32[]{:S(2)}) collective-permute-start(f32[256,1536]{1,0:T(8,128)} %collective-permute-done.2.refs_0_), channel_id=1, source_target_pairs={{1,2},{2,1},{5,6},{6,5},{9,10},{10,9},{13,14},{14,13},{17,18},{18,... | collective-permute-start | bytes 4718600 | tf_op jit(solution)/shard_map/ppermute | solution.py:174
  43.2 43.1 %collective-permute-start.1 = (f32[256,1536]{1,0:T(8,128)}, f32[256,1536]{1,0:T(8,128)}, u32[]{:S(2)}, u32[]{:S(2)}) collective-permute-start(f32[256,1536]{1,0:T(8,128)} %collective-permute-done.refs_1_), channel_id=1, source_target_pairs={{1,0},{2,3},{5,4},{6,7},{9,8},{10,11},{13,12},{14,15},{17,16},{18,... | collective-permute-start | bytes 4718600 | tf_op jit(solution)/shard_map/ppermute | solution.py:174
  45.6 9.0 %copy-start.6 = (f32[4,32,1024]{2,1,0:T(8,128)}, f32[4,32,1024]{2,1,0:T(8,128)S(1)}, u32[]{:S(2)}) copy-start(f32[4,32,1024]{2,1,0:T(8,128)S(1)} %bitcast_add_fusion.3) | copy-start | bytes 1572868
  52.5 8.3 %collective-permute-start.7 = (f32[2,32,1024]{2,1,0:T(8,128)S(1)}, f32[2,32,1024]{2,1,0:T(8,128)}, u32[]{:S(2)}, u32[]{:S(2)}) collective-permute-start(f32[2,32,1024]{2,1,0:T(8,128)S(1)} %dynamic-slice_bitcast_fusion.5), channel_id=1, source_target_pairs={{0,8},{4,12},{8,0},{12,4},{16,24},{20,28},{24,16},{28,20},{1,9},{5... | collective-permute-start | bytes 786440 | tf_op jit(solution)/shard_map/ppermute | solution.py:146
  54.7 6.2 %copy-start.7 = (f32[4,32,1024]{2,1,0:T(8,128)S(1)}, f32[4,32,1024]{2,1,0:T(8,128)}, u32[]{:S(2)}) copy-start(f32[4,32,1024]{2,1,0:T(8,128)} %copy-done.6) | copy-start | bytes 1572868
  60.9 10.9 %collective-permute-start.9 = (f32[4,32,1024]{2,1,0:T(8,128)}, f32[4,32,1024]{2,1,0:T(8,128)}, u32[]{:S(2)}, u32[]{:S(2)}) collective-permute-start(f32[4,32,1024]{2,1,0:T(8,128)} %dynamic-slice_bitcast_fusion.2), channel_id=1, source_target_pairs={{0,4},{4,0},{8,12},{12,8},{16,20},{20,16},{24,28},{28,24},{1,5},{5... | collective-permute-start | bytes 1572872 | tf_op jit(solution)/shard_map/ppermute | solution.py:146
  61.9 6.4 %collective-permute-start.8 = (f32[1,32,1024]{2,1,0:T(8,128)S(1)}, f32[1,32,1024]{2,1,0:T(8,128)}, u32[]{:S(2)}, u32[]{:S(2)}) collective-permute-start(f32[1,32,1024]{2,1,0:T(8,128)S(1)} %constant_dynamic-slice_fusion.1), channel_id=1, source_target_pairs={{0,16},{4,20},{8,24},{12,28},{16,0},{20,4},{24,8},{28,12},{1,17},{... | collective-permute-start | bytes 393224 | tf_op jit(solution)/shard_map/ppermute | solution.py:146
  64.0 22.3 %collective-permute-start.10 = (f32[256,512]{1,0:T(8,128)S(1)}, f32[256,512]{1,0:T(8,128)S(1)}, u32[]{:S(2)}, u32[]{:S(2)}) collective-permute-start(f32[256,512]{1,0:T(8,128)S(1)} %collective-permute-done.4.refs_1_), channel_id=1, source_target_pairs={{1,2},{2,1},{5,6},{6,5},{9,10},{10,9},{13,14},{14,13},{17,18},{18,... | collective-permute-start | bytes 1572872 | tf_op jit(solution)/shard_map/ppermute | solution.py:174
  68.3 29.2 %collective-permute-start.13 = (f32[256,512]{1,0:T(8,128)S(1)}, f32[256,512]{1,0:T(8,128)S(1)}, u32[]{:S(2)}, u32[]{:S(2)}) collective-permute-start(f32[256,512]{1,0:T(8,128)S(1)} %collective-permute-done.5.refs_1_), channel_id=1, source_target_pairs={{1,0},{2,3},{5,4},{6,7},{9,8},{10,11},{13,12},{14,15},{17,16},{18,... | collective-permute-start | bytes 1572872 | tf_op jit(solution)/shard_map/ppermute | solution.py:174
  70.5 60.8 %collective-permute-start.12 = (f32[256,1536]{1,0:T(8,128)}, f32[256,1536]{1,0:T(8,128)}, u32[]{:S(2)}, u32[]{:S(2)}) collective-permute-start(f32[256,1536]{1,0:T(8,128)} %collective-permute-done.3.refs_1_), channel_id=1, source_target_pairs={{1,0},{2,3},{5,4},{6,7},{9,8},{10,11},{13,12},{14,15},{17,16},{18,... | collective-permute-start | bytes 4718600 | tf_op jit(solution)/shard_map/ppermute | solution.py:174
  97.5 10.4 %collective-permute-start.14 = (f32[2,32,1024]{2,1,0:T(8,128)S(1)}, f32[2,32,1024]{2,1,0:T(8,128)S(1)}, u32[]{:S(2)}, u32[]{:S(2)}) collective-permute-start(f32[2,32,1024]{2,1,0:T(8,128)S(1)} %dynamic-slice_bitcast_fusion.4), channel_id=1, source_target_pairs={{0,8},{4,12},{8,0},{12,4},{16,24},{20,28},{24,16},{28,20},{1,9},{5... | collective-permute-start | bytes 786440 | tf_op jit(solution)/shard_map/ppermute | solution.py:146
  105.9 8.3 %copy-start.5 = (f32[256,1024]{1,0:T(8,128)S(1)}, f32[256,1024]{1,0:T(8,128)}, u32[]{:S(2)}) copy-start(f32[256,1024]{1,0:T(8,128)} %shard_map.48) | copy-start | bytes 3145732
  107.9 6.3 %collective-permute-start.16 = (f32[4,32,1024]{2,1,0:T(8,128)}, f32[4,32,1024]{2,1,0:T(8,128)}, u32[]{:S(2)}, u32[]{:S(2)}) collective-permute-start(f32[4,32,1024]{2,1,0:T(8,128)} %dynamic-slice_bitcast_fusion.1), channel_id=1, source_target_pairs={{0,4},{4,0},{8,12},{12,8},{16,20},{20,16},{24,28},{28,24},{1,5},{5... | collective-permute-start | bytes 1572872 | tf_op jit(solution)/shard_map/ppermute | solution.py:146
  107.9 6.2 %collective-permute-start.15 = (f32[1,32,1024]{2,1,0:T(8,128)S(1)}, f32[1,32,1024]{2,1,0:T(8,128)S(1)}, u32[]{:S(2)}, u32[]{:S(2)}) collective-permute-start(f32[1,32,1024]{2,1,0:T(8,128)S(1)} %constant_dynamic-slice_fusion), channel_id=1, source_target_pairs={{0,16},{4,20},{8,24},{12,28},{16,0},{20,4},{24,8},{28,12},{1,17},{... | collective-permute-start | bytes 393224 | tf_op jit(solution)/shard_map/ppermute | solution.py:146
  110.2 32.2 %collective-permute-start.11 = (f32[256,512]{1,0:T(8,128)S(1)}, f32[256,512]{1,0:T(8,128)S(1)}, u32[]{:S(2)}, u32[]{:S(2)}) collective-permute-start(f32[256,512]{1,0:T(8,128)S(1)} %collective-permute-done.10.refs_3_), channel_id=1, source_target_pairs={{1,0},{2,3},{5,4},{6,7},{9,8},{10,11},{13,12},{14,15},{17,16},{18,... | collective-permute-start | bytes 1572872 | tf_op jit(solution)/shard_map/ppermute | solution.py:174
  131.3 9.2 %collective-permute-start.17 = (f32[32,1024]{1,0:T(8,128)S(1)}, f32[32,1024]{1,0:T(8,128)S(1)}, u32[]{:S(2)}, u32[]{:S(2)}) collective-permute-start(f32[32,1024]{1,0:T(8,128)S(1)} %get-tuple-element.62), channel_id=1, source_target_pairs={{0,8},{4,12},{8,0},{12,4},{16,24},{20,28},{24,16},{28,20},{1,9},{5... | collective-permute-start | bytes 393224 | tf_op jit(solution)/shard_map/ppermute | solution.py:169
  133.3 7.2 %collective-permute-start.18 = (f32[32,1024]{1,0:T(8,128)S(1)}, f32[32,1024]{1,0:T(8,128)S(1)}, u32[]{:S(2)}, u32[]{:S(2)}) collective-permute-start(f32[32,1024]{1,0:T(8,128)S(1)} %get-tuple-element.64), channel_id=1, source_target_pairs={{0,16},{4,20},{8,24},{12,28},{16,0},{20,4},{24,8},{28,12},{1,17},{... | collective-permute-start | bytes 393224 | tf_op jit(solution)/shard_map/ppermute | solution.py:169
  134.9 5.9 %collective-permute-start.19 = (f32[32,1024]{1,0:T(8,128)S(1)}, f32[32,1024]{1,0:T(8,128)S(1)}, u32[]{:S(2)}, u32[]{:S(2)}) collective-permute-start(f32[32,1024]{1,0:T(8,128)S(1)} %get-tuple-element.63), channel_id=1, source_target_pairs={{0,24},{4,28},{8,16},{12,20},{16,8},{20,12},{24,0},{28,4},{1,25},{... | collective-permute-start | bytes 393224 | tf_op jit(solution)/shard_map/ppermute | solution.py:169
  135.0 9.4 %collective-permute-start.20 = (f32[32,1024]{1,0:T(8,128)S(1)}, f32[32,1024]{1,0:T(8,128)S(1)}, u32[]{:S(2)}, u32[]{:S(2)}) collective-permute-start(f32[32,1024]{1,0:T(8,128)S(1)} %add_bitcast_fusion), channel_id=1, source_target_pairs={{0,1},{1,0},{2,3},{3,2},{4,5},{5,4},{6,7},{7,6},{8,9},{9,8},{10,11... | collective-permute-start | bytes 393224 | tf_op jit(solution)/shard_map/ppermute | solution.py:174
  149.2 2.0 %collective-permute-start.22 = (f32[4,32,1024]{2,1,0:T(8,128)S(1)}, f32[4,32,1024]{2,1,0:T(8,128)S(1)}, u32[]{:S(2)}, u32[]{:S(2)}) collective-permute-start(f32[4,32,1024]{2,1,0:T(8,128)S(1)} %dynamic-slice_bitcast_fusion), channel_id=1, source_target_pairs={{0,4},{4,0},{8,12},{12,8},{16,20},{20,16},{24,28},{28,24},{1,5},{5... | collective-permute-start | bytes 1572872 | tf_op jit(solution)/shard_map/ppermute | solution.py:146
  151.3 19.7 %copy-start.8 = (f32[32,4096]{1,0:T(8,128)S(1)}, f32[32,4096]{1,0:T(8,128)}, u32[]{:S(2)}) copy-start(f32[32,4096]{1,0:T(8,128)} %param.7) | copy-start | bytes 1572868
  151.4 6.3 %collective-permute-start.23 = (f32[32,1024]{1,0:T(8,128)S(1)}, f32[32,1024]{1,0:T(8,128)S(1)}, u32[]{:S(2)}, u32[]{:S(2)}) collective-permute-start(f32[32,1024]{1,0:T(8,128)S(1)} %get-tuple-element.59), channel_id=1, source_target_pairs={{0,8},{4,12},{8,0},{12,4},{16,24},{20,28},{24,16},{28,20},{1,9},{5... | collective-permute-start | bytes 393224 | tf_op jit(solution)/shard_map/ppermute | solution.py:169
  153.7 8.1 %collective-permute-start.24 = (f32[32,1024]{1,0:T(8,128)S(1)}, f32[32,1024]{1,0:T(8,128)S(1)}, u32[]{:S(2)}, u32[]{:S(2)}) collective-permute-start(f32[32,1024]{1,0:T(8,128)S(1)} %get-tuple-element.61), channel_id=1, source_target_pairs={{0,16},{4,20},{8,24},{12,28},{16,0},{20,4},{24,8},{28,12},{1,17},{... | collective-permute-start | bytes 393224 | tf_op jit(solution)/shard_map/ppermute | solution.py:169
  155.2 6.6 %collective-permute-start.25 = (f32[32,1024]{1,0:T(8,128)S(1)}, f32[32,1024]{1,0:T(8,128)S(1)}, u32[]{:S(2)}, u32[]{:S(2)}) collective-permute-start(f32[32,1024]{1,0:T(8,128)S(1)} %get-tuple-element.60), channel_id=1, source_target_pairs={{0,24},{4,28},{8,16},{12,20},{16,8},{20,12},{24,0},{28,4},{1,25},{... | collective-permute-start | bytes 393224 | tf_op jit(solution)/shard_map/ppermute | solution.py:169
  155.2 8.7 %collective-permute-start.21 = (f32[32,1024]{1,0:T(8,128)S(1)}, f32[32,1024]{1,0:T(8,128)S(1)}, u32[]{:S(2)}, u32[]{:S(2)}) collective-permute-start(f32[32,1024]{1,0:T(8,128)S(1)} %fusion.3), channel_id=1, source_target_pairs={{0,2},{2,0},{1,3},{3,1},{4,6},{6,4},{5,7},{7,5},{8,10},{10,8},{9,1... | collective-permute-start | bytes 393224 | tf_op jit(solution)/shard_map/ppermute | solution.py:174
  163.9 7.1 %collective-permute-start.26 = (f32[32,1024]{1,0:T(8,128)S(1)}, f32[32,1024]{1,0:T(8,128)S(1)}, u32[]{:S(2)}, u32[]{:S(2)}) collective-permute-start(f32[32,1024]{1,0:T(8,128)S(1)} %fusion.1), channel_id=1, source_target_pairs={{0,3},{3,0},{1,2},{2,1},{4,7},{7,4},{5,6},{6,5},{8,11},{11,8},{9,1... | collective-permute-start | bytes 393224 | tf_op jit(solution)/shard_map/ppermute | solution.py:174

commit v2 on v1

--- a/solution.py
+++ b/solution.py
@@ -60,9 +60,11 @@
     )(live, left, right)
 
 
-def product_kernel(layout, first, scalars, *refs):
+def product_kernel(layout, added, scalars, *refs):
     count = len(layout)
-    left_refs, (high_ref, low_ref, out_ref, *lefts) = refs[: sum(layout)], refs[sum(layout) :]
+    left_refs, refs = refs[: sum(layout)], refs[sum(layout) :]
+    (high_ref, low_ref), refs = refs[:2], refs[2:]
+    added_ref, (out_ref, *lefts) = (refs[0], refs[1:]) if added else (None, refs)
     lefts, (high, low, left_sems, sems) = lefts[:count], lefts[count:]
     steps = high.shape[0]
 
@@ -81,13 +83,13 @@
         pairs = (high_ref, high), (low_ref, low)
         right_copies.append(
             [
-                pltpu.make_async_copy(source.at[first + step], target.at[step], sems.at[i, step])
+                pltpu.make_async_copy(source.at[step], target.at[step], sems.at[i, step])
                 for i, (source, target) in enumerate(pairs)
             ]
         )
         for copy in right_copies[-1]:
             copy.start()
-    out_ref[...] = jnp.zeros_like(out_ref)
+    out_ref[...] = added_ref[...] if added else jnp.zeros_like(out_ref)
 
     step = 0
     for i, left in enumerate(lefts):
@@ -104,16 +106,19 @@
             step += 1
 
 
-def product(lists, which, right, live, first=0):
+def product(lists, which, right, live, added=None):
     rows, columns = lists[0][0].shape[0], right[0].shape[2]
     widths = [candidates[0].shape[1] for candidates in lists]
     steps = sum(widths) // TILE
     lefts = [x for candidates in lists for x in candidates]
-    anywhere, hbm = (pl.BlockSpec(memory_space=space) for space in (pl.ANY, pltpu.HBM))
+    anywhere, vmem = (pl.BlockSpec(memory_space=space) for space in (pl.ANY, pltpu.VMEM))
+    more = [] if added is None else [added]
     return pl.pallas_call(
-        functools.partial(product_kernel, [len(candidates) for candidates in lists], first),
+        functools.partial(product_kernel, [len(candidates) for candidates in lists], added is not None),
         out_shape=jax.ShapeDtypeStruct((rows, columns), jnp.float32),
-        in_specs=[pl.BlockSpec(memory_space=pltpu.SMEM)] + [anywhere] * len(lefts) + [hbm] * 2,
+        in_specs=[pl.BlockSpec(memory_space=pltpu.SMEM)]
+        + [anywhere] * (len(lefts) + 2)
+        + [vmem] * len(more),
         out_specs=pl.BlockSpec(memory_space=pltpu.VMEM),
         scratch_shapes=[pltpu.VMEM((rows, width), jnp.float32) for width in widths]
         + [
@@ -122,13 +127,13 @@
             pltpu.SemaphoreType.DMA((len(lists),)),
             pltpu.SemaphoreType.DMA((2, steps)),
         ],
-        compiler_params=pltpu.CompilerParams(vmem_limit_bytes=52 * MIB),
+        compiler_params=pltpu.CompilerParams(vmem_limit_bytes=(52 if steps > 2 else 10) * MIB),
         cost_estimate=pl.CostEstimate(
             flops=2 * rows * TILE * columns * steps,
             bytes_accessed=4 * rows * (steps * TILE + columns),
             transcendentals=0,
         ),
-    )(jnp.concatenate([jnp.int32(which)[None], live[first : first + steps]]), *lefts, *right)
+    )(jnp.concatenate([jnp.int32(which)[None], live[:steps]]), *lefts, *right, *more)
 
 
 def cut(left, tiles):
@@ -220,7 +225,9 @@
     sum_2 = core_sum(product(candidates, inner, split_right, live))
     sum_1 = chip_sum(sum_1)
 
-    three_end[0], sum_1, sum_2 = after(three_end[0], sum_1, sum_2)
+    last_right = [x[kept:] for x in split_right]
+
+    three_end[0], sum_1, sum_2, last_right = after(three_end[0], sum_1, sum_2, last_right)
     candidates = [[three_end[0], three_inner[0]]]
     partial_3 = product(candidates, inner, split_right, live)
     sum_2 = chip_sum_direct(sum_2)
@@ -228,7 +235,7 @@
 
     three_end[1], partial_3, sum_2, home_1 = after(three_end[1], partial_3, sum_2, home_1)
     candidates = [[three_end[1], three_inner[1]]]
-    partial_3 += product(candidates, inner, split_right, live, kept)
+    partial_3 = product(candidates, inner, last_right, live[kept:], partial_3)
     sum_3 = chip_sum_direct(core_sum(partial_3))
     home_2 = send(sum_2, swap_2)
 

time: 172 us -> 171 us (level)
  waiting for transfers between devices: 86.7 us -> 82.5 us
  local copies, waits for them, and re-layouts: 15 us -> 18.9 us
  Pallas kernels: 24 us -> 21 us
  other arithmetic: 7.93 us -> 10.3 us
    pallas_call x4, Pallas kernels: 20.7 us -> 17.6 us  [product(): pl.pallas_call(functools.partial(product_kernel, [len(candidates) for can...]
    slice x1 -> x3, local copies, waits for them, and re-layouts: 0.07 us -> 2.66 us  [the longest x2 2.59 us: ladder_line(): last_right = [x[kept:] for x in split_right]]
    ppermute x13, waiting for transfers between devices: 74.2 us -> 71.8 us  [send(): return lax.ppermute(x, 'ab', pairs)]
    unnamed x18 -> x24, local copies, waits for them, and re-layouts: 7.41 us -> 7.42 us
  transfers between devices with their start and end apart: 27 -> 27, of which waited for: 14 -> 13; matrix products, arithmetic and copies ran while one was open for 6% -> 10% of each run, Pallas kernels for 12% -> 12%
where the time goes in v2:
time: 171 us; the launch traced here: 169 us
  waiting for transfers between devices  82.5 us (48%)
  starting transfers between devices  36.5 us (21%)
  Pallas kernels  21 us (12%)
  local copies, waits for them, and re-layouts  18.9 us (11%)
  other arithmetic  10.3 us (6%)
    ppermute x13, waiting for transfers between devices, send(): return lax.ppermute(x, 'ab', pairs)  71.8 us
    ppermute x13, starting transfers between devices, send(): return lax.ppermute(x, 'ab', pairs)  22 us
    pallas_call x4, Pallas kernels, product(): pl.pallas_call(functools.partial(product_kernel, [len(candidates) for can...  17.6 us
    unnamed x24, local copies, waits for them, and re-layouts  7.42 us
    ppermute x6, starting transfers between devices, chip_sum_direct(): total += lax.ppermute(take(blocks, chip ^ flip, 0), 'cd', pairs)  7.32 us
    ppermute x8, starting transfers between devices, halve(): lax.ppermute(take(blocks, 1 - mine, axis), 'cd', pairs)  7.11 us
    ppermute x8, waiting for transfers between devices, halve(): lax.ppermute(take(blocks, 1 - mine, axis), 'cd', pairs)  6.51 us
    squeeze x11, local copies, waits for them, and re-layouts, take(): return lax.dynamic_index_in_dim(blocks, at, axis, keepdims=False)  5.17 us
  transfers between devices with their start and end apart: 27, of which 13 were waited for; matrix products, arithmetic and copies ran while one was open for 10% of the time, Pallas kernels for 12%

profile of v2, /device:TPU:0, one launch (start us, length us, event | category | flops | bytes accessed | tf_op | source)
XLA Modules:
  0.0 169.5 jit_solution(6170849510773925823)
XLA Ops:
  0.0 2.8 %slice.18 = f32[256,1536]{1,0:T(8,128)} slice(f32[256,2048]{1,0:T(8,128)} %left_ref.1), slice={[0:256], [0:1536]} | slice | bytes 3145728 | tf_op jit(solution)/shard_map/slice | solution.py:141
  2.8 3.0 %collective-permute-start.2 = (f32[256,1536]{1,0:T(8,128)}, f32[256,1536]{1,0:T(8,128)}, u32[]{:S(2)}, u32[]{:S(2)}) collective-permute-start(f32[256,1536]{1,0:T(8,128)} %slice.18), channel_id=1, source_target_pairs={{0,1},{1,0},{2,3},{3,2},{4,5},{5,4},{6,7},{7,6},{8,9},{9,8},{10,11... | collective-permute-start | bytes 4718600 | tf_op jit(solution)/shard_map/ppermute | solution.py:179
  5.8 1.8 %collective-permute-start = (f32[256,1536]{1,0:T(8,128)}, f32[256,1536]{1,0:T(8,128)}, u32[]{:S(2)}, u32[]{:S(2)}) collective-permute-start(f32[256,1536]{1,0:T(8,128)} %slice.18), channel_id=1, source_target_pairs={{1,2},{2,1},{5,6},{6,5},{9,10},{10,9},{13,14},{14,13},{17,18},{18,... | collective-permute-start | bytes 4718600 | tf_op jit(solution)/shard_map/ppermute | solution.py:179
  7.7 3.4 %copy-done.2 = f32[2048,1024]{1,0:T(8,128)S(1)} copy-done((f32[2048,1024]{1,0:T(8,128)S(1)}, f32[2048,1024]{1,0:T(8,128)}, u32[]{:S(2)}) %copy-start.2) | copy-done | bytes 8388632
  11.0 3.3 %shard_map.46 = (f32[256,1024]{1,0:T(8,128)S(1)}, bf16[8,256,1024]{2,1,0:T(8,128)(2,1)S(1)}, bf16[8,256,1024]{2,1,0:T(8,128)(2,1)S(1)}) custom-call(s32[8]{0:T(128)S(1)} %copy-done.6, f32[256,2048]{1,0:T(8,128)S(1)} %copy-done.3, f32[8,256,1024]{2,1,0:T(8,128)S(1)} %bitcast.73), custom_call_target="tpu_custom_call" | custom-call | flops 1073741824 | bytes 3145728 | tf_op jit(solution)/shard_map/pallas_call | solution.py:45
  14.4 2.0 %copy-done = bf16[8,256,1024]{2,1,0:T(8,128)(2,1)} copy-done((bf16[8,256,1024]{2,1,0:T(8,128)(2,1)}, bf16[8,256,1024]{2,1,0:T(8,128)(2,1)S(1)}, u32[]{:S(2)}) %copy-start) | copy-done | bytes 4194328
  16.4 2.0 %copy-done.1 = bf16[8,256,1024]{2,1,0:T(8,128)(2,1)} copy-done((bf16[8,256,1024]{2,1,0:T(8,128)(2,1)}, bf16[8,256,1024]{2,1,0:T(8,128)(2,1)S(1)}, u32[]{:S(2)}) %copy-start.1) | copy-done | bytes 4194328
  20.1 3.3 %collective-permute-start.4 = (f32[256,512]{1,0:T(8,128)}, f32[256,512]{1,0:T(8,128)S(1)}, u32[]{:S(2)}, u32[]{:S(2)}) collective-permute-start(f32[256,512]{1,0:T(8,128)} %slice.19), channel_id=1, source_target_pairs={{0,1},{1,0},{2,3},{3,2},{4,5},{5,4},{6,7},{7,6},{8,9},{9,8},{10,11... | collective-permute-start | bytes 1572872 | tf_op jit(solution)/shard_map/ppermute | solution.py:179
  24.0 17.3 %collective-permute-done.2.refs_0_ = f32[256,1536]{1,0:T(8,128)} collective-permute-done((f32[256,1536]{1,0:T(8,128)}, f32[256,1536]{1,0:T(8,128)}, u32[]{:S(2)}, u32[]{:S(2)}) %collective-permute-start.2) | collective-permute-done | bytes 1572896 | tf_op jit(solution)/shard_map/ppermute | solution.py:179
  41.4 1.8 %collective-permute-start.3 = (f32[256,1536]{1,0:T(8,128)}, f32[256,1536]{1,0:T(8,128)}, u32[]{:S(2)}, u32[]{:S(2)}) collective-permute-start(f32[256,1536]{1,0:T(8,128)} %collective-permute-done.2.refs_0_), channel_id=1, source_target_pairs={{1,2},{2,1},{5,6},{6,5},{9,10},{10,9},{13,14},{14,13},{17,18},{18,... | collective-permute-start | bytes 4718600 | tf_op jit(solution)/shard_map/ppermute | solution.py:179
  43.2 1.3 collective-permute-start.1
  44.5 1.1 bitcast_add_fusion.3
  45.6 6.9 %collective-permute-done.4.refs_1_ = f32[256,512]{1,0:T(8,128)S(1)} collective-permute-done((f32[256,512]{1,0:T(8,128)}, f32[256,512]{1,0:T(8,128)S(1)}, u32[]{:S(2)}, u32[]{:S(2)}) %collective-permute-start.4) | collective-permute-done | bytes 524320 | tf_op jit(solution)/shard_map/ppermute | solution.py:179
  52.5 2.0 %collective-permute-start.7 = (f32[2,32,1024]{2,1,0:T(8,128)S(1)}, f32[2,32,1024]{2,1,0:T(8,128)}, u32[]{:S(2)}, u32[]{:S(2)}) collective-permute-start(f32[2,32,1024]{2,1,0:T(8,128)S(1)} %dynamic-slice_bitcast_fusion.5), channel_id=1, source_target_pairs={{0,8},{4,12},{8,0},{12,4},{16,24},{20,28},{24,16},{28,20},{1,9},{5... | collective-permute-start | bytes 786440 | tf_op jit(solution)/shard_map/ppermute | solution.py:151
  54.7 4.8 %shard_map.47 = f32[256,1024]{1,0:T(8,128)S(1)} custom-call(s32[9]{0:T(128)S(1)} %get-tuple-element.70.scalars, f32[256,1536]{1,0:T(8,128)} %collective-permute-done.2.refs_0_, f32[256,512]{1,0:T(8,128)S(1)} %collective-permute-done.4.refs_1_, bf16[8,256,1024]{2,1,0:T(8,128)(2,1)} %copy-done, bf16[8,256,1024]{2,1,0:T(8,128)(2,1)} %copy-done.1), custom_call_target="tpu_custom_call" | custom-call | flops 1073741824 | bytes 3145728 | tf_op jit(solution)/shard_map/pallas_call | solution.py:116
  60.3 1.0 bitcast_add_fusion.5
  61.3 1.5 collective-permute-start.8
  63.5 3.9 %collective-permute-done.8 = f32[1,32,1024]{2,1,0:T(8,128)} collective-permute-done((f32[1,32,1024]{2,1,0:T(8,128)S(1)}, f32[1,32,1024]{2,1,0:T(8,128)}, u32[]{:S(2)}, u32[]{:S(2)}) %collective-permute-start.8) | collective-permute-done | bytes 131104 | tf_op jit(solution)/shard_map/ppermute | solution.py:151
  67.4 1.3 collective-permute-start.13
  69.6 1.3 collective-permute-start.12
  71.0 1.1 bitcast_add_fusion.2
  72.1 14.2 %collective-permute-done.1.refs_0_ = f32[256,1536]{1,0:T(8,128)} collective-permute-done((f32[256,1536]{1,0:T(8,128)}, f32[256,1536]{1,0:T(8,128)}, u32[]{:S(2)}, u32[]{:S(2)}) %collective-permute-start.1) | collective-permute-done | bytes 1572896 | tf_op jit(solution)/shard_map/ppermute | solution.py:179
  86.3 11.1 %collective-permute-done.13.refs_2_ = f32[256,512]{1,0:T(8,128)S(1)} collective-permute-done((f32[256,512]{1,0:T(8,128)S(1)}, f32[256,512]{1,0:T(8,128)S(1)}, u32[]{:S(2)}, u32[]{:S(2)}) %collective-permute-start.13) | collective-permute-done | bytes 524320 | tf_op jit(solution)/shard_map/ppermute | solution.py:179
  97.5 2.0 %collective-permute-start.14 = (f32[2,32,1024]{2,1,0:T(8,128)S(1)}, f32[2,32,1024]{2,1,0:T(8,128)S(1)}, u32[]{:S(2)}, u32[]{:S(2)}) collective-permute-start(f32[2,32,1024]{2,1,0:T(8,128)S(1)} %dynamic-slice_bitcast_fusion.4), channel_id=1, source_target_pairs={{0,8},{4,12},{8,0},{12,4},{16,24},{20,28},{24,16},{28,20},{1,9},{5... | collective-permute-start | bytes 786440 | tf_op jit(solution)/shard_map/ppermute | solution.py:151
  99.5 5.8 %shard_map.48 = f32[256,1024]{1,0:T(8,128)} custom-call(s32[9]{0:T(128)S(1)} %get-tuple-element.69.scalars, f32[256,1536]{1,0:T(8,128)} %collective-permute-done.1.refs_0_, f32[256,1536]{1,0:T(8,128)} %collective-permute-done.3.refs_1_, f32[256,512]{1,0:T(8,128)S(1)} %collective-permute-done.13.refs_2_, f32[256,512]{1,0:T(8,128)S(1)} %collective-permute-done.10.refs_3_, ...), custom_call_target="tpu_custom_call" | custom-call | flops 1073741824 | bytes 3145728 | tf_op jit(solution)/shard_map/pallas_call | solution.py:116
  105.3 1.9 %dynamic-slice_bitcast_fusion.1 = f32[4,32,1024]{2,1,0:T(8,128)} fusion(f32[4,2,32,1024]{3,2,1,0:T(8,128)} %bitcast.81, s32[]{:T(128)S(6)} %select_n.67), kind=kLoop, calls=%fused_computation.7 | loop fusion | bytes 1048580 | tf_op jit(solution)/shard_map/jit(dynamic_index_in_dim)/squeeze | solution.py:145
  107.9 1.4 collective-permute-start.15
  109.4 1.3 slice.21.refs_2_
  110.7 1.3 slice.22.refs_3_
  112.1 1.3 collective-permute-start.11
  114.2 1.6 add_bitcast_fusion
  115.7 1.3 bitcast_add_fusion.1
  117.0 14.2 %collective-permute-done.12.refs_0_ = f32[256,1536]{1,0:T(8,128)} collective-permute-done((f32[256,1536]{1,0:T(8,128)}, f32[256,1536]{1,0:T(8,128)}, u32[]{:S(2)}, u32[]{:S(2)}) %collective-permute-start.12) | collective-permute-done | bytes 1572896 | tf_op jit(solution)/shard_map/ppermute | solution.py:179
  132.0 2.0 %collective-permute-start.17 = (f32[32,1024]{1,0:T(8,128)}, f32[32,1024]{1,0:T(8,128)}, u32[]{:S(2)}, u32[]{:S(2)}) collective-permute-start(f32[32,1024]{1,0:T(8,128)} %get-tuple-element.66), channel_id=1, source_target_pairs={{0,8},{4,12},{8,0},{12,4},{16,24},{20,28},{24,16},{28,20},{1,9},{5... | collective-permute-start | bytes 393224 | tf_op jit(solution)/shard_map/ppermute | solution.py:174
  134.0 1.5 collective-permute-start.18
  135.6 5.6 %shard_map.49.refs_4_ = f32[256,1024]{1,0:T(8,128)S(1)} custom-call(s32[7]{0:T(128)S(1)} %pad_add_fusion.1.scalars, f32[256,1536]{1,0:T(8,128)} %collective-permute-done.12.refs_0_, f32[256,1536]{1,0:T(8,128)} %collective-permute-done.refs_1_, bf16[8,256,1024]{2,1,0:T(8,128)(2,1)} %copy-done, bf16[8,256,1024]{2,1,0:T(8,128)(2,1)} %copy-done.1), custom_call_target="tpu_custom_call" | custom-call | flops 805306368 | bytes 2621440 | tf_op jit(solution)/shard_map/pallas_call | solution.py:116
  141.5 1.1 fusion.3
  142.6 1.9 %collective-permute-done.20 = f32[32,1024]{1,0:T(8,128)} collective-permute-done((f32[32,1024]{1,0:T(8,128)S(1)}, f32[32,1024]{1,0:T(8,128)}, u32[]{:S(2)}, u32[]{:S(2)}) %collective-permute-start.20) | collective-permute-done | bytes 131104 | tf_op jit(solution)/shard_map/ppermute | solution.py:179
  144.5 1.4 shard_map.50
  146.0 1.9 %collective-permute-done.22 = f32[4,32,1024]{2,1,0:T(8,128)S(1)} collective-permute-done((f32[4,32,1024]{2,1,0:T(8,128)S(1)}, f32[4,32,1024]{2,1,0:T(8,128)S(1)}, u32[]{:S(2)}, u32[]{:S(2)}) %collective-permute-start.22) | collective-permute-done | bytes 524320 | tf_op jit(solution)/shard_map/ppermute | solution.py:151
  148.1 1.2 collective-permute-start.23
  149.2 2.7 %collective-permute-start.24 = (f32[32,1024]{1,0:T(8,128)S(1)}, f32[32,1024]{1,0:T(8,128)S(1)}, u32[]{:S(2)}, u32[]{:S(2)}) collective-permute-start(f32[32,1024]{1,0:T(8,128)S(1)} %get-tuple-element.65), channel_id=1, source_target_pairs={{0,16},{4,20},{8,24},{12,28},{16,0},{20,4},{24,8},{28,12},{1,17},{... | collective-permute-start | bytes 393224 | tf_op jit(solution)/shard_map/ppermute | solution.py:174
  151.9 2.3 %collective-permute-start.21 = (f32[32,1024]{1,0:T(8,128)S(1)}, f32[32,1024]{1,0:T(8,128)S(1)}, u32[]{:S(2)}, u32[]{:S(2)}) collective-permute-start(f32[32,1024]{1,0:T(8,128)S(1)} %fusion.3), channel_id=1, source_target_pairs={{0,2},{2,0},{1,3},{3,1},{4,6},{6,4},{5,7},{7,5},{8,10},{10,8},{9,1... | collective-permute-start | bytes 393224 | tf_op jit(solution)/shard_map/ppermute | solution.py:179
  154.2 4.0 %collective-permute-done.24 = f32[32,1024]{1,0:T(8,128)S(1)} collective-permute-done((f32[32,1024]{1,0:T(8,128)S(1)}, f32[32,1024]{1,0:T(8,128)S(1)}, u32[]{:S(2)}, u32[]{:S(2)}) %collective-permute-start.24) | collective-permute-done | bytes 131104 | tf_op jit(solution)/shard_map/ppermute | solution.py:174
  158.2 2.3 %collective-permute-done.21 = f32[32,1024]{1,0:T(8,128)S(1)} collective-permute-done((f32[32,1024]{1,0:T(8,128)S(1)}, f32[32,1024]{1,0:T(8,128)S(1)}, u32[]{:S(2)}, u32[]{:S(2)}) %collective-permute-start.21) | collective-permute-done | bytes 131104 | tf_op jit(solution)/shard_map/ppermute | solution.py:179
  160.6 3.2 %collective-permute-start.26 = (f32[32,1024]{1,0:T(8,128)S(1)}, f32[32,1024]{1,0:T(8,128)S(1)}, u32[]{:S(2)}, u32[]{:S(2)}) collective-permute-start(f32[32,1024]{1,0:T(8,128)S(1)} %fusion.1), channel_id=1, source_target_pairs={{0,3},{3,0},{1,2},{2,1},{4,7},{7,4},{5,6},{6,5},{8,11},{11,8},{9,1... | collective-permute-start | bytes 393224 | tf_op jit(solution)/shard_map/ppermute | solution.py:179
  163.8 3.8 %collective-permute-done.26 = f32[32,1024]{1,0:T(8,128)S(1)} collective-permute-done((f32[32,1024]{1,0:T(8,128)S(1)}, f32[32,1024]{1,0:T(8,128)S(1)}, u32[]{:S(2)}, u32[]{:S(2)}) %collective-permute-start.26) | collective-permute-done | bytes 131104 | tf_op jit(solution)/shard_map/ppermute | solution.py:179
  167.6 0.9 pad_maximum_fusion
  (66 shorter events, 8.8 us)
Async XLA Ops:
  0.0 7.6 %copy-start.3 = (f32[256,2048]{1,0:T(8,128)S(1)}, f32[256,2048]{1,0:T(8,128)}, u32[]{:S(2)}) copy-start(f32[256,2048]{1,0:T(8,128)} %left_ref.1) | copy-start | bytes 6291460
  0.0 7.6 %copy-start.6 = (s32[8]{0:T(128)S(1)}, s32[8]{0:T(128)}, u32[]{:S(2)}) copy-start(s32[8]{0:T(128)} %live.1) | copy-start | bytes 100
  2.8 38.6 %collective-permute-start.2 = (f32[256,1536]{1,0:T(8,128)}, f32[256,1536]{1,0:T(8,128)}, u32[]{:S(2)}, u32[]{:S(2)}) collective-permute-start(f32[256,1536]{1,0:T(8,128)} %slice.18), channel_id=1, source_target_pairs={{0,1},{1,0},{2,3},{3,2},{4,5},{5,4},{6,7},{7,6},{8,9},{9,8},{10,11... | collective-permute-start | bytes 4718600 | tf_op jit(solution)/shard_map/ppermute | solution.py:179
  5.8 37.4 %collective-permute-start = (f32[256,1536]{1,0:T(8,128)}, f32[256,1536]{1,0:T(8,128)}, u32[]{:S(2)}, u32[]{:S(2)}) collective-permute-start(f32[256,1536]{1,0:T(8,128)} %slice.18), channel_id=1, source_target_pairs={{1,2},{2,1},{5,6},{6,5},{9,10},{10,9},{13,14},{14,13},{17,18},{18,... | collective-permute-start | bytes 4718600 | tf_op jit(solution)/shard_map/ppermute | solution.py:179
  7.7 3.4 %copy-start.2 = (f32[2048,1024]{1,0:T(8,128)S(1)}, f32[2048,1024]{1,0:T(8,128)}, u32[]{:S(2)}) copy-start(f32[2048,1024]{1,0:T(8,128)} %param.5) | copy-start | bytes 25165828
  14.4 2.0 %copy-start = (bf16[8,256,1024]{2,1,0:T(8,128)(2,1)}, bf16[8,256,1024]{2,1,0:T(8,128)(2,1)S(1)}, u32[]{:S(2)}) copy-start(bf16[8,256,1024]{2,1,0:T(8,128)(2,1)S(1)} %get-tuple-element.37.refs_2_.refs_4_) | copy-start | bytes 12582916
  16.4 2.0 %copy-start.1 = (bf16[8,256,1024]{2,1,0:T(8,128)(2,1)}, bf16[8,256,1024]{2,1,0:T(8,128)(2,1)S(1)}, u32[]{:S(2)}) copy-start(bf16[8,256,1024]{2,1,0:T(8,128)(2,1)S(1)} %get-tuple-element.38.refs_3_.refs_5_) | copy-start | bytes 12582916
  19.2 25.2 %collective-permute-start.6 = (f32[4,32,1024]{2,1,0:T(8,128)}, f32[4,32,1024]{2,1,0:T(8,128)}, u32[]{:S(2)}, u32[]{:S(2)}) collective-permute-start(f32[4,32,1024]{2,1,0:T(8,128)} %dynamic-slice_bitcast_fusion.3), channel_id=1, source_target_pairs={{0,4},{4,0},{8,12},{12,8},{16,20},{20,16},{24,28},{28,24},{1,5},{5... | collective-permute-start | bytes 1572872 | tf_op jit(solution)/shard_map/ppermute | solution.py:151
  20.1 32.4 %collective-permute-start.4 = (f32[256,512]{1,0:T(8,128)}, f32[256,512]{1,0:T(8,128)S(1)}, u32[]{:S(2)}, u32[]{:S(2)}) collective-permute-start(f32[256,512]{1,0:T(8,128)} %slice.19), channel_id=1, source_target_pairs={{0,1},{1,0},{2,3},{3,2},{4,5},{5,4},{6,7},{7,6},{8,9},{9,8},{10,11... | collective-permute-start | bytes 1572872 | tf_op jit(solution)/shard_map/ppermute | solution.py:179
  23.4 29.1 %collective-permute-start.5 = (f32[256,512]{1,0:T(8,128)}, f32[256,512]{1,0:T(8,128)S(1)}, u32[]{:S(2)}, u32[]{:S(2)}) collective-permute-start(f32[256,512]{1,0:T(8,128)} %slice.19), channel_id=1, source_target_pairs={{1,2},{2,1},{5,6},{6,5},{9,10},{10,9},{13,14},{14,13},{17,18},{18,... | collective-permute-start | bytes 1572872 | tf_op jit(solution)/shard_map/ppermute | solution.py:179
  41.4 28.3 %collective-permute-start.3 = (f32[256,1536]{1,0:T(8,128)}, f32[256,1536]{1,0:T(8,128)}, u32[]{:S(2)}, u32[]{:S(2)}) collective-permute-start(f32[256,1536]{1,0:T(8,128)} %collective-permute-done.2.refs_0_), channel_id=1, source_target_pairs={{1,2},{2,1},{5,6},{6,5},{9,10},{10,9},{13,14},{14,13},{17,18},{18,... | collective-permute-start | bytes 4718600 | tf_op jit(solution)/shard_map/ppermute | solution.py:179
  43.2 43.1 %collective-permute-start.1 = (f32[256,1536]{1,0:T(8,128)}, f32[256,1536]{1,0:T(8,128)}, u32[]{:S(2)}, u32[]{:S(2)}) collective-permute-start(f32[256,1536]{1,0:T(8,128)} %collective-permute-done.refs_1_), channel_id=1, source_target_pairs={{1,0},{2,3},{5,4},{6,7},{9,8},{10,11},{13,12},{14,15},{17,16},{18,... | collective-permute-start | bytes 4718600 | tf_op jit(solution)/shard_map/ppermute | solution.py:179
  45.6 9.0 %copy-start.8 = (f32[4,32,1024]{2,1,0:T(8,128)}, f32[4,32,1024]{2,1,0:T(8,128)S(1)}, u32[]{:S(2)}) copy-start(f32[4,32,1024]{2,1,0:T(8,128)S(1)} %bitcast_add_fusion.3) | copy-start | bytes 1572868
  52.5 14.9 %copy-start.4 = (f32[256,512]{1,0:T(8,128)}, f32[256,512]{1,0:T(8,128)S(1)}, u32[]{:S(2)}) copy-start(f32[256,512]{1,0:T(8,128)S(1)} %collective-permute-done.5.refs_1_) | copy-start | bytes 1572868
  52.5 7.8 %collective-permute-start.7 = (f32[2,32,1024]{2,1,0:T(8,128)S(1)}, f32[2,32,1024]{2,1,0:T(8,128)}, u32[]{:S(2)}, u32[]{:S(2)}) collective-permute-start(f32[2,32,1024]{2,1,0:T(8,128)S(1)} %dynamic-slice_bitcast_fusion.5), channel_id=1, source_target_pairs={{0,8},{4,12},{8,0},{12,4},{16,24},{20,28},{24,16},{28,20},{1,9},{5... | collective-permute-start | bytes 786440 | tf_op jit(solution)/shard_map/ppermute | solution.py:151
  54.6 5.7 %copy-start.9 = (f32[4,32,1024]{2,1,0:T(8,128)S(1)}, f32[4,32,1024]{2,1,0:T(8,128)}, u32[]{:S(2)}) copy-start(f32[4,32,1024]{2,1,0:T(8,128)} %copy-done.8) | copy-start | bytes 1572868
  60.3 10.6 %collective-permute-start.9 = (f32[4,32,1024]{2,1,0:T(8,128)}, f32[4,32,1024]{2,1,0:T(8,128)}, u32[]{:S(2)}, u32[]{:S(2)}) collective-permute-start(f32[4,32,1024]{2,1,0:T(8,128)} %dynamic-slice_bitcast_fusion.2), channel_id=1, source_target_pairs={{0,4},{4,0},{8,12},{12,8},{16,20},{20,16},{24,28},{28,24},{1,5},{5... | collective-permute-start | bytes 1572872 | tf_op jit(solution)/shard_map/ppermute | solution.py:151
  61.3 6.1 %collective-permute-start.8 = (f32[1,32,1024]{2,1,0:T(8,128)S(1)}, f32[1,32,1024]{2,1,0:T(8,128)}, u32[]{:S(2)}, u32[]{:S(2)}) collective-permute-start(f32[1,32,1024]{2,1,0:T(8,128)S(1)} %constant_dynamic-slice_fusion.1), channel_id=1, source_target_pairs={{0,16},{4,20},{8,24},{12,28},{16,0},{20,4},{24,8},{28,12},{1,17},{... | collective-permute-start | bytes 393224 | tf_op jit(solution)/shard_map/ppermute | solution.py:151
  62.8 23.5 %collective-permute-start.10 = (f32[256,512]{1,0:T(8,128)S(1)}, f32[256,512]{1,0:T(8,128)S(1)}, u32[]{:S(2)}, u32[]{:S(2)}) collective-permute-start(f32[256,512]{1,0:T(8,128)S(1)} %collective-permute-done.4.refs_1_), channel_id=1, source_target_pairs={{1,2},{2,1},{5,6},{6,5},{9,10},{10,9},{13,14},{14,13},{17,18},{18,... | collective-permute-start | bytes 1572872 | tf_op jit(solution)/shard_map/ppermute | solution.py:179
  67.4 30.0 %collective-permute-start.13 = (f32[256,512]{1,0:T(8,128)S(1)}, f32[256,512]{1,0:T(8,128)S(1)}, u32[]{:S(2)}, u32[]{:S(2)}) collective-permute-start(f32[256,512]{1,0:T(8,128)S(1)} %collective-permute-done.5.refs_1_), channel_id=1, source_target_pairs={{1,0},{2,3},{5,4},{6,7},{9,8},{10,11},{13,12},{14,15},{17,16},{18,... | collective-permute-start | bytes 1572872 | tf_op jit(solution)/shard_map/ppermute | solution.py:179
  69.6 61.6 %collective-permute-start.12 = (f32[256,1536]{1,0:T(8,128)}, f32[256,1536]{1,0:T(8,128)}, u32[]{:S(2)}, u32[]{:S(2)}) collective-permute-start(f32[256,1536]{1,0:T(8,128)} %collective-permute-done.3.refs_1_), channel_id=1, source_target_pairs={{1,0},{2,3},{5,4},{6,7},{9,8},{10,11},{13,12},{14,15},{17,16},{18,... | collective-permute-start | bytes 4718600 | tf_op jit(solution)/shard_map/ppermute | solution.py:179
  97.5 9.8 %collective-permute-start.14 = (f32[2,32,1024]{2,1,0:T(8,128)S(1)}, f32[2,32,1024]{2,1,0:T(8,128)S(1)}, u32[]{:S(2)}, u32[]{:S(2)}) collective-permute-start(f32[2,32,1024]{2,1,0:T(8,128)S(1)} %dynamic-slice_bitcast_fusion.4), channel_id=1, source_target_pairs={{0,8},{4,12},{8,0},{12,4},{16,24},{20,28},{24,16},{28,20},{1,9},{5... | collective-permute-start | bytes 786440 | tf_op jit(solution)/shard_map/ppermute | solution.py:151
  107.2 8.5 %collective-permute-start.16 = (f32[4,32,1024]{2,1,0:T(8,128)}, f32[4,32,1024]{2,1,0:T(8,128)}, u32[]{:S(2)}, u32[]{:S(2)}) collective-permute-start(f32[4,32,1024]{2,1,0:T(8,128)} %dynamic-slice_bitcast_fusion.1), channel_id=1, source_target_pairs={{0,4},{4,0},{8,12},{12,8},{16,20},{20,16},{24,28},{28,24},{1,5},{5... | collective-permute-start | bytes 1572872 | tf_op jit(solution)/shard_map/ppermute | solution.py:151
  107.9 6.2 %collective-permute-start.15 = (f32[1,32,1024]{2,1,0:T(8,128)}, f32[1,32,1024]{2,1,0:T(8,128)}, u32[]{:S(2)}, u32[]{:S(2)}) collective-permute-start(f32[1,32,1024]{2,1,0:T(8,128)} %constant_dynamic-slice_fusion), channel_id=1, source_target_pairs={{0,16},{4,20},{8,24},{12,28},{16,0},{20,4},{24,8},{28,12},{1,17},{... | collective-permute-start | bytes 393224 | tf_op jit(solution)/shard_map/ppermute | solution.py:151
  112.1 30.4 %collective-permute-start.11 = (f32[256,512]{1,0:T(8,128)S(1)}, f32[256,512]{1,0:T(8,128)S(1)}, u32[]{:S(2)}, u32[]{:S(2)}) collective-permute-start(f32[256,512]{1,0:T(8,128)S(1)} %collective-permute-done.10.refs_3_), channel_id=1, source_target_pairs={{1,0},{2,3},{5,4},{6,7},{9,8},{10,11},{13,12},{14,15},{17,16},{18,... | collective-permute-start | bytes 1572872 | tf_op jit(solution)/shard_map/ppermute | solution.py:179
  115.7 19.8 %copy-start.11 = (f32[32,1024]{1,0:T(8,128)S(1)}, f32[32,1024]{1,0:T(8,128)}, u32[]{:S(2)}) copy-start(f32[32,1024]{1,0:T(8,128)} %add_bitcast_fusion) | copy-start | bytes 393220
  117.0 18.4 %copy-start.7 = (f32[4,32,1024]{2,1,0:T(8,128)}, f32[4,32,1024]{2,1,0:T(8,128)S(1)}, u32[]{:S(2)}) copy-start(f32[4,32,1024]{2,1,0:T(8,128)S(1)} %bitcast_add_fusion.1) | copy-start | bytes 1572868
  132.0 9.2 %collective-permute-start.17 = (f32[32,1024]{1,0:T(8,128)}, f32[32,1024]{1,0:T(8,128)}, u32[]{:S(2)}, u32[]{:S(2)}) collective-permute-start(f32[32,1024]{1,0:T(8,128)} %get-tuple-element.66), channel_id=1, source_target_pairs={{0,8},{4,12},{8,0},{12,4},{16,24},{20,28},{24,16},{28,20},{1,9},{5... | collective-permute-start | bytes 393224 | tf_op jit(solution)/shard_map/ppermute | solution.py:174
  134.0 7.2 %collective-permute-start.18 = (f32[32,1024]{1,0:T(8,128)}, f32[32,1024]{1,0:T(8,128)}, u32[]{:S(2)}, u32[]{:S(2)}) collective-permute-start(f32[32,1024]{1,0:T(8,128)} %get-tuple-element.68), channel_id=1, source_target_pairs={{0,16},{4,20},{8,24},{12,28},{16,0},{20,4},{24,8},{28,12},{1,17},{... | collective-permute-start | bytes 393224 | tf_op jit(solution)/shard_map/ppermute | solution.py:174
  135.5 6.0 %collective-permute-start.19 = (f32[32,1024]{1,0:T(8,128)S(1)}, f32[32,1024]{1,0:T(8,128)}, u32[]{:S(2)}, u32[]{:S(2)}) collective-permute-start(f32[32,1024]{1,0:T(8,128)S(1)} %get-tuple-element.67), channel_id=1, source_target_pairs={{0,24},{4,28},{8,16},{12,20},{16,8},{20,12},{24,0},{28,4},{1,25},{... | collective-permute-start | bytes 393224 | tf_op jit(solution)/shard_map/ppermute | solution.py:174
  135.6 8.9 %copy-start.5 = (f32[256,512]{1,0:T(8,128)S(1)}, f32[256,512]{1,0:T(8,128)}, u32[]{:S(2)}) copy-start(f32[256,512]{1,0:T(8,128)} %copy-done.4) | copy-start | bytes 1572868
  135.6 8.9 %collective-permute-start.20 = (f32[32,1024]{1,0:T(8,128)S(1)}, f32[32,1024]{1,0:T(8,128)}, u32[]{:S(2)}, u32[]{:S(2)}) collective-permute-start(f32[32,1024]{1,0:T(8,128)S(1)} %copy-done.11), channel_id=1, source_target_pairs={{0,1},{1,0},{2,3},{3,2},{4,5},{5,4},{6,7},{7,6},{8,9},{9,8},{10,11... | collective-permute-start | bytes 393224 | tf_op jit(solution)/shard_map/ppermute | solution.py:179
  146.0 2.0 %collective-permute-start.22 = (f32[4,32,1024]{2,1,0:T(8,128)S(1)}, f32[4,32,1024]{2,1,0:T(8,128)S(1)}, u32[]{:S(2)}, u32[]{:S(2)}) collective-permute-start(f32[4,32,1024]{2,1,0:T(8,128)S(1)} %dynamic-slice_bitcast_fusion), channel_id=1, source_target_pairs={{0,4},{4,0},{8,12},{12,8},{16,20},{20,16},{24,28},{28,24},{1,5},{5... | collective-permute-start | bytes 1572872 | tf_op jit(solution)/shard_map/ppermute | solution.py:151
  148.1 20.5 %copy-start.10 = (f32[32,4096]{1,0:T(8,128)S(1)}, f32[32,4096]{1,0:T(8,128)}, u32[]{:S(2)}) copy-start(f32[32,4096]{1,0:T(8,128)} %param.7) | copy-start | bytes 1572868
  148.1 6.2 %collective-permute-start.23 = (f32[32,1024]{1,0:T(8,128)S(1)}, f32[32,1024]{1,0:T(8,128)S(1)}, u32[]{:S(2)}, u32[]{:S(2)}) collective-permute-start(f32[32,1024]{1,0:T(8,128)S(1)} %get-tuple-element.63), channel_id=1, source_target_pairs={{0,8},{4,12},{8,0},{12,4},{16,24},{20,28},{24,16},{28,20},{1,9},{5... | collective-permute-start | bytes 393224 | tf_op jit(solution)/shard_map/ppermute | solution.py:174
  149.2 9.0 %collective-permute-start.24 = (f32[32,1024]{1,0:T(8,128)S(1)}, f32[32,1024]{1,0:T(8,128)S(1)}, u32[]{:S(2)}, u32[]{:S(2)}) collective-permute-start(f32[32,1024]{1,0:T(8,128)S(1)} %get-tuple-element.65), channel_id=1, source_target_pairs={{0,16},{4,20},{8,24},{12,28},{16,0},{20,4},{24,8},{28,12},{1,17},{... | collective-permute-start | bytes 393224 | tf_op jit(solution)/shard_map/ppermute | solution.py:174
  151.9 6.3 %collective-permute-start.25 = (f32[32,1024]{1,0:T(8,128)S(1)}, f32[32,1024]{1,0:T(8,128)S(1)}, u32[]{:S(2)}, u32[]{:S(2)}) collective-permute-start(f32[32,1024]{1,0:T(8,128)S(1)} %get-tuple-element.64), channel_id=1, source_target_pairs={{0,24},{4,28},{8,16},{12,20},{16,8},{20,12},{24,0},{28,4},{1,25},{... | collective-permute-start | bytes 393224 | tf_op jit(solution)/shard_map/ppermute | solution.py:174
  151.9 8.7 %collective-permute-start.21 = (f32[32,1024]{1,0:T(8,128)S(1)}, f32[32,1024]{1,0:T(8,128)S(1)}, u32[]{:S(2)}, u32[]{:S(2)}) collective-permute-start(f32[32,1024]{1,0:T(8,128)S(1)} %fusion.3), channel_id=1, source_target_pairs={{0,2},{2,0},{1,3},{3,1},{4,6},{6,4},{5,7},{7,5},{8,10},{10,8},{9,1... | collective-permute-start | bytes 393224 | tf_op jit(solution)/shard_map/ppermute | solution.py:179
  160.6 7.0 %collective-permute-start.26 = (f32[32,1024]{1,0:T(8,128)S(1)}, f32[32,1024]{1,0:T(8,128)S(1)}, u32[]{:S(2)}, u32[]{:S(2)}) collective-permute-start(f32[32,1024]{1,0:T(8,128)S(1)} %fusion.1), channel_id=1, source_target_pairs={{0,3},{3,0},{1,2},{2,1},{4,7},{7,4},{5,6},{6,5},{8,11},{11,8},{9,1... | collective-permute-start | bytes 393224 | tf_op jit(solution)/shard_map/ppermute | solution.py:179

commit v3 on v2

--- a/solution.py
+++ b/solution.py
@@ -183,6 +183,16 @@
     return lax.optimization_barrier(values)
 
 
+def place(home):
+    at, parts = lax.axis_index("ab"), []
+    for i in range(len(home)):
+        part = home[0]
+        for flip in range(1, len(home)):
+            part = jnp.where(at ^ i == flip, home[flip], part)
+        parts.append(part)
+    return jnp.concatenate(parts, axis=1)
+
+
 def ladder_any(amplitudes, live, right):
     count = lax.axis_size("ab")
     first, *split_right = first_product(amplitudes, right, live)
@@ -192,7 +202,7 @@
         lists = [[send(x, pairs)] for x in cut(amplitudes, live.shape[0])]
         partial_rows = product(lists, 0, split_right, live)
         home.append(send(chip_sum(core_sum(partial_rows)), pairs))
-    return [take(jnp.stack(home), lax.axis_index("ab") ^ i, 0) for i in range(count)]
+    return place(home)
 
 
 def ladder_line(amplitudes, live, right):
@@ -202,25 +212,25 @@
     swap_2 = [(0, 2), (2, 0), (1, 3), (3, 1)]
     swap_3 = [(0, 3), (3, 0), (1, 2), (2, 1)]
     swap_inner, to_end = [(1, 2), (2, 1)], [(1, 0), (2, 3)]
-    lists = cut(amplitudes, live.shape[0])
-    kept = lists[0].shape[1] // TILE
-
-    one = [send(x, swap_1) for x in lists]
-    three_inner = [send(x, swap_inner) for x in lists]
-    two_inner = [send(x, swap_inner) for x in one]
-    two_end = [send(x, to_end) for x in three_inner]
+    tiles = live.shape[0]
+    kept = tiles - tiles // 4
+
+    one, three_inner = send(amplitudes, swap_1), send(amplitudes, swap_inner)
+    two_end = send(three_inner, to_end)
+    two_inner = [send(x, swap_inner) for x in cut(one, tiles)]
     three_end = [send(x, to_end) for x in two_inner]
 
     first, *split_right = first_product(amplitudes, right, live)
     sum_0 = core_sum(first)
 
-    one[0], three_inner[0], sum_0 = after(one[0], three_inner[0], sum_0)
-    one[1], three_inner[1], sum_0 = after(one[1], three_inner[1], sum_0)
-    sum_1 = core_sum(product([[x] for x in one], 0, split_right, live))
+    one, three_inner, sum_0 = after(one, three_inner, sum_0)
+    three_inner = cut(three_inner, tiles)
+    sum_1 = core_sum(product([[one]], 0, split_right, live))
     home_0 = chip_sum(sum_0)
 
-    two_end[0], two_inner[0], home_0, sum_1 = after(two_end[0], two_inner[0], home_0, sum_1)
-    two_end[1], two_inner[1], sum_1 = after(two_end[1], two_inner[1], sum_1)
+    two_inner[0], home_0, sum_1 = after(two_inner[0], home_0, sum_1)
+    two_end, two_inner[1], three_inner, sum_1 = after(two_end, two_inner[1], three_inner, sum_1)
+    two_end = cut(two_end, tiles)
     candidates = [list(pair) for pair in zip(two_end, two_inner)]
     sum_2 = core_sum(product(candidates, inner, split_right, live))
     sum_1 = chip_sum(sum_1)
@@ -240,14 +250,13 @@
     home_2 = send(sum_2, swap_2)
 
     home_2, sum_3 = after(home_2, sum_3)
-    home = jnp.stack([home_0, home_1, home_2, send(sum_3, swap_3)])
-    return [take(home, at ^ i, 0) for i in range(4)]
+    return place([home_0, home_1, home_2, send(sum_3, swap_3)])
 
 
 def per_device(amplitudes, integrals, live_tiles, residual_in):
     right = integrals.reshape(live_tiles.shape[0], TILE, integrals.shape[1])
     ladder = ladder_line if lax.axis_size("ab") == 4 else ladder_any
-    return residual_in + jnp.concatenate(ladder(amplitudes, live_tiles, right), axis=1)
+    return residual_in + ladder(amplitudes, live_tiles, right)
 
 
 def solution(mesh):

time: 171 us -> 173 us (1.012)
  Pallas kernels: 21 us -> 30.2 us
  starting transfers between devices: 36.5 us -> 28.2 us
  local copies, waits for them, and re-layouts: 18.9 us -> 25.9 us
  other arithmetic: 10.3 us -> 7.26 us
  waiting for transfers between devices: 82.5 us -> 80.1 us
    slice x2 -> x6, local copies, waits for them, and re-layouts: 3.65 us -> 11.3 us  [cut(): return [left[:, :kept], left[:, kept:]]]
    pallas_call x4, Pallas kernels: 17.6 us -> 25.1 us  [product(): pl.pallas_call(functools.partial(product_kernel, [len(candidates) for can...]
    ppermute x13 -> x10, starting transfers between devices: 22 us -> 17.8 us  [send(): return lax.ppermute(x, 'ab', pairs)]
    ppermute x8, starting transfers between devices: 7.11 us -> 3.33 us  [halve(): lax.ppermute(take(blocks, 1 - mine, axis), 'cd', pairs)]
    add x6, other arithmetic: 4.6 us -> 1.56 us  [halve(): take(blocks, mine, axis)]
    ppermute x8, waiting for transfers between devices: 6.51 us -> 4.56 us  [halve(): lax.ppermute(take(blocks, 1 - mine, axis), 'cd', pairs)]
    pallas_call x1, Pallas kernels: 3.35 us -> 5.08 us  [first_product(): pl.pallas_call(first_kernel, out_shape=(jax.ShapeDtypeStruct((rows, colum...]
    ppermute x13 -> x10, waiting for transfers between devices: 71.8 us -> 72.7 us  [send(): return lax.ppermute(x, 'ab', pairs)]
  transfers between devices with their start and end apart: 27 -> 24, of which waited for: 13 -> 9; matrix products, arithmetic and copies ran while one was open for 10% -> 14% of each run, Pallas kernels for 12% -> 16%
where the time goes in v3:
time: 173 us; the launch traced here: 172 us
  waiting for transfers between devices  80.1 us (46%)
  Pallas kernels  30.2 us (17%)
  starting transfers between devices  28.2 us (16%)
  local copies, waits for them, and re-layouts  25.9 us (15%)
  other arithmetic  7.26 us (4%)
    ppermute x10, waiting for transfers between devices, send(): return lax.ppermute(x, 'ab', pairs)  72.7 us
    pallas_call x4, Pallas kernels, product(): pl.pallas_call(functools.partial(product_kernel, [len(candidates) for can...  25.1 us
    ppermute x10, starting transfers between devices, send(): return lax.ppermute(x, 'ab', pairs)  17.8 us
    slice x6, local copies, waits for them, and re-layouts, cut(): return [left[:, :kept], left[:, kept:]]  11.3 us
    unnamed x20, local copies, waits for them, and re-layouts  7.67 us
    ppermute x6, starting transfers between devices, chip_sum_direct(): total += lax.ppermute(take(blocks, chip ^ flip, 0), 'cd', pairs)  7.04 us
    pallas_call x1, Pallas kernels, first_product(): pl.pallas_call(first_kernel, out_shape=(jax.ShapeDtypeStruct((rows, colum...  5.08 us
    ppermute x8, waiting for transfers between devices, halve(): lax.ppermute(take(blocks, 1 - mine, axis), 'cd', pairs)  4.56 us
  transfers between devices with their start and end apart: 24, of which 9 were waited for; matrix products, arithmetic and copies ran while one was open for 14% of the time, Pallas kernels for 16%

profile of v3, /device:TPU:0, one launch (start us, length us, event | category | flops | bytes accessed | tf_op | source)
XLA Modules:
  0.0 172.1 jit_solution(3298909654172312424)
XLA Ops:
  0.0 2.0 %collective-permute-start.5 = (f32[256,2048]{1,0:T(8,128)}, f32[256,2048]{1,0:T(8,128)}, u32[]{:S(2)}, u32[]{:S(2)}) collective-permute-start(f32[256,2048]{1,0:T(8,128)} %left_ref.1), channel_id=1, source_target_pairs={{1,2},{2,1},{5,6},{6,5},{9,10},{10,9},{13,14},{14,13},{17,18},{18,... | collective-permute-start | bytes 6291464 | tf_op jit(solution)/shard_map/ppermute | solution.py:179
  2.0 4.5 %collective-permute-start = (f32[256,2048]{1,0:T(8,128)}, f32[256,2048]{1,0:T(8,128)}, u32[]{:S(2)}, u32[]{:S(2)}) collective-permute-start(f32[256,2048]{1,0:T(8,128)} %left_ref.1), channel_id=1, source_target_pairs={{0,1},{1,0},{2,3},{3,2},{4,5},{5,4},{6,7},{7,6},{8,9},{9,8},{10,11... | collective-permute-start | bytes 6291464 | tf_op jit(solution)/shard_map/ppermute | solution.py:179
  6.6 3.4 %copy-done.2 = f32[2048,1024]{1,0:T(8,128)S(1)} copy-done((f32[2048,1024]{1,0:T(8,128)S(1)}, f32[2048,1024]{1,0:T(8,128)}, u32[]{:S(2)}) %copy-start.2) | copy-done | bytes 8388632
  10.0 1.6 copy-done.3
  12.2 5.1 %shard_map.46 = (f32[256,1024]{1,0:T(8,128)S(1)}, bf16[8,256,1024]{2,1,0:T(8,128)(2,1)S(1)}, bf16[8,256,1024]{2,1,0:T(8,128)(2,1)S(1)}) custom-call(s32[8]{0:T(128)S(1)} %copy-done.5, f32[256,2048]{1,0:T(8,128)S(1)} %copy-done.3, f32[8,256,1024]{2,1,0:T(8,128)S(1)} %bitcast.61), custom_call_target="tpu_custom_call" | custom-call | flops 1073741824 | bytes 3145728 | tf_op jit(solution)/shard_map/pallas_call | solution.py:45
  17.3 2.0 %copy-done.1 = bf16[8,256,1024]{2,1,0:T(8,128)(2,1)} copy-done((bf16[8,256,1024]{2,1,0:T(8,128)(2,1)}, bf16[8,256,1024]{2,1,0:T(8,128)(2,1)S(1)}, u32[]{:S(2)}) %copy-start.1) | copy-done | bytes 4194328
  19.5 1.3 collective-permute-start.6
  20.8 31.5 %collective-permute-done.refs_0_ = f32[256,2048]{1,0:T(8,128)} collective-permute-done((f32[256,2048]{1,0:T(8,128)}, f32[256,2048]{1,0:T(8,128)}, u32[]{:S(2)}, u32[]{:S(2)}) %collective-permute-start) | collective-permute-done | bytes 2097184 | tf_op jit(solution)/shard_map/ppermute | solution.py:179
  52.2 2.7 %slice.41 = f32[256,1536]{1,0:T(8,128)} slice(f32[256,2048]{1,0:T(8,128)} %collective-permute-done.refs_0_), slice={[0:256], [0:1536]} | slice | bytes 3145728 | tf_op jit(solution)/shard_map/slice | solution.py:141
  55.0 1.8 %collective-permute-start.3 = (f32[256,1536]{1,0:T(8,128)}, f32[256,1536]{1,0:T(8,128)}, u32[]{:S(2)}, u32[]{:S(2)}) collective-permute-start(f32[256,1536]{1,0:T(8,128)} %slice.41), channel_id=1, source_target_pairs={{1,2},{2,1},{5,6},{6,5},{9,10},{10,9},{13,14},{14,13},{17,18},{18,... | collective-permute-start | bytes 4718600 | tf_op jit(solution)/shard_map/ppermute | solution.py:179
  56.9 1.6 collective-permute-start.8
  58.5 8.7 %shard_map.47 = f32[256,1024]{1,0:T(8,128)S(1)} custom-call(s32[9]{0:T(128)S(1)} %get-tuple-element.66.scalars, f32[256,2048]{1,0:T(8,128)} %collective-permute-done.refs_0_, bf16[8,256,1024]{2,1,0:T(8,128)(2,1)} %copy-done, bf16[8,256,1024]{2,1,0:T(8,128)(2,1)} %copy-done.1), custom_call_target="tpu_custom_call" | custom-call | flops 1073741824 | bytes 3145728 | tf_op jit(solution)/shard_map/pallas_call | solution.py:116
  67.2 0.8 dynamic-slice_bitcast_fusion.2
  68.2 1.1 slice.40
  69.3 0.7 collective-permute-start.1
  70.0 2.7 %slice.33.refs_1_ = f32[256,1536]{1,0:T(8,128)} slice(f32[256,2048]{1,0:T(8,128)} %collective-permute-done.5), slice={[0:256], [0:1536]} | slice | bytes 3145728 | tf_op jit(solution)/shard_map/slice | solution.py:141
  72.6 1.1 slice.34.refs_1_
  74.2 0.9 add_bitcast_fusion.1
  75.1 1.3 collective-permute-start.4
  76.5 24.2 %collective-permute-done.6 = f32[256,2048]{1,0:T(8,128)} collective-permute-done((f32[256,2048]{1,0:T(8,128)}, f32[256,2048]{1,0:T(8,128)}, u32[]{:S(2)}, u32[]{:S(2)}) %collective-permute-start.6) | collective-permute-done | bytes 2097184 | tf_op jit(solution)/shard_map/ppermute | solution.py:179
  100.7 1.6 collective-permute-start.11
  102.3 2.7 %slice.35.refs_0_ = f32[256,1536]{1,0:T(8,128)} slice(f32[256,2048]{1,0:T(8,128)} %collective-permute-done.6), slice={[0:256], [0:1536]} | slice | bytes 3145728 | tf_op jit(solution)/shard_map/slice | solution.py:141
  105.0 1.1 slice.36.refs_2_
  106.1 7.7 %shard_map.48 = f32[256,1024]{1,0:T(8,128)} custom-call(s32[9]{0:T(128)S(1)} %get-tuple-element.65.scalars, f32[256,1536]{1,0:T(8,128)} %slice.35.refs_0_, f32[256,1536]{1,0:T(8,128)} %collective-permute-done.3.refs_1_, f32[256,512]{1,0:T(8,128)S(1)} %slice.36.refs_2_, f32[256,512]{1,0:T(8,128)S(1)} %collective-permute-done.1.refs_3_, ...), custom_call_target="tpu_custom_call" | custom-call | flops 1073741824 | bytes 3145728 | tf_op jit(solution)/shard_map/pallas_call | solution.py:116
  113.8 1.9 %dynamic-slice_bitcast_fusion.1 = f32[4,32,1024]{2,1,0:T(8,128)} fusion(f32[4,2,32,1024]{3,2,1,0:T(8,128)} %bitcast.69, s32[]{:T(128)S(6)} %select_n.130), kind=kLoop, calls=%fused_computation.6 | loop fusion | bytes 1048580 | tf_op jit(solution)/shard_map/jit(dynamic_index_in_dim)/squeeze | solution.py:145
  115.7 0.7 constant_dynamic-slice_fusion
  116.4 1.3 slice.37.refs_2_
  117.7 1.3 slice.38.refs_3_
  119.2 1.3 collective-permute-start.2
  120.5 2.2 %collective-permute-done.12 = f32[1,32,1024]{2,1,0:T(8,128)} collective-permute-done((f32[1,32,1024]{2,1,0:T(8,128)}, f32[1,32,1024]{2,1,0:T(8,128)}, u32[]{:S(2)}, u32[]{:S(2)}) %collective-permute-start.12) | collective-permute-done | bytes 131104 | tf_op jit(solution)/shard_map/ppermute | solution.py:151
  122.6 1.6 add_bitcast_fusion
  124.2 1.3 bitcast_add_fusion.1
  125.5 8.9 %collective-permute-done.4.refs_0_ = f32[256,1536]{1,0:T(8,128)} collective-permute-done((f32[256,1536]{1,0:T(8,128)}, f32[256,1536]{1,0:T(8,128)}, u32[]{:S(2)}, u32[]{:S(2)}) %collective-permute-start.4) | collective-permute-done | bytes 1572896 | tf_op jit(solution)/shard_map/ppermute | solution.py:179
  134.4 0.7 dynamic-slice_bitcast_fusion.11
  135.2 1.5 collective-permute-start.14
  136.7 1.5 collective-permute-start.15
  138.8 6.7 %shard_map.49.refs_4_ = f32[256,1024]{1,0:T(8,128)S(1)} custom-call(s32[7]{0:T(128)S(1)} %pad_add_fusion.scalars, f32[256,1536]{1,0:T(8,128)} %collective-permute-done.4.refs_0_, f32[256,1536]{1,0:T(8,128)} %slice.33.refs_1_, bf16[8,256,1024]{2,1,0:T(8,128)(2,1)} %copy-done, bf16[8,256,1024]{2,1,0:T(8,128)(2,1)} %copy-done.1), custom_call_target="tpu_custom_call" | custom-call | flops 805306368 | bytes 2621440 | tf_op jit(solution)/shard_map/pallas_call | solution.py:116
  145.5 1.1 fusion.3
  146.7 2.0 %shard_map.50 = f32[256,1024]{1,0:T(8,128)S(1)} custom-call(s32[3]{0:T(128)S(1)} %pad_add_fusion.3.scalars, f32[256,512]{1,0:T(8,128)S(1)} %collective-permute-done.2.refs_0_, f32[256,512]{1,0:T(8,128)S(1)} %slice.34.refs_1_, bf16[2,256,1024]{2,1,0:T(8,128)(2,1)S(1)} %slice.37.refs_2_, bf16[2,256,1024]{2,1,0:T(8,128)(2,1)S(1)} %slice.38.refs_3_, ...), custom_call_target="tpu_custom_call" | custom-call | flops 268435456 | bytes 1572864 | tf_op jit(solution)/shard_map/pallas_call | solution.py:116
  148.8 1.9 %collective-permute-done.19 = f32[4,32,1024]{2,1,0:T(8,128)S(1)} collective-permute-done((f32[4,32,1024]{2,1,0:T(8,128)S(1)}, f32[4,32,1024]{2,1,0:T(8,128)S(1)}, u32[]{:S(2)}, u32[]{:S(2)}) %collective-permute-start.19) | collective-permute-done | bytes 524320 | tf_op jit(solution)/shard_map/ppermute | solution.py:151
  151.3 2.7 %collective-permute-start.21 = (f32[32,1024]{1,0:T(8,128)S(1)}, f32[32,1024]{1,0:T(8,128)S(1)}, u32[]{:S(2)}, u32[]{:S(2)}) collective-permute-start(f32[32,1024]{1,0:T(8,128)S(1)} %get-tuple-element.61), channel_id=1, source_target_pairs={{0,16},{4,20},{8,24},{12,28},{16,0},{20,4},{24,8},{28,12},{1,17},{... | collective-permute-start | bytes 393224 | tf_op jit(solution)/shard_map/ppermute | solution.py:174
  154.4 3.0 %collective-permute-start.18 = (f32[32,1024]{1,0:T(8,128)S(1)}, f32[32,1024]{1,0:T(8,128)S(1)}, u32[]{:S(2)}, u32[]{:S(2)}) collective-permute-start(f32[32,1024]{1,0:T(8,128)S(1)} %fusion.3), channel_id=1, source_target_pairs={{0,2},{2,0},{1,3},{3,1},{4,6},{6,4},{5,7},{7,5},{8,10},{10,8},{9,1... | collective-permute-start | bytes 393224 | tf_op jit(solution)/shard_map/ppermute | solution.py:179
  157.4 2.8 %collective-permute-done.21 = f32[32,1024]{1,0:T(8,128)S(1)} collective-permute-done((f32[32,1024]{1,0:T(8,128)S(1)}, f32[32,1024]{1,0:T(8,128)S(1)}, u32[]{:S(2)}, u32[]{:S(2)}) %collective-permute-start.21) | collective-permute-done | bytes 131104 | tf_op jit(solution)/shard_map/ppermute | solution.py:174
  160.3 3.2 %collective-permute-done.18 = f32[32,1024]{1,0:T(8,128)S(1)} collective-permute-done((f32[32,1024]{1,0:T(8,128)S(1)}, f32[32,1024]{1,0:T(8,128)S(1)}, u32[]{:S(2)}, u32[]{:S(2)}) %collective-permute-start.18) | collective-permute-done | bytes 131104 | tf_op jit(solution)/shard_map/ppermute | solution.py:179
  163.5 1.8 %collective-permute-start.23 = (f32[32,1024]{1,0:T(8,128)S(1)}, f32[32,1024]{1,0:T(8,128)S(1)}, u32[]{:S(2)}, u32[]{:S(2)}) collective-permute-start(f32[32,1024]{1,0:T(8,128)S(1)} %fusion.1), channel_id=1, source_target_pairs={{0,3},{3,0},{1,2},{2,1},{4,7},{7,4},{5,6},{6,5},{8,11},{11,8},{9,1... | collective-permute-start | bytes 393224 | tf_op jit(solution)/shard_map/ppermute | solution.py:179
  165.4 4.9 %collective-permute-done.23 = f32[32,1024]{1,0:T(8,128)S(1)} collective-permute-done((f32[32,1024]{1,0:T(8,128)S(1)}, f32[32,1024]{1,0:T(8,128)S(1)}, u32[]{:S(2)}, u32[]{:S(2)}) %collective-permute-start.23) | collective-permute-done | bytes 131104 | tf_op jit(solution)/shard_map/ppermute | solution.py:179
  170.3 1.0 select_select_fusion.3
  171.3 0.8 maximum_add_fusion
  (59 shorter events, 3.6 us)
Async XLA Ops:
  0.0 19.5 %collective-permute-start.5 = (f32[256,2048]{1,0:T(8,128)}, f32[256,2048]{1,0:T(8,128)}, u32[]{:S(2)}, u32[]{:S(2)}) collective-permute-start(f32[256,2048]{1,0:T(8,128)} %left_ref.1), channel_id=1, source_target_pairs={{1,2},{2,1},{5,6},{6,5},{9,10},{10,9},{13,14},{14,13},{17,18},{18,... | collective-permute-start | bytes 6291464 | tf_op jit(solution)/shard_map/ppermute | solution.py:179
  2.0 50.2 %collective-permute-start = (f32[256,2048]{1,0:T(8,128)}, f32[256,2048]{1,0:T(8,128)}, u32[]{:S(2)}, u32[]{:S(2)}) collective-permute-start(f32[256,2048]{1,0:T(8,128)} %left_ref.1), channel_id=1, source_target_pairs={{0,1},{1,0},{2,3},{3,2},{4,5},{5,4},{6,7},{7,6},{8,9},{9,8},{10,11... | collective-permute-start | bytes 6291464 | tf_op jit(solution)/shard_map/ppermute | solution.py:179
  6.6 3.4 %copy-start.2 = (f32[2048,1024]{1,0:T(8,128)S(1)}, f32[2048,1024]{1,0:T(8,128)}, u32[]{:S(2)}) copy-start(f32[2048,1024]{1,0:T(8,128)} %param.5) | copy-start | bytes 25165828
  10.0 1.6 copy-start.3
  11.5 0.7 copy-start.5
  17.3 2.0 %copy-start.1 = (bf16[8,256,1024]{2,1,0:T(8,128)(2,1)}, bf16[8,256,1024]{2,1,0:T(8,128)(2,1)S(1)}, u32[]{:S(2)}) copy-start(bf16[8,256,1024]{2,1,0:T(8,128)(2,1)S(1)} %get-tuple-element.35.refs_2_.refs_5_.refs_3_) | copy-start | bytes 12582916
  19.3 35.6 %copy-start = (bf16[8,256,1024]{2,1,0:T(8,128)(2,1)}, bf16[8,256,1024]{2,1,0:T(8,128)(2,1)S(1)}, u32[]{:S(2)}) copy-start(bf16[8,256,1024]{2,1,0:T(8,128)(2,1)S(1)} %get-tuple-element.34.refs_1_.refs_4_.refs_2_) | copy-start | bytes 12582916
  19.4 39.1 %copy-start.6 = (s32[8]{0:T(128)S(1)}, s32[8]{0:T(128)}, u32[]{:S(2)}) copy-start(s32[8]{0:T(128)} %live.1) | copy-start | bytes 100
  19.4 37.4 %collective-permute-start.7 = (f32[4,32,1024]{2,1,0:T(8,128)S(1)}, f32[4,32,1024]{2,1,0:T(8,128)S(1)}, u32[]{:S(2)}, u32[]{:S(2)}) collective-permute-start(f32[4,32,1024]{2,1,0:T(8,128)S(1)} %dynamic-slice_bitcast_fusion.3), channel_id=1, source_target_pairs={{0,4},{4,0},{8,12},{12,8},{16,20},{20,16},{24,28},{28,24},{1,5},{5... | collective-permute-start | bytes 1572872 | tf_op jit(solution)/shard_map/ppermute | solution.py:151
  19.5 81.3 %collective-permute-start.6 = (f32[256,2048]{1,0:T(8,128)}, f32[256,2048]{1,0:T(8,128)}, u32[]{:S(2)}, u32[]{:S(2)}) collective-permute-start(f32[256,2048]{1,0:T(8,128)} %collective-permute-done.5), channel_id=1, source_target_pairs={{1,0},{2,3},{5,4},{6,7},{9,8},{10,11},{13,12},{14,15},{17,16},{18,... | collective-permute-start | bytes 6291464 | tf_op jit(solution)/shard_map/ppermute | solution.py:179
  55.0 20.2 %collective-permute-start.3 = (f32[256,1536]{1,0:T(8,128)}, f32[256,1536]{1,0:T(8,128)}, u32[]{:S(2)}, u32[]{:S(2)}) collective-permute-start(f32[256,1536]{1,0:T(8,128)} %slice.41), channel_id=1, source_target_pairs={{1,2},{2,1},{5,6},{6,5},{9,10},{10,9},{13,14},{14,13},{17,18},{18,... | collective-permute-start | bytes 4718600 | tf_op jit(solution)/shard_map/ppermute | solution.py:179
  56.9 11.2 %collective-permute-start.8 = (f32[2,32,1024]{2,1,0:T(8,128)S(1)}, f32[2,32,1024]{2,1,0:T(8,128)S(1)}, u32[]{:S(2)}, u32[]{:S(2)}) collective-permute-start(f32[2,32,1024]{2,1,0:T(8,128)S(1)} %dynamic-slice_bitcast_fusion.5), channel_id=1, source_target_pairs={{0,8},{4,12},{8,0},{12,4},{16,24},{20,28},{24,16},{28,20},{1,9},{5... | collective-permute-start | bytes 786440 | tf_op jit(solution)/shard_map/ppermute | solution.py:151
  68.0 8.4 %collective-permute-start.10 = (f32[4,32,1024]{2,1,0:T(8,128)}, f32[4,32,1024]{2,1,0:T(8,128)S(1)}, u32[]{:S(2)}, u32[]{:S(2)}) collective-permute-start(f32[4,32,1024]{2,1,0:T(8,128)} %dynamic-slice_bitcast_fusion.2), channel_id=1, source_target_pairs={{0,4},{4,0},{8,12},{12,8},{16,20},{20,16},{24,28},{28,24},{1,5},{5... | collective-permute-start | bytes 1572872 | tf_op jit(solution)/shard_map/ppermute | solution.py:151
  68.1 6.1 %collective-permute-start.9 = (f32[1,32,1024]{2,1,0:T(8,128)S(1)}, f32[1,32,1024]{2,1,0:T(8,128)}, u32[]{:S(2)}, u32[]{:S(2)}) collective-permute-start(f32[1,32,1024]{2,1,0:T(8,128)S(1)} %constant_dynamic-slice_fusion.1), channel_id=1, source_target_pairs={{0,16},{4,20},{8,24},{12,28},{16,0},{20,4},{24,8},{28,12},{1,17},{... | collective-permute-start | bytes 393224 | tf_op jit(solution)/shard_map/ppermute | solution.py:151
  69.3 7.2 %collective-permute-start.1 = (f32[256,512]{1,0:T(8,128)S(1)}, f32[256,512]{1,0:T(8,128)S(1)}, u32[]{:S(2)}, u32[]{:S(2)}) collective-permute-start(f32[256,512]{1,0:T(8,128)S(1)} %slice.40), channel_id=1, source_target_pairs={{1,2},{2,1},{5,6},{6,5},{9,10},{10,9},{13,14},{14,13},{17,18},{18,... | collective-permute-start | bytes 1572872 | tf_op jit(solution)/shard_map/ppermute | solution.py:179
  75.1 59.3 %collective-permute-start.4 = (f32[256,1536]{1,0:T(8,128)}, f32[256,1536]{1,0:T(8,128)}, u32[]{:S(2)}, u32[]{:S(2)}) collective-permute-start(f32[256,1536]{1,0:T(8,128)} %collective-permute-done.3.refs_1_), channel_id=1, source_target_pairs={{1,0},{2,3},{5,4},{6,7},{9,8},{10,11},{13,12},{14,15},{17,16},{18,... | collective-permute-start | bytes 4718600 | tf_op jit(solution)/shard_map/ppermute | solution.py:179
  76.5 29.5 %copy-start.4 = (f32[256,512]{1,0:T(8,128)}, f32[256,512]{1,0:T(8,128)S(1)}, u32[]{:S(2)}) copy-start(f32[256,512]{1,0:T(8,128)S(1)} %collective-permute-done.1.refs_3_) | copy-start | bytes 1572868
  100.7 15.0 %collective-permute-start.11 = (f32[2,32,1024]{2,1,0:T(8,128)S(1)}, f32[2,32,1024]{2,1,0:T(8,128)S(1)}, u32[]{:S(2)}, u32[]{:S(2)}) collective-permute-start(f32[2,32,1024]{2,1,0:T(8,128)S(1)} %dynamic-slice_bitcast_fusion.4), channel_id=1, source_target_pairs={{0,8},{4,12},{8,0},{12,4},{16,24},{20,28},{24,16},{28,20},{1,9},{5... | collective-permute-start | bytes 786440 | tf_op jit(solution)/shard_map/ppermute | solution.py:151
  115.7 8.5 %collective-permute-start.13 = (f32[4,32,1024]{2,1,0:T(8,128)}, f32[4,32,1024]{2,1,0:T(8,128)}, u32[]{:S(2)}, u32[]{:S(2)}) collective-permute-start(f32[4,32,1024]{2,1,0:T(8,128)} %dynamic-slice_bitcast_fusion.1), channel_id=1, source_target_pairs={{0,4},{4,0},{8,12},{12,8},{16,20},{20,16},{24,28},{28,24},{1,5},{5... | collective-permute-start | bytes 1572872 | tf_op jit(solution)/shard_map/ppermute | solution.py:151
  116.4 6.2 %collective-permute-start.12 = (f32[1,32,1024]{2,1,0:T(8,128)}, f32[1,32,1024]{2,1,0:T(8,128)}, u32[]{:S(2)}, u32[]{:S(2)}) collective-permute-start(f32[1,32,1024]{2,1,0:T(8,128)} %constant_dynamic-slice_fusion), channel_id=1, source_target_pairs={{0,16},{4,20},{8,24},{12,28},{16,0},{20,4},{24,8},{28,12},{1,17},{... | collective-permute-start | bytes 393224 | tf_op jit(solution)/shard_map/ppermute | solution.py:151
  119.2 27.5 %collective-permute-start.2 = (f32[256,512]{1,0:T(8,128)}, f32[256,512]{1,0:T(8,128)S(1)}, u32[]{:S(2)}, u32[]{:S(2)}) collective-permute-start(f32[256,512]{1,0:T(8,128)} %copy-done.4), channel_id=1, source_target_pairs={{1,0},{2,3},{5,4},{6,7},{9,8},{10,11},{13,12},{14,15},{17,16},{18,... | collective-permute-start | bytes 1572872 | tf_op jit(solution)/shard_map/ppermute | solution.py:179
  124.2 14.5 %copy-start.9 = (f32[32,1024]{1,0:T(8,128)S(1)}, f32[32,1024]{1,0:T(8,128)}, u32[]{:S(2)}) copy-start(f32[32,1024]{1,0:T(8,128)} %add_bitcast_fusion) | copy-start | bytes 393220
  125.5 12.7 %copy-start.7 = (f32[4,32,1024]{2,1,0:T(8,128)}, f32[4,32,1024]{2,1,0:T(8,128)S(1)}, u32[]{:S(2)}) copy-start(f32[4,32,1024]{2,1,0:T(8,128)S(1)} %bitcast_add_fusion.1) | copy-start | bytes 1572868
  135.2 10.3 %collective-permute-start.14 = (f32[32,1024]{1,0:T(8,128)}, f32[32,1024]{1,0:T(8,128)}, u32[]{:S(2)}, u32[]{:S(2)}) collective-permute-start(f32[32,1024]{1,0:T(8,128)} %get-tuple-element.62), channel_id=1, source_target_pairs={{0,8},{4,12},{8,0},{12,4},{16,24},{20,28},{24,16},{28,20},{1,9},{5... | collective-permute-start | bytes 393224 | tf_op jit(solution)/shard_map/ppermute | solution.py:174
  136.7 8.8 %collective-permute-start.15 = (f32[32,1024]{1,0:T(8,128)}, f32[32,1024]{1,0:T(8,128)}, u32[]{:S(2)}, u32[]{:S(2)}) collective-permute-start(f32[32,1024]{1,0:T(8,128)} %get-tuple-element.64), channel_id=1, source_target_pairs={{0,16},{4,20},{8,24},{12,28},{16,0},{20,4},{24,8},{28,12},{1,17},{... | collective-permute-start | bytes 393224 | tf_op jit(solution)/shard_map/ppermute | solution.py:174
  138.2 7.3 %collective-permute-start.16 = (f32[32,1024]{1,0:T(8,128)S(1)}, f32[32,1024]{1,0:T(8,128)}, u32[]{:S(2)}, u32[]{:S(2)}) collective-permute-start(f32[32,1024]{1,0:T(8,128)S(1)} %get-tuple-element.63), channel_id=1, source_target_pairs={{0,24},{4,28},{8,16},{12,20},{16,8},{20,12},{24,0},{28,4},{1,25},{... | collective-permute-start | bytes 393224 | tf_op jit(solution)/shard_map/ppermute | solution.py:174
  138.7 7.9 %collective-permute-start.17 = (f32[32,1024]{1,0:T(8,128)S(1)}, f32[32,1024]{1,0:T(8,128)}, u32[]{:S(2)}, u32[]{:S(2)}) collective-permute-start(f32[32,1024]{1,0:T(8,128)S(1)} %copy-done.9), channel_id=1, source_target_pairs={{0,1},{1,0},{2,3},{3,2},{4,5},{5,4},{6,7},{7,6},{8,9},{9,8},{10,11... | collective-permute-start | bytes 393224 | tf_op jit(solution)/shard_map/ppermute | solution.py:179
  148.8 22.5 %copy-start.8 = (f32[32,4096]{1,0:T(8,128)S(1)}, f32[32,4096]{1,0:T(8,128)}, u32[]{:S(2)}) copy-start(f32[32,4096]{1,0:T(8,128)} %param.7) | copy-start | bytes 1572868
  148.8 2.0 %collective-permute-start.19 = (f32[4,32,1024]{2,1,0:T(8,128)S(1)}, f32[4,32,1024]{2,1,0:T(8,128)S(1)}, u32[]{:S(2)}, u32[]{:S(2)}) collective-permute-start(f32[4,32,1024]{2,1,0:T(8,128)S(1)} %dynamic-slice_bitcast_fusion), channel_id=1, source_target_pairs={{0,4},{4,0},{8,12},{12,8},{16,20},{20,16},{24,28},{28,24},{1,5},{5... | collective-permute-start | bytes 1572872 | tf_op jit(solution)/shard_map/ppermute | solution.py:151
  150.9 6.6 %collective-permute-start.20 = (f32[32,1024]{1,0:T(8,128)S(1)}, f32[32,1024]{1,0:T(8,128)S(1)}, u32[]{:S(2)}, u32[]{:S(2)}) collective-permute-start(f32[32,1024]{1,0:T(8,128)S(1)} %get-tuple-element.59), channel_id=1, source_target_pairs={{0,8},{4,12},{8,0},{12,4},{16,24},{20,28},{24,16},{28,20},{1,9},{5... | collective-permute-start | bytes 393224 | tf_op jit(solution)/shard_map/ppermute | solution.py:174
  151.3 9.0 %collective-permute-start.21 = (f32[32,1024]{1,0:T(8,128)S(1)}, f32[32,1024]{1,0:T(8,128)S(1)}, u32[]{:S(2)}, u32[]{:S(2)}) collective-permute-start(f32[32,1024]{1,0:T(8,128)S(1)} %get-tuple-element.61), channel_id=1, source_target_pairs={{0,16},{4,20},{8,24},{12,28},{16,0},{20,4},{24,8},{28,12},{1,17},{... | collective-permute-start | bytes 393224 | tf_op jit(solution)/shard_map/ppermute | solution.py:174
  153.9 6.3 %collective-permute-start.22 = (f32[32,1024]{1,0:T(8,128)S(1)}, f32[32,1024]{1,0:T(8,128)S(1)}, u32[]{:S(2)}, u32[]{:S(2)}) collective-permute-start(f32[32,1024]{1,0:T(8,128)S(1)} %get-tuple-element.60), channel_id=1, source_target_pairs={{0,24},{4,28},{8,16},{12,20},{16,8},{20,12},{24,0},{28,4},{1,25},{... | collective-permute-start | bytes 393224 | tf_op jit(solution)/shard_map/ppermute | solution.py:174
  154.4 9.1 %collective-permute-start.18 = (f32[32,1024]{1,0:T(8,128)S(1)}, f32[32,1024]{1,0:T(8,128)S(1)}, u32[]{:S(2)}, u32[]{:S(2)}) collective-permute-start(f32[32,1024]{1,0:T(8,128)S(1)} %fusion.3), channel_id=1, source_target_pairs={{0,2},{2,0},{1,3},{3,1},{4,6},{6,4},{5,7},{7,5},{8,10},{10,8},{9,1... | collective-permute-start | bytes 393224 | tf_op jit(solution)/shard_map/ppermute | solution.py:179
  163.5 6.8 %collective-permute-start.23 = (f32[32,1024]{1,0:T(8,128)S(1)}, f32[32,1024]{1,0:T(8,128)S(1)}, u32[]{:S(2)}, u32[]{:S(2)}) collective-permute-start(f32[32,1024]{1,0:T(8,128)S(1)} %fusion.1), channel_id=1, source_target_pairs={{0,3},{3,0},{1,2},{2,1},{4,7},{7,4},{5,6},{6,5},{8,11},{11,8},{9,1... | collective-permute-start | bytes 393224 | tf_op jit(solution)/shard_map/ppermute | solution.py:179

commit v4 on v2

--- a/solution.py
+++ b/solution.py
@@ -231,15 +231,14 @@
     candidates = [[three_end[0], three_inner[0]]]
     partial_3 = product(candidates, inner, split_right, live)
     sum_2 = chip_sum_direct(sum_2)
-    home_1 = send(sum_1, swap_1)
-
-    three_end[1], partial_3, sum_2, home_1 = after(three_end[1], partial_3, sum_2, home_1)
+
+    three_end[1], partial_3, sum_2 = after(three_end[1], partial_3, sum_2)
     candidates = [[three_end[1], three_inner[1]]]
     partial_3 = product(candidates, inner, last_right, live[kept:], partial_3)
     sum_3 = chip_sum_direct(core_sum(partial_3))
-    home_2 = send(sum_2, swap_2)
-
-    home_2, sum_3 = after(home_2, sum_3)
+    home_1, home_2 = send(sum_1, swap_1), send(sum_2, swap_2)
+
+    home_1, home_2, sum_3 = after(home_1, home_2, sum_3)
     home = jnp.stack([home_0, home_1, home_2, send(sum_3, swap_3)])
     return [take(home, at ^ i, 0) for i in range(4)]
 

time: 171 us -> 170 us (level)
  waiting for transfers between devices: 82.5 us -> 79.8 us
  Pallas kernels: 21 us -> 23.2 us
    ppermute x6, waiting for transfers between devices: 4.23 us -> 2.16 us  [chip_sum_direct(): total += lax.ppermute(take(blocks, chip ^ flip, 0), 'cd', pairs)]
  transfers between devices with their start and end apart: 27 -> 27, of which waited for: 13 -> 12; matrix products, arithmetic and copies ran while one was open for 10% -> 10% of each run, Pallas kernels for 12% -> 13%
where the time goes in v4:
time: 170 us; the launch traced here: 169 us
  waiting for transfers between devices  79.8 us (47%)
  starting transfers between devices  37.4 us (22%)
  Pallas kernels  23.2 us (14%)
  local copies, waits for them, and re-layouts  18.9 us (11%)
  other arithmetic  9.27 us (5%)
    ppermute x13, waiting for transfers between devices, send(): return lax.ppermute(x, 'ab', pairs)  70.3 us
    ppermute x13, starting transfers between devices, send(): return lax.ppermute(x, 'ab', pairs)  23 us
    pallas_call x4, Pallas kernels, product(): pl.pallas_call(functools.partial(product_kernel, [len(candidates) for can...  19.3 us
    ppermute x6, starting transfers between devices, chip_sum_direct(): total += lax.ppermute(take(blocks, chip ^ flip, 0), 'cd', pairs)  8.2 us
    ppermute x8, waiting for transfers between devices, halve(): lax.ppermute(take(blocks, 1 - mine, axis), 'cd', pairs)  7.42 us
    unnamed x24, local copies, waits for them, and re-layouts  7.42 us
    ppermute x8, starting transfers between devices, halve(): lax.ppermute(take(blocks, 1 - mine, axis), 'cd', pairs)  6.2 us
    squeeze x11, local copies, waits for them, and re-layouts, take(): return lax.dynamic_index_in_dim(blocks, at, axis, keepdims=False)  5.17 us
  transfers between devices with their start and end apart: 27, of which 12 were waited for; matrix products, arithmetic and copies ran while one was open for 10% of the time, Pallas kernels for 13%

profile of v4, /device:TPU:0, one launch (start us, length us, event | category | flops | bytes accessed | tf_op | source)
XLA Modules:
  0.0 169.0 jit_solution(9607269941712422825)
XLA Ops:
  0.0 2.8 %slice.18 = f32[256,1536]{1,0:T(8,128)} slice(f32[256,2048]{1,0:T(8,128)} %left_ref.1), slice={[0:256], [0:1536]} | slice | bytes 3145728 | tf_op jit(solution)/shard_map/slice | solution.py:141
  2.8 3.0 %collective-permute-start.2 = (f32[256,1536]{1,0:T(8,128)}, f32[256,1536]{1,0:T(8,128)}, u32[]{:S(2)}, u32[]{:S(2)}) collective-permute-start(f32[256,1536]{1,0:T(8,128)} %slice.18), channel_id=1, source_target_pairs={{0,1},{1,0},{2,3},{3,2},{4,5},{5,4},{6,7},{7,6},{8,9},{9,8},{10,11... | collective-permute-start | bytes 4718600 | tf_op jit(solution)/shard_map/ppermute | solution.py:179
  5.8 1.8 %collective-permute-start = (f32[256,1536]{1,0:T(8,128)}, f32[256,1536]{1,0:T(8,128)}, u32[]{:S(2)}, u32[]{:S(2)}) collective-permute-start(f32[256,1536]{1,0:T(8,128)} %slice.18), channel_id=1, source_target_pairs={{1,2},{2,1},{5,6},{6,5},{9,10},{10,9},{13,14},{14,13},{17,18},{18,... | collective-permute-start | bytes 4718600 | tf_op jit(solution)/shard_map/ppermute | solution.py:179
  7.7 3.4 %copy-done.2 = f32[2048,1024]{1,0:T(8,128)S(1)} copy-done((f32[2048,1024]{1,0:T(8,128)S(1)}, f32[2048,1024]{1,0:T(8,128)}, u32[]{:S(2)}) %copy-start.2) | copy-done | bytes 8388632
  11.0 3.9 %shard_map.46 = (f32[256,1024]{1,0:T(8,128)S(1)}, bf16[8,256,1024]{2,1,0:T(8,128)(2,1)S(1)}, bf16[8,256,1024]{2,1,0:T(8,128)(2,1)S(1)}) custom-call(s32[8]{0:T(128)S(1)} %copy-done.6, f32[256,2048]{1,0:T(8,128)S(1)} %copy-done.3, f32[8,256,1024]{2,1,0:T(8,128)S(1)} %bitcast.73), custom_call_target="tpu_custom_call" | custom-call | flops 1073741824 | bytes 3145728 | tf_op jit(solution)/shard_map/pallas_call | solution.py:45
  15.0 2.0 %copy-done = bf16[8,256,1024]{2,1,0:T(8,128)(2,1)} copy-done((bf16[8,256,1024]{2,1,0:T(8,128)(2,1)}, bf16[8,256,1024]{2,1,0:T(8,128)(2,1)S(1)}, u32[]{:S(2)}) %copy-start) | copy-done | bytes 4194328
  17.0 2.0 %copy-done.1 = bf16[8,256,1024]{2,1,0:T(8,128)(2,1)} copy-done((bf16[8,256,1024]{2,1,0:T(8,128)(2,1)}, bf16[8,256,1024]{2,1,0:T(8,128)(2,1)S(1)}, u32[]{:S(2)}) %copy-start.1) | copy-done | bytes 4194328
  20.7 3.3 %collective-permute-start.4 = (f32[256,512]{1,0:T(8,128)}, f32[256,512]{1,0:T(8,128)S(1)}, u32[]{:S(2)}, u32[]{:S(2)}) collective-permute-start(f32[256,512]{1,0:T(8,128)} %slice.19), channel_id=1, source_target_pairs={{0,1},{1,0},{2,3},{3,2},{4,5},{5,4},{6,7},{7,6},{8,9},{9,8},{10,11... | collective-permute-start | bytes 1572872 | tf_op jit(solution)/shard_map/ppermute | solution.py:179
  24.6 16.7 %collective-permute-done.2.refs_0_ = f32[256,1536]{1,0:T(8,128)} collective-permute-done((f32[256,1536]{1,0:T(8,128)}, f32[256,1536]{1,0:T(8,128)}, u32[]{:S(2)}, u32[]{:S(2)}) %collective-permute-start.2) | collective-permute-done | bytes 1572896 | tf_op jit(solution)/shard_map/ppermute | solution.py:179
  41.4 1.8 %collective-permute-start.3 = (f32[256,1536]{1,0:T(8,128)}, f32[256,1536]{1,0:T(8,128)}, u32[]{:S(2)}, u32[]{:S(2)}) collective-permute-start(f32[256,1536]{1,0:T(8,128)} %collective-permute-done.2.refs_0_), channel_id=1, source_target_pairs={{1,2},{2,1},{5,6},{6,5},{9,10},{10,9},{13,14},{14,13},{17,18},{18,... | collective-permute-start | bytes 4718600 | tf_op jit(solution)/shard_map/ppermute | solution.py:179
  43.2 1.3 collective-permute-start.1
  44.5 1.1 bitcast_add_fusion.3
  45.6 6.9 %collective-permute-done.4.refs_1_ = f32[256,512]{1,0:T(8,128)S(1)} collective-permute-done((f32[256,512]{1,0:T(8,128)}, f32[256,512]{1,0:T(8,128)S(1)}, u32[]{:S(2)}, u32[]{:S(2)}) %collective-permute-start.4) | collective-permute-done | bytes 524320 | tf_op jit(solution)/shard_map/ppermute | solution.py:179
  52.5 2.0 %collective-permute-start.7 = (f32[2,32,1024]{2,1,0:T(8,128)S(1)}, f32[2,32,1024]{2,1,0:T(8,128)}, u32[]{:S(2)}, u32[]{:S(2)}) collective-permute-start(f32[2,32,1024]{2,1,0:T(8,128)S(1)} %dynamic-slice_bitcast_fusion.5), channel_id=1, source_target_pairs={{0,8},{4,12},{8,0},{12,4},{16,24},{20,28},{24,16},{28,20},{1,9},{5... | collective-permute-start | bytes 786440 | tf_op jit(solution)/shard_map/ppermute | solution.py:151
  54.7 5.3 %shard_map.47 = f32[256,1024]{1,0:T(8,128)S(1)} custom-call(s32[9]{0:T(128)S(1)} %get-tuple-element.70.scalars, f32[256,1536]{1,0:T(8,128)} %collective-permute-done.2.refs_0_, f32[256,512]{1,0:T(8,128)S(1)} %collective-permute-done.4.refs_1_, bf16[8,256,1024]{2,1,0:T(8,128)(2,1)} %copy-done, bf16[8,256,1024]{2,1,0:T(8,128)(2,1)} %copy-done.1), custom_call_target="tpu_custom_call" | custom-call | flops 1073741824 | bytes 3145728 | tf_op jit(solution)/shard_map/pallas_call | solution.py:116
  60.0 0.8 dynamic-slice_bitcast_fusion.2
  60.9 1.0 bitcast_add_fusion.5
  61.9 1.1 collective-permute-start.8
  63.6 4.3 %collective-permute-done.8 = f32[1,32,1024]{2,1,0:T(8,128)} collective-permute-done((f32[1,32,1024]{2,1,0:T(8,128)S(1)}, f32[1,32,1024]{2,1,0:T(8,128)}, u32[]{:S(2)}, u32[]{:S(2)}) %collective-permute-start.8) | collective-permute-done | bytes 131104 | tf_op jit(solution)/shard_map/ppermute | solution.py:151
  67.9 1.3 collective-permute-start.11
  69.2 0.9 add_bitcast_fusion.1
  70.2 1.3 collective-permute-start.10
  71.5 1.1 bitcast_add_fusion.2
  72.6 13.7 %collective-permute-done.1.refs_0_ = f32[256,1536]{1,0:T(8,128)} collective-permute-done((f32[256,1536]{1,0:T(8,128)}, f32[256,1536]{1,0:T(8,128)}, u32[]{:S(2)}, u32[]{:S(2)}) %collective-permute-start.1) | collective-permute-done | bytes 1572896 | tf_op jit(solution)/shard_map/ppermute | solution.py:179
  86.3 11.1 %collective-permute-done.11.refs_2_ = f32[256,512]{1,0:T(8,128)S(1)} collective-permute-done((f32[256,512]{1,0:T(8,128)S(1)}, f32[256,512]{1,0:T(8,128)S(1)}, u32[]{:S(2)}, u32[]{:S(2)}) %collective-permute-start.11) | collective-permute-done | bytes 524320 | tf_op jit(solution)/shard_map/ppermute | solution.py:179
  97.5 2.0 %collective-permute-start.13 = (f32[2,32,1024]{2,1,0:T(8,128)S(1)}, f32[2,32,1024]{2,1,0:T(8,128)S(1)}, u32[]{:S(2)}, u32[]{:S(2)}) collective-permute-start(f32[2,32,1024]{2,1,0:T(8,128)S(1)} %dynamic-slice_bitcast_fusion.4), channel_id=1, source_target_pairs={{0,8},{4,12},{8,0},{12,4},{16,24},{20,28},{24,16},{28,20},{1,9},{5... | collective-permute-start | bytes 786440 | tf_op jit(solution)/shard_map/ppermute | solution.py:151
  99.5 6.3 %shard_map.48 = f32[256,1024]{1,0:T(8,128)} custom-call(s32[9]{0:T(128)S(1)} %get-tuple-element.69.scalars, f32[256,1536]{1,0:T(8,128)} %collective-permute-done.1.refs_0_, f32[256,1536]{1,0:T(8,128)} %collective-permute-done.3.refs_1_, f32[256,512]{1,0:T(8,128)S(1)} %collective-permute-done.11.refs_2_, f32[256,512]{1,0:T(8,128)S(1)} %collective-permute-done.12.refs_3_, ...), custom_call_target="tpu_custom_call" | custom-call | flops 1073741824 | bytes 3145728 | tf_op jit(solution)/shard_map/pallas_call | solution.py:116
  105.9 1.9 %dynamic-slice_bitcast_fusion.1 = f32[4,32,1024]{2,1,0:T(8,128)} fusion(f32[4,2,32,1024]{3,2,1,0:T(8,128)} %bitcast.81, s32[]{:T(128)S(6)} %select_n.67), kind=kLoop, calls=%fused_computation.7 | loop fusion | bytes 1048580 | tf_op jit(solution)/shard_map/jit(dynamic_index_in_dim)/squeeze | solution.py:145
  108.5 1.0 collective-permute-start.14
  109.5 1.3 slice.20.refs_2_
  110.8 1.3 slice.21.refs_3_
  112.2 1.3 collective-permute-start.17
  113.5 1.2 collective-permute-done.14
  114.7 1.6 add_bitcast_fusion
  116.3 1.3 bitcast_add_fusion.1
  117.5 13.7 %collective-permute-done.10.refs_0_ = f32[256,1536]{1,0:T(8,128)} collective-permute-done((f32[256,1536]{1,0:T(8,128)}, f32[256,1536]{1,0:T(8,128)}, u32[]{:S(2)}, u32[]{:S(2)}) %collective-permute-start.10) | collective-permute-done | bytes 1572896 | tf_op jit(solution)/shard_map/ppermute | solution.py:179
  132.0 2.0 %collective-permute-start.18 = (f32[32,1024]{1,0:T(8,128)}, f32[32,1024]{1,0:T(8,128)S(1)}, u32[]{:S(2)}, u32[]{:S(2)}) collective-permute-start(f32[32,1024]{1,0:T(8,128)} %get-tuple-element.66), channel_id=1, source_target_pairs={{0,8},{4,12},{8,0},{12,4},{16,24},{20,28},{24,16},{28,20},{1,9},{5... | collective-permute-start | bytes 393224 | tf_op jit(solution)/shard_map/ppermute | solution.py:174
  134.0 1.5 collective-permute-start.19
  135.6 6.1 %shard_map.49.refs_4_ = f32[256,1024]{1,0:T(8,128)S(1)} custom-call(s32[7]{0:T(128)S(1)} %pad_add_fusion.2.scalars, f32[256,1536]{1,0:T(8,128)} %collective-permute-done.10.refs_0_, f32[256,1536]{1,0:T(8,128)} %collective-permute-done.refs_1_, bf16[8,256,1024]{2,1,0:T(8,128)(2,1)} %copy-done, bf16[8,256,1024]{2,1,0:T(8,128)(2,1)} %copy-done.1), custom_call_target="tpu_custom_call" | custom-call | flops 805306368 | bytes 2621440 | tf_op jit(solution)/shard_map/pallas_call | solution.py:116
  141.8 1.1 fusion.3
  142.9 1.4 shard_map.50
  144.4 1.9 %collective-permute-done.22 = f32[4,32,1024]{2,1,0:T(8,128)S(1)} collective-permute-done((f32[4,32,1024]{2,1,0:T(8,128)S(1)}, f32[4,32,1024]{2,1,0:T(8,128)S(1)}, u32[]{:S(2)}, u32[]{:S(2)}) %collective-permute-start.22) | collective-permute-done | bytes 524320 | tf_op jit(solution)/shard_map/ppermute | solution.py:151
  146.8 4.4 %collective-permute-start.24 = (f32[32,1024]{1,0:T(8,128)S(1)}, f32[32,1024]{1,0:T(8,128)S(1)}, u32[]{:S(2)}, u32[]{:S(2)}) collective-permute-start(f32[32,1024]{1,0:T(8,128)S(1)} %get-tuple-element.65), channel_id=1, source_target_pairs={{0,16},{4,20},{8,24},{12,28},{16,0},{20,4},{24,8},{28,12},{1,17},{... | collective-permute-start | bytes 393224 | tf_op jit(solution)/shard_map/ppermute | solution.py:174
  151.2 4.2 %collective-permute-start.21 = (f32[32,1024]{1,0:T(8,128)S(1)}, f32[32,1024]{1,0:T(8,128)S(1)}, u32[]{:S(2)}, u32[]{:S(2)}) collective-permute-start(f32[32,1024]{1,0:T(8,128)S(1)} %fusion.3), channel_id=1, source_target_pairs={{0,2},{2,0},{1,3},{3,1},{4,6},{6,4},{5,7},{7,5},{8,10},{10,8},{9,1... | collective-permute-start | bytes 393224 | tf_op jit(solution)/shard_map/ppermute | solution.py:179
  155.3 2.1 %collective-permute-done.24 = f32[32,1024]{1,0:T(8,128)S(1)} collective-permute-done((f32[32,1024]{1,0:T(8,128)S(1)}, f32[32,1024]{1,0:T(8,128)S(1)}, u32[]{:S(2)}, u32[]{:S(2)}) %collective-permute-start.24) | collective-permute-done | bytes 131104 | tf_op jit(solution)/shard_map/ppermute | solution.py:174
  158.1 3.0 %collective-permute-done.21 = f32[32,1024]{1,0:T(8,128)S(1)} collective-permute-done((f32[32,1024]{1,0:T(8,128)S(1)}, f32[32,1024]{1,0:T(8,128)S(1)}, u32[]{:S(2)}, u32[]{:S(2)}) %collective-permute-start.21) | collective-permute-done | bytes 131104 | tf_op jit(solution)/shard_map/ppermute | solution.py:179
  161.1 2.4 %collective-permute-start.26 = (f32[32,1024]{1,0:T(8,128)S(1)}, f32[32,1024]{1,0:T(8,128)S(1)}, u32[]{:S(2)}, u32[]{:S(2)}) collective-permute-start(f32[32,1024]{1,0:T(8,128)S(1)} %fusion.1), channel_id=1, source_target_pairs={{0,3},{3,0},{1,2},{2,1},{4,7},{7,4},{5,6},{6,5},{8,11},{11,8},{9,1... | collective-permute-start | bytes 393224 | tf_op jit(solution)/shard_map/ppermute | solution.py:179
  163.6 4.4 %collective-permute-done.26 = f32[32,1024]{1,0:T(8,128)S(1)} collective-permute-done((f32[32,1024]{1,0:T(8,128)S(1)}, f32[32,1024]{1,0:T(8,128)S(1)}, u32[]{:S(2)}, u32[]{:S(2)}) %collective-permute-start.26) | collective-permute-done | bytes 131104 | tf_op jit(solution)/shard_map/ppermute | solution.py:179
  (66 shorter events, 7.0 us)
Async XLA Ops:
  0.0 7.6 %copy-start.3 = (f32[256,2048]{1,0:T(8,128)S(1)}, f32[256,2048]{1,0:T(8,128)}, u32[]{:S(2)}) copy-start(f32[256,2048]{1,0:T(8,128)} %left_ref.1) | copy-start | bytes 6291460
  0.0 7.6 %copy-start.6 = (s32[8]{0:T(128)S(1)}, s32[8]{0:T(128)}, u32[]{:S(2)}) copy-start(s32[8]{0:T(128)} %live.1) | copy-start | bytes 100
  2.8 38.6 %collective-permute-start.2 = (f32[256,1536]{1,0:T(8,128)}, f32[256,1536]{1,0:T(8,128)}, u32[]{:S(2)}, u32[]{:S(2)}) collective-permute-start(f32[256,1536]{1,0:T(8,128)} %slice.18), channel_id=1, source_target_pairs={{0,1},{1,0},{2,3},{3,2},{4,5},{5,4},{6,7},{7,6},{8,9},{9,8},{10,11... | collective-permute-start | bytes 4718600 | tf_op jit(solution)/shard_map/ppermute | solution.py:179
  5.8 37.4 %collective-permute-start = (f32[256,1536]{1,0:T(8,128)}, f32[256,1536]{1,0:T(8,128)}, u32[]{:S(2)}, u32[]{:S(2)}) collective-permute-start(f32[256,1536]{1,0:T(8,128)} %slice.18), channel_id=1, source_target_pairs={{1,2},{2,1},{5,6},{6,5},{9,10},{10,9},{13,14},{14,13},{17,18},{18,... | collective-permute-start | bytes 4718600 | tf_op jit(solution)/shard_map/ppermute | solution.py:179
  7.7 3.4 %copy-start.2 = (f32[2048,1024]{1,0:T(8,128)S(1)}, f32[2048,1024]{1,0:T(8,128)}, u32[]{:S(2)}) copy-start(f32[2048,1024]{1,0:T(8,128)} %param.5) | copy-start | bytes 25165828
  15.0 2.0 %copy-start = (bf16[8,256,1024]{2,1,0:T(8,128)(2,1)}, bf16[8,256,1024]{2,1,0:T(8,128)(2,1)S(1)}, u32[]{:S(2)}) copy-start(bf16[8,256,1024]{2,1,0:T(8,128)(2,1)S(1)} %get-tuple-element.37.refs_2_.refs_4_) | copy-start | bytes 12582916
  16.9 2.0 %copy-start.1 = (bf16[8,256,1024]{2,1,0:T(8,128)(2,1)}, bf16[8,256,1024]{2,1,0:T(8,128)(2,1)S(1)}, u32[]{:S(2)}) copy-start(bf16[8,256,1024]{2,1,0:T(8,128)(2,1)S(1)} %get-tuple-element.38.refs_3_.refs_5_) | copy-start | bytes 12582916
  19.8 24.7 %collective-permute-start.6 = (f32[4,32,1024]{2,1,0:T(8,128)}, f32[4,32,1024]{2,1,0:T(8,128)}, u32[]{:S(2)}, u32[]{:S(2)}) collective-permute-start(f32[4,32,1024]{2,1,0:T(8,128)} %dynamic-slice_bitcast_fusion.3), channel_id=1, source_target_pairs={{0,4},{4,0},{8,12},{12,8},{16,20},{20,16},{24,28},{28,24},{1,5},{5... | collective-permute-start | bytes 1572872 | tf_op jit(solution)/shard_map/ppermute | solution.py:151
  20.7 31.8 %collective-permute-start.4 = (f32[256,512]{1,0:T(8,128)}, f32[256,512]{1,0:T(8,128)S(1)}, u32[]{:S(2)}, u32[]{:S(2)}) collective-permute-start(f32[256,512]{1,0:T(8,128)} %slice.19), channel_id=1, source_target_pairs={{0,1},{1,0},{2,3},{3,2},{4,5},{5,4},{6,7},{7,6},{8,9},{9,8},{10,11... | collective-permute-start | bytes 1572872 | tf_op jit(solution)/shard_map/ppermute | solution.py:179
  23.9 28.6 %collective-permute-start.5 = (f32[256,512]{1,0:T(8,128)}, f32[256,512]{1,0:T(8,128)S(1)}, u32[]{:S(2)}, u32[]{:S(2)}) collective-permute-start(f32[256,512]{1,0:T(8,128)} %slice.19), channel_id=1, source_target_pairs={{1,2},{2,1},{5,6},{6,5},{9,10},{10,9},{13,14},{14,13},{17,18},{18,... | collective-permute-start | bytes 1572872 | tf_op jit(solution)/shard_map/ppermute | solution.py:179
  41.4 28.8 %collective-permute-start.3 = (f32[256,1536]{1,0:T(8,128)}, f32[256,1536]{1,0:T(8,128)}, u32[]{:S(2)}, u32[]{:S(2)}) collective-permute-start(f32[256,1536]{1,0:T(8,128)} %collective-permute-done.2.refs_0_), channel_id=1, source_target_pairs={{1,2},{2,1},{5,6},{6,5},{9,10},{10,9},{13,14},{14,13},{17,18},{18,... | collective-permute-start | bytes 4718600 | tf_op jit(solution)/shard_map/ppermute | solution.py:179
  43.2 43.1 %collective-permute-start.1 = (f32[256,1536]{1,0:T(8,128)}, f32[256,1536]{1,0:T(8,128)}, u32[]{:S(2)}, u32[]{:S(2)}) collective-permute-start(f32[256,1536]{1,0:T(8,128)} %collective-permute-done.refs_1_), channel_id=1, source_target_pairs={{1,0},{2,3},{5,4},{6,7},{9,8},{10,11},{13,12},{14,15},{17,16},{18,... | collective-permute-start | bytes 4718600 | tf_op jit(solution)/shard_map/ppermute | solution.py:179
  45.6 9.0 %copy-start.8 = (f32[4,32,1024]{2,1,0:T(8,128)}, f32[4,32,1024]{2,1,0:T(8,128)S(1)}, u32[]{:S(2)}) copy-start(f32[4,32,1024]{2,1,0:T(8,128)S(1)} %bitcast_add_fusion.3) | copy-start | bytes 1572868
  52.5 15.4 %copy-start.4 = (f32[256,512]{1,0:T(8,128)}, f32[256,512]{1,0:T(8,128)S(1)}, u32[]{:S(2)}) copy-start(f32[256,512]{1,0:T(8,128)S(1)} %collective-permute-done.5.refs_1_) | copy-start | bytes 1572868
  52.5 8.3 %collective-permute-start.7 = (f32[2,32,1024]{2,1,0:T(8,128)S(1)}, f32[2,32,1024]{2,1,0:T(8,128)}, u32[]{:S(2)}, u32[]{:S(2)}) collective-permute-start(f32[2,32,1024]{2,1,0:T(8,128)S(1)} %dynamic-slice_bitcast_fusion.5), channel_id=1, source_target_pairs={{0,8},{4,12},{8,0},{12,4},{16,24},{20,28},{24,16},{28,20},{1,9},{5... | collective-permute-start | bytes 786440 | tf_op jit(solution)/shard_map/ppermute | solution.py:151
  54.6 6.2 %copy-start.9 = (f32[4,32,1024]{2,1,0:T(8,128)S(1)}, f32[4,32,1024]{2,1,0:T(8,128)}, u32[]{:S(2)}) copy-start(f32[4,32,1024]{2,1,0:T(8,128)} %copy-done.8) | copy-start | bytes 1572868
  60.8 10.6 %collective-permute-start.9 = (f32[4,32,1024]{2,1,0:T(8,128)}, f32[4,32,1024]{2,1,0:T(8,128)}, u32[]{:S(2)}, u32[]{:S(2)}) collective-permute-start(f32[4,32,1024]{2,1,0:T(8,128)} %dynamic-slice_bitcast_fusion.2), channel_id=1, source_target_pairs={{0,4},{4,0},{8,12},{12,8},{16,20},{20,16},{24,28},{28,24},{1,5},{5... | collective-permute-start | bytes 1572872 | tf_op jit(solution)/shard_map/ppermute | solution.py:151
  61.9 6.1 %collective-permute-start.8 = (f32[1,32,1024]{2,1,0:T(8,128)S(1)}, f32[1,32,1024]{2,1,0:T(8,128)}, u32[]{:S(2)}, u32[]{:S(2)}) collective-permute-start(f32[1,32,1024]{2,1,0:T(8,128)S(1)} %constant_dynamic-slice_fusion.1), channel_id=1, source_target_pairs={{0,16},{4,20},{8,24},{12,28},{16,0},{20,4},{24,8},{28,12},{1,17},{... | collective-permute-start | bytes 393224 | tf_op jit(solution)/shard_map/ppermute | solution.py:151
  62.9 23.4 %collective-permute-start.12 = (f32[256,512]{1,0:T(8,128)S(1)}, f32[256,512]{1,0:T(8,128)S(1)}, u32[]{:S(2)}, u32[]{:S(2)}) collective-permute-start(f32[256,512]{1,0:T(8,128)S(1)} %collective-permute-done.4.refs_1_), channel_id=1, source_target_pairs={{1,2},{2,1},{5,6},{6,5},{9,10},{10,9},{13,14},{14,13},{17,18},{18,... | collective-permute-start | bytes 1572872 | tf_op jit(solution)/shard_map/ppermute | solution.py:179
  67.9 29.5 %collective-permute-start.11 = (f32[256,512]{1,0:T(8,128)S(1)}, f32[256,512]{1,0:T(8,128)S(1)}, u32[]{:S(2)}, u32[]{:S(2)}) collective-permute-start(f32[256,512]{1,0:T(8,128)S(1)} %collective-permute-done.5.refs_1_), channel_id=1, source_target_pairs={{1,0},{2,3},{5,4},{6,7},{9,8},{10,11},{13,12},{14,15},{17,16},{18,... | collective-permute-start | bytes 1572872 | tf_op jit(solution)/shard_map/ppermute | solution.py:179
  70.2 61.1 %collective-permute-start.10 = (f32[256,1536]{1,0:T(8,128)}, f32[256,1536]{1,0:T(8,128)}, u32[]{:S(2)}, u32[]{:S(2)}) collective-permute-start(f32[256,1536]{1,0:T(8,128)} %collective-permute-done.3.refs_1_), channel_id=1, source_target_pairs={{1,0},{2,3},{5,4},{6,7},{9,8},{10,11},{13,12},{14,15},{17,16},{18,... | collective-permute-start | bytes 4718600 | tf_op jit(solution)/shard_map/ppermute | solution.py:179
  97.5 10.3 %collective-permute-start.13 = (f32[2,32,1024]{2,1,0:T(8,128)S(1)}, f32[2,32,1024]{2,1,0:T(8,128)S(1)}, u32[]{:S(2)}, u32[]{:S(2)}) collective-permute-start(f32[2,32,1024]{2,1,0:T(8,128)S(1)} %dynamic-slice_bitcast_fusion.4), channel_id=1, source_target_pairs={{0,8},{4,12},{8,0},{12,4},{16,24},{20,28},{24,16},{28,20},{1,9},{5... | collective-permute-start | bytes 786440 | tf_op jit(solution)/shard_map/ppermute | solution.py:151
  107.8 8.5 %collective-permute-start.15 = (f32[4,32,1024]{2,1,0:T(8,128)}, f32[4,32,1024]{2,1,0:T(8,128)}, u32[]{:S(2)}, u32[]{:S(2)}) collective-permute-start(f32[4,32,1024]{2,1,0:T(8,128)} %dynamic-slice_bitcast_fusion.1), channel_id=1, source_target_pairs={{0,4},{4,0},{8,12},{12,8},{16,20},{20,16},{24,28},{28,24},{1,5},{5... | collective-permute-start | bytes 1572872 | tf_op jit(solution)/shard_map/ppermute | solution.py:151
  108.5 6.2 %collective-permute-start.14 = (f32[1,32,1024]{2,1,0:T(8,128)}, f32[1,32,1024]{2,1,0:T(8,128)}, u32[]{:S(2)}, u32[]{:S(2)}) collective-permute-start(f32[1,32,1024]{2,1,0:T(8,128)} %constant_dynamic-slice_fusion), channel_id=1, source_target_pairs={{0,16},{4,20},{8,24},{12,28},{16,0},{20,4},{24,8},{28,12},{1,17},{... | collective-permute-start | bytes 393224 | tf_op jit(solution)/shard_map/ppermute | solution.py:151
  112.2 30.6 %collective-permute-start.17 = (f32[256,512]{1,0:T(8,128)S(1)}, f32[256,512]{1,0:T(8,128)S(1)}, u32[]{:S(2)}, u32[]{:S(2)}) collective-permute-start(f32[256,512]{1,0:T(8,128)S(1)} %collective-permute-done.12.refs_3_), channel_id=1, source_target_pairs={{1,0},{2,3},{5,4},{6,7},{9,8},{10,11},{13,12},{14,15},{17,16},{18,... | collective-permute-start | bytes 1572872 | tf_op jit(solution)/shard_map/ppermute | solution.py:179
  117.5 18.0 %copy-start.7 = (f32[4,32,1024]{2,1,0:T(8,128)}, f32[4,32,1024]{2,1,0:T(8,128)S(1)}, u32[]{:S(2)}) copy-start(f32[4,32,1024]{2,1,0:T(8,128)S(1)} %bitcast_add_fusion.1) | copy-start | bytes 1572868
  132.0 9.7 %collective-permute-start.18 = (f32[32,1024]{1,0:T(8,128)}, f32[32,1024]{1,0:T(8,128)S(1)}, u32[]{:S(2)}, u32[]{:S(2)}) collective-permute-start(f32[32,1024]{1,0:T(8,128)} %get-tuple-element.66), channel_id=1, source_target_pairs={{0,8},{4,12},{8,0},{12,4},{16,24},{20,28},{24,16},{28,20},{1,9},{5... | collective-permute-start | bytes 393224 | tf_op jit(solution)/shard_map/ppermute | solution.py:174
  134.0 7.8 %collective-permute-start.19 = (f32[32,1024]{1,0:T(8,128)}, f32[32,1024]{1,0:T(8,128)}, u32[]{:S(2)}, u32[]{:S(2)}) collective-permute-start(f32[32,1024]{1,0:T(8,128)} %get-tuple-element.68), channel_id=1, source_target_pairs={{0,16},{4,20},{8,24},{12,28},{16,0},{20,4},{24,8},{28,12},{1,17},{... | collective-permute-start | bytes 393224 | tf_op jit(solution)/shard_map/ppermute | solution.py:174
  135.5 6.3 %collective-permute-start.20 = (f32[32,1024]{1,0:T(8,128)S(1)}, f32[32,1024]{1,0:T(8,128)}, u32[]{:S(2)}, u32[]{:S(2)}) collective-permute-start(f32[32,1024]{1,0:T(8,128)S(1)} %get-tuple-element.67), channel_id=1, source_target_pairs={{0,24},{4,28},{8,16},{12,20},{16,8},{20,12},{24,0},{28,4},{1,25},{... | collective-permute-start | bytes 393224 | tf_op jit(solution)/shard_map/ppermute | solution.py:174
  135.6 7.3 %copy-start.5 = (f32[256,512]{1,0:T(8,128)S(1)}, f32[256,512]{1,0:T(8,128)}, u32[]{:S(2)}) copy-start(f32[256,512]{1,0:T(8,128)} %copy-done.4) | copy-start | bytes 1572868
  144.3 6.9 %copy-start.11 = (f32[32,1024]{1,0:T(8,128)S(1)}, f32[32,1024]{1,0:T(8,128)}, u32[]{:S(2)}) copy-start(f32[32,1024]{1,0:T(8,128)} %add_bitcast_fusion) | copy-start | bytes 393220
  144.4 2.0 %collective-permute-start.22 = (f32[4,32,1024]{2,1,0:T(8,128)S(1)}, f32[4,32,1024]{2,1,0:T(8,128)S(1)}, u32[]{:S(2)}, u32[]{:S(2)}) collective-permute-start(f32[4,32,1024]{2,1,0:T(8,128)S(1)} %dynamic-slice_bitcast_fusion), channel_id=1, source_target_pairs={{0,4},{4,0},{8,12},{12,8},{16,20},{20,16},{24,28},{28,24},{1,5},{5... | collective-permute-start | bytes 1572872 | tf_op jit(solution)/shard_map/ppermute | solution.py:151
  146.4 21.7 %copy-start.10 = (f32[32,4096]{1,0:T(8,128)S(1)}, f32[32,4096]{1,0:T(8,128)}, u32[]{:S(2)}) copy-start(f32[32,4096]{1,0:T(8,128)} %param.7) | copy-start | bytes 1572868
  146.5 8.9 %collective-permute-start.23 = (f32[32,1024]{1,0:T(8,128)S(1)}, f32[32,1024]{1,0:T(8,128)S(1)}, u32[]{:S(2)}, u32[]{:S(2)}) collective-permute-start(f32[32,1024]{1,0:T(8,128)S(1)} %get-tuple-element.63), channel_id=1, source_target_pairs={{0,8},{4,12},{8,0},{12,4},{16,24},{20,28},{24,16},{28,20},{1,9},{5... | collective-permute-start | bytes 393224 | tf_op jit(solution)/shard_map/ppermute | solution.py:174
  146.8 10.7 %collective-permute-start.24 = (f32[32,1024]{1,0:T(8,128)S(1)}, f32[32,1024]{1,0:T(8,128)S(1)}, u32[]{:S(2)}, u32[]{:S(2)}) collective-permute-start(f32[32,1024]{1,0:T(8,128)S(1)} %get-tuple-element.65), channel_id=1, source_target_pairs={{0,16},{4,20},{8,24},{12,28},{16,0},{20,4},{24,8},{28,12},{1,17},{... | collective-permute-start | bytes 393224 | tf_op jit(solution)/shard_map/ppermute | solution.py:174
  151.2 6.3 %collective-permute-start.25 = (f32[32,1024]{1,0:T(8,128)S(1)}, f32[32,1024]{1,0:T(8,128)S(1)}, u32[]{:S(2)}, u32[]{:S(2)}) collective-permute-start(f32[32,1024]{1,0:T(8,128)S(1)} %get-tuple-element.64), channel_id=1, source_target_pairs={{0,24},{4,28},{8,16},{12,20},{16,8},{20,12},{24,0},{28,4},{1,25},{... | collective-permute-start | bytes 393224 | tf_op jit(solution)/shard_map/ppermute | solution.py:174
  151.2 7.0 %collective-permute-start.16 = (f32[32,1024]{1,0:T(8,128)S(1)}, f32[32,1024]{1,0:T(8,128)S(1)}, u32[]{:S(2)}, u32[]{:S(2)}) collective-permute-start(f32[32,1024]{1,0:T(8,128)S(1)} %copy-done.11), channel_id=1, source_target_pairs={{0,1},{1,0},{2,3},{3,2},{4,5},{5,4},{6,7},{7,6},{8,9},{9,8},{10,11... | collective-permute-start | bytes 393224 | tf_op jit(solution)/shard_map/ppermute | solution.py:179
  151.2 10.0 %collective-permute-start.21 = (f32[32,1024]{1,0:T(8,128)S(1)}, f32[32,1024]{1,0:T(8,128)S(1)}, u32[]{:S(2)}, u32[]{:S(2)}) collective-permute-start(f32[32,1024]{1,0:T(8,128)S(1)} %fusion.3), channel_id=1, source_target_pairs={{0,2},{2,0},{1,3},{3,1},{4,6},{6,4},{5,7},{7,5},{8,10},{10,8},{9,1... | collective-permute-start | bytes 393224 | tf_op jit(solution)/shard_map/ppermute | solution.py:179
  161.1 6.9 %collective-permute-start.26 = (f32[32,1024]{1,0:T(8,128)S(1)}, f32[32,1024]{1,0:T(8,128)S(1)}, u32[]{:S(2)}, u32[]{:S(2)}) collective-permute-start(f32[32,1024]{1,0:T(8,128)S(1)} %fusion.1), channel_id=1, source_target_pairs={{0,3},{3,0},{1,2},{2,1},{4,7},{7,4},{5,6},{6,5},{8,11},{11,8},{9,1... | collective-permute-start | bytes 393224 | tf_op jit(solution)/shard_map/ppermute | solution.py:179

commit v5 on v4

--- a/solution.py
+++ b/solution.py
@@ -35,6 +35,11 @@
     def _():
         high_ref[0], low_ref[0] = split(right_ref[0])
         multiply_add(out_ref, left_ref[...], high_ref[0], low_ref[0])
+
+    @pl.when(live[step] == 0)
+    def _():
+        high_ref[...] = jnp.zeros_like(high_ref)
+        low_ref[...] = jnp.zeros_like(low_ref)
 
 
 def first_product(left, right, live):
@@ -94,16 +99,22 @@
     step = 0
     for i, left in enumerate(lefts):
         left_copies[i].wait()
-        for tile in range(left.shape[1] // TILE):
-            for copy in right_copies[step]:
-                copy.wait()
-
-            @pl.when(scalars[1 + step] > 0)
+        tiles = left.shape[1] // TILE
+        for tile in range(0, tiles, 2):
+            count = min(2, tiles - tile)
+            for copy in right_copies[step : step + count]:
+                copy[0].wait()
+                copy[1].wait()
+            alive = [scalars[1 + step + j] for j in range(count)]
+
+            @pl.when(sum(alive) > 0)
             def _():
-                left_tile = left[:, tile * TILE : (tile + 1) * TILE]
-                multiply_add(out_ref, left_tile, high[step], low[step])
-
-            step += 1
+                pieces = [left[:, (tile + j) * TILE : (tile + j + 1) * TILE] for j in range(count)]
+                pieces = [jnp.where(x > 0, piece, 0.0) for x, piece in zip(alive, pieces)]
+                rights = [x[step : step + count].reshape(count * TILE, -1) for x in (high, low)]
+                multiply_add(out_ref, jnp.concatenate(pieces, axis=1), *rights)
+
+            step += count
 
 
 def product(lists, which, right, live, added=None):

time: 170 us -> 170 us (level)
  starting transfers between devices: 37.4 us -> 43.5 us
  waiting for transfers between devices: 79.8 us -> 75.7 us
  Pallas kernels: 23.2 us -> 21.1 us
    ppermute x8, starting transfers between devices: 6.2 us -> 11.8 us  [halve(): lax.ppermute(take(blocks, 1 - mine, axis), 'cd', pairs)]
    ppermute x13, waiting for transfers between devices: 70.3 us -> 67.3 us  [send(): return lax.ppermute(x, 'ab', pairs)]
    pallas_call x4, Pallas kernels: 19.3 us -> 17.5 us  [product(): pl.pallas_call(functools.partial(product_kernel, [len(candidates) for can...]
  transfers between devices with their start and end apart: 27 -> 27, of which waited for: 12 -> 13; matrix products, arithmetic and copies ran while one was open for 10% -> 10% of each run, Pallas kernels for 13% -> 12%
where the time goes in v5:
time: 170 us; the launch traced here: 169 us
  waiting for transfers between devices  75.7 us (45%)
  starting transfers between devices  43.5 us (26%)
  Pallas kernels  21.1 us (12%)
  local copies, waits for them, and re-layouts  18.9 us (11%)
  other arithmetic  9.27 us (5%)
    ppermute x13, waiting for transfers between devices, send(): return lax.ppermute(x, 'ab', pairs)  67.3 us
    ppermute x13, starting transfers between devices, send(): return lax.ppermute(x, 'ab', pairs)  22.7 us
    pallas_call x4, Pallas kernels, product(): pl.pallas_call(functools.partial(product_kernel, [len(candidates) for can...  17.5 us
    ppermute x8, starting transfers between devices, halve(): lax.ppermute(take(blocks, 1 - mine, axis), 'cd', pairs)  11.8 us
    ppermute x6, starting transfers between devices, chip_sum_direct(): total += lax.ppermute(take(blocks, chip ^ flip, 0), 'cd', pairs)  8.98 us
    unnamed x24, local copies, waits for them, and re-layouts  7.42 us
    ppermute x8, waiting for transfers between devices, halve(): lax.ppermute(take(blocks, 1 - mine, axis), 'cd', pairs)  5.91 us
    squeeze x11, local copies, waits for them, and re-layouts, take(): return lax.dynamic_index_in_dim(blocks, at, axis, keepdims=False)  5.17 us
  transfers between devices with their start and end apart: 27, of which 13 were waited for; matrix products, arithmetic and copies ran while one was open for 10% of the time, Pallas kernels for 12%

profile of v5, /device:TPU:0, one launch (start us, length us, event | category | flops | bytes accessed | tf_op | source)
XLA Modules:
  0.0 168.9 jit_solution(1862735114837738605)
XLA Ops:
  0.0 2.8 %slice.18 = f32[256,1536]{1,0:T(8,128)} slice(f32[256,2048]{1,0:T(8,128)} %left_ref.1), slice={[0:256], [0:1536]} | slice | bytes 3145728 | tf_op jit(solution)/shard_map/slice | solution.py:152
  2.8 3.0 %collective-permute-start.2 = (f32[256,1536]{1,0:T(8,128)}, f32[256,1536]{1,0:T(8,128)}, u32[]{:S(2)}, u32[]{:S(2)}) collective-permute-start(f32[256,1536]{1,0:T(8,128)} %slice.18), channel_id=1, source_target_pairs={{0,1},{1,0},{2,3},{3,2},{4,5},{5,4},{6,7},{7,6},{8,9},{9,8},{10,11... | collective-permute-start | bytes 4718600 | tf_op jit(solution)/shard_map/ppermute | solution.py:190
  5.8 1.8 %collective-permute-start = (f32[256,1536]{1,0:T(8,128)}, f32[256,1536]{1,0:T(8,128)}, u32[]{:S(2)}, u32[]{:S(2)}) collective-permute-start(f32[256,1536]{1,0:T(8,128)} %slice.18), channel_id=1, source_target_pairs={{1,2},{2,1},{5,6},{6,5},{9,10},{10,9},{13,14},{14,13},{17,18},{18,... | collective-permute-start | bytes 4718600 | tf_op jit(solution)/shard_map/ppermute | solution.py:190
  7.7 3.4 %copy-done.2 = f32[2048,1024]{1,0:T(8,128)S(1)} copy-done((f32[2048,1024]{1,0:T(8,128)S(1)}, f32[2048,1024]{1,0:T(8,128)}, u32[]{:S(2)}) %copy-start.2) | copy-done | bytes 8388632
  11.0 3.7 %shard_map.46 = (f32[256,1024]{1,0:T(8,128)S(1)}, bf16[8,256,1024]{2,1,0:T(8,128)(2,1)S(1)}, bf16[8,256,1024]{2,1,0:T(8,128)(2,1)S(1)}) custom-call(s32[8]{0:T(128)S(1)} %copy-done.6, f32[256,2048]{1,0:T(8,128)S(1)} %copy-done.3, f32[8,256,1024]{2,1,0:T(8,128)S(1)} %bitcast.73), custom_call_target="tpu_custom_call" | custom-call | flops 1073741824 | bytes 3145728 | tf_op jit(solution)/shard_map/pallas_call | solution.py:50
  14.7 2.0 %copy-done = bf16[8,256,1024]{2,1,0:T(8,128)(2,1)} copy-done((bf16[8,256,1024]{2,1,0:T(8,128)(2,1)}, bf16[8,256,1024]{2,1,0:T(8,128)(2,1)S(1)}, u32[]{:S(2)}) %copy-start) | copy-done | bytes 4194328
  16.7 2.0 %copy-done.1 = bf16[8,256,1024]{2,1,0:T(8,128)(2,1)} copy-done((bf16[8,256,1024]{2,1,0:T(8,128)(2,1)}, bf16[8,256,1024]{2,1,0:T(8,128)(2,1)S(1)}, u32[]{:S(2)}) %copy-start.1) | copy-done | bytes 4194328
  19.6 1.1 collective-permute-start.6
  21.5 3.0 %collective-permute-start.4 = (f32[256,512]{1,0:T(8,128)}, f32[256,512]{1,0:T(8,128)S(1)}, u32[]{:S(2)}, u32[]{:S(2)}) collective-permute-start(f32[256,512]{1,0:T(8,128)} %slice.19), channel_id=1, source_target_pairs={{0,1},{1,0},{2,3},{3,2},{4,5},{5,4},{6,7},{7,6},{8,9},{9,8},{10,11... | collective-permute-start | bytes 1572872 | tf_op jit(solution)/shard_map/ppermute | solution.py:190
  25.2 16.2 %collective-permute-done.2.refs_0_ = f32[256,1536]{1,0:T(8,128)} collective-permute-done((f32[256,1536]{1,0:T(8,128)}, f32[256,1536]{1,0:T(8,128)}, u32[]{:S(2)}, u32[]{:S(2)}) %collective-permute-start.2) | collective-permute-done | bytes 1572896 | tf_op jit(solution)/shard_map/ppermute | solution.py:190
  41.4 1.8 %collective-permute-start.3 = (f32[256,1536]{1,0:T(8,128)}, f32[256,1536]{1,0:T(8,128)}, u32[]{:S(2)}, u32[]{:S(2)}) collective-permute-start(f32[256,1536]{1,0:T(8,128)} %collective-permute-done.2.refs_0_), channel_id=1, source_target_pairs={{1,2},{2,1},{5,6},{6,5},{9,10},{10,9},{13,14},{14,13},{17,18},{18,... | collective-permute-start | bytes 4718600 | tf_op jit(solution)/shard_map/ppermute | solution.py:190
  43.2 1.3 collective-permute-start.1
  44.5 1.1 bitcast_add_fusion.3
  45.6 6.9 %collective-permute-done.4.refs_1_ = f32[256,512]{1,0:T(8,128)S(1)} collective-permute-done((f32[256,512]{1,0:T(8,128)}, f32[256,512]{1,0:T(8,128)S(1)}, u32[]{:S(2)}, u32[]{:S(2)}) %collective-permute-start.4) | collective-permute-done | bytes 524320 | tf_op jit(solution)/shard_map/ppermute | solution.py:190
  52.5 2.0 %collective-permute-start.7 = (f32[2,32,1024]{2,1,0:T(8,128)S(1)}, f32[2,32,1024]{2,1,0:T(8,128)}, u32[]{:S(2)}, u32[]{:S(2)}) collective-permute-start(f32[2,32,1024]{2,1,0:T(8,128)S(1)} %dynamic-slice_bitcast_fusion.5), channel_id=1, source_target_pairs={{0,8},{4,12},{8,0},{12,4},{16,24},{20,28},{24,16},{28,20},{1,9},{5... | collective-permute-start | bytes 786440 | tf_op jit(solution)/shard_map/ppermute | solution.py:162
  54.7 4.9 %shard_map.47 = f32[256,1024]{1,0:T(8,128)S(1)} custom-call(s32[9]{0:T(128)S(1)} %get-tuple-element.70.scalars, f32[256,1536]{1,0:T(8,128)} %collective-permute-done.2.refs_0_, f32[256,512]{1,0:T(8,128)S(1)} %collective-permute-done.4.refs_1_, bf16[8,256,1024]{2,1,0:T(8,128)(2,1)} %copy-done, bf16[8,256,1024]{2,1,0:T(8,128)(2,1)} %copy-done.1), custom_call_target="tpu_custom_call" | custom-call | flops 1073741824 | bytes 3145728 | tf_op jit(solution)/shard_map/pallas_call | solution.py:127
  60.4 1.0 bitcast_add_fusion.5
  61.5 3.3 %collective-permute-start.8 = (f32[1,32,1024]{2,1,0:T(8,128)S(1)}, f32[1,32,1024]{2,1,0:T(8,128)}, u32[]{:S(2)}, u32[]{:S(2)}) collective-permute-start(f32[1,32,1024]{2,1,0:T(8,128)S(1)} %constant_dynamic-slice_fusion.1), channel_id=1, source_target_pairs={{0,16},{4,20},{8,24},{12,28},{16,0},{20,4},{24,8},{28,12},{1,17},{... | collective-permute-start | bytes 393224 | tf_op jit(solution)/shard_map/ppermute | solution.py:162
  65.4 3.6 %collective-permute-done.8 = f32[1,32,1024]{2,1,0:T(8,128)} collective-permute-done((f32[1,32,1024]{2,1,0:T(8,128)S(1)}, f32[1,32,1024]{2,1,0:T(8,128)}, u32[]{:S(2)}, u32[]{:S(2)}) %collective-permute-start.8) | collective-permute-done | bytes 131104 | tf_op jit(solution)/shard_map/ppermute | solution.py:162
  69.0 1.3 collective-permute-start.11
  70.3 0.9 add_bitcast_fusion.1
  71.3 1.3 collective-permute-start.10
  72.6 1.1 bitcast_add_fusion.2
  73.7 12.6 %collective-permute-done.1.refs_0_ = f32[256,1536]{1,0:T(8,128)} collective-permute-done((f32[256,1536]{1,0:T(8,128)}, f32[256,1536]{1,0:T(8,128)}, u32[]{:S(2)}, u32[]{:S(2)}) %collective-permute-start.1) | collective-permute-done | bytes 1572896 | tf_op jit(solution)/shard_map/ppermute | solution.py:190
  86.3 11.1 %collective-permute-done.11.refs_2_ = f32[256,512]{1,0:T(8,128)S(1)} collective-permute-done((f32[256,512]{1,0:T(8,128)S(1)}, f32[256,512]{1,0:T(8,128)S(1)}, u32[]{:S(2)}, u32[]{:S(2)}) %collective-permute-start.11) | collective-permute-done | bytes 524320 | tf_op jit(solution)/shard_map/ppermute | solution.py:190
  97.5 2.0 %collective-permute-start.13 = (f32[2,32,1024]{2,1,0:T(8,128)S(1)}, f32[2,32,1024]{2,1,0:T(8,128)S(1)}, u32[]{:S(2)}, u32[]{:S(2)}) collective-permute-start(f32[2,32,1024]{2,1,0:T(8,128)S(1)} %dynamic-slice_bitcast_fusion.4), channel_id=1, source_target_pairs={{0,8},{4,12},{8,0},{12,4},{16,24},{20,28},{24,16},{28,20},{1,9},{5... | collective-permute-start | bytes 786440 | tf_op jit(solution)/shard_map/ppermute | solution.py:162
  99.5 5.9 %shard_map.48 = f32[256,1024]{1,0:T(8,128)} custom-call(s32[9]{0:T(128)S(1)} %get-tuple-element.69.scalars, f32[256,1536]{1,0:T(8,128)} %collective-permute-done.1.refs_0_, f32[256,1536]{1,0:T(8,128)} %collective-permute-done.3.refs_1_, f32[256,512]{1,0:T(8,128)S(1)} %collective-permute-done.11.refs_2_, f32[256,512]{1,0:T(8,128)S(1)} %collective-permute-done.12.refs_3_, ...), custom_call_target="tpu_custom_call" | custom-call | flops 1073741824 | bytes 3145728 | tf_op jit(solution)/shard_map/pallas_call | solution.py:127
  105.4 1.9 %dynamic-slice_bitcast_fusion.1 = f32[4,32,1024]{2,1,0:T(8,128)} fusion(f32[4,2,32,1024]{3,2,1,0:T(8,128)} %bitcast.81, s32[]{:T(128)S(6)} %select_n.67), kind=kLoop, calls=%fused_computation.7 | loop fusion | bytes 1048580 | tf_op jit(solution)/shard_map/jit(dynamic_index_in_dim)/squeeze | solution.py:156
  108.0 3.2 %collective-permute-start.14 = (f32[1,32,1024]{2,1,0:T(8,128)}, f32[1,32,1024]{2,1,0:T(8,128)}, u32[]{:S(2)}, u32[]{:S(2)}) collective-permute-start(f32[1,32,1024]{2,1,0:T(8,128)} %constant_dynamic-slice_fusion), channel_id=1, source_target_pairs={{0,16},{4,20},{8,24},{12,28},{16,0},{20,4},{24,8},{28,12},{1,17},{... | collective-permute-start | bytes 393224 | tf_op jit(solution)/shard_map/ppermute | solution.py:162
  111.3 1.3 slice.20.refs_2_
  112.6 1.3 slice.21.refs_3_
  114.1 1.3 collective-permute-start.17
  115.8 1.6 add_bitcast_fusion
  117.3 1.3 bitcast_add_fusion.1
  118.6 12.6 %collective-permute-done.10.refs_0_ = f32[256,1536]{1,0:T(8,128)} collective-permute-done((f32[256,1536]{1,0:T(8,128)}, f32[256,1536]{1,0:T(8,128)}, u32[]{:S(2)}, u32[]{:S(2)}) %collective-permute-start.10) | collective-permute-done | bytes 1572896 | tf_op jit(solution)/shard_map/ppermute | solution.py:190
  132.0 2.0 %collective-permute-start.18 = (f32[32,1024]{1,0:T(8,128)}, f32[32,1024]{1,0:T(8,128)S(1)}, u32[]{:S(2)}, u32[]{:S(2)}) collective-permute-start(f32[32,1024]{1,0:T(8,128)} %get-tuple-element.66), channel_id=1, source_target_pairs={{0,8},{4,12},{8,0},{12,4},{16,24},{20,28},{24,16},{28,20},{1,9},{5... | collective-permute-start | bytes 393224 | tf_op jit(solution)/shard_map/ppermute | solution.py:185
  134.0 1.5 collective-permute-start.19
  135.6 5.8 %shard_map.49.refs_4_ = f32[256,1024]{1,0:T(8,128)S(1)} custom-call(s32[7]{0:T(128)S(1)} %pad_add_fusion.2.scalars, f32[256,1536]{1,0:T(8,128)} %collective-permute-done.10.refs_0_, f32[256,1536]{1,0:T(8,128)} %collective-permute-done.refs_1_, bf16[8,256,1024]{2,1,0:T(8,128)(2,1)} %copy-done, bf16[8,256,1024]{2,1,0:T(8,128)(2,1)} %copy-done.1), custom_call_target="tpu_custom_call" | custom-call | flops 805306368 | bytes 2621440 | tf_op jit(solution)/shard_map/pallas_call | solution.py:127
  141.5 1.1 fusion.3
  142.6 0.9 shard_map.50
  143.6 1.9 %collective-permute-done.22 = f32[4,32,1024]{2,1,0:T(8,128)S(1)} collective-permute-done((f32[4,32,1024]{2,1,0:T(8,128)S(1)}, f32[4,32,1024]{2,1,0:T(8,128)S(1)}, u32[]{:S(2)}, u32[]{:S(2)}) %collective-permute-start.22) | collective-permute-done | bytes 524320 | tf_op jit(solution)/shard_map/ppermute | solution.py:162
  145.6 3.9 %collective-permute-start.23 = (f32[32,1024]{1,0:T(8,128)S(1)}, f32[32,1024]{1,0:T(8,128)S(1)}, u32[]{:S(2)}, u32[]{:S(2)}) collective-permute-start(f32[32,1024]{1,0:T(8,128)S(1)} %get-tuple-element.63), channel_id=1, source_target_pairs={{0,8},{4,12},{8,0},{12,4},{16,24},{20,28},{24,16},{28,20},{1,9},{5... | collective-permute-start | bytes 393224 | tf_op jit(solution)/shard_map/ppermute | solution.py:185
  149.5 1.5 collective-permute-start.24
  151.1 4.2 %collective-permute-start.21 = (f32[32,1024]{1,0:T(8,128)S(1)}, f32[32,1024]{1,0:T(8,128)S(1)}, u32[]{:S(2)}, u32[]{:S(2)}) collective-permute-start(f32[32,1024]{1,0:T(8,128)S(1)} %fusion.3), channel_id=1, source_target_pairs={{0,2},{2,0},{1,3},{3,1},{4,6},{6,4},{5,7},{7,5},{8,10},{10,8},{9,1... | collective-permute-start | bytes 393224 | tf_op jit(solution)/shard_map/ppermute | solution.py:190
  155.2 2.4 %collective-permute-done.24 = f32[32,1024]{1,0:T(8,128)S(1)} collective-permute-done((f32[32,1024]{1,0:T(8,128)S(1)}, f32[32,1024]{1,0:T(8,128)S(1)}, u32[]{:S(2)}, u32[]{:S(2)}) %collective-permute-start.24) | collective-permute-done | bytes 131104 | tf_op jit(solution)/shard_map/ppermute | solution.py:185
  158.0 3.0 %collective-permute-done.21 = f32[32,1024]{1,0:T(8,128)S(1)} collective-permute-done((f32[32,1024]{1,0:T(8,128)S(1)}, f32[32,1024]{1,0:T(8,128)S(1)}, u32[]{:S(2)}, u32[]{:S(2)}) %collective-permute-start.21) | collective-permute-done | bytes 131104 | tf_op jit(solution)/shard_map/ppermute | solution.py:190
  161.0 2.4 %collective-permute-start.26 = (f32[32,1024]{1,0:T(8,128)S(1)}, f32[32,1024]{1,0:T(8,128)S(1)}, u32[]{:S(2)}, u32[]{:S(2)}) collective-permute-start(f32[32,1024]{1,0:T(8,128)S(1)} %fusion.1), channel_id=1, source_target_pairs={{0,3},{3,0},{1,2},{2,1},{4,7},{7,4},{5,6},{6,5},{8,11},{11,8},{9,1... | collective-permute-start | bytes 393224 | tf_op jit(solution)/shard_map/ppermute | solution.py:190
  163.5 4.5 %collective-permute-done.26 = f32[32,1024]{1,0:T(8,128)S(1)} collective-permute-done((f32[32,1024]{1,0:T(8,128)S(1)}, f32[32,1024]{1,0:T(8,128)S(1)}, u32[]{:S(2)}, u32[]{:S(2)}) %collective-permute-start.26) | collective-permute-done | bytes 131104 | tf_op jit(solution)/shard_map/ppermute | solution.py:190
  (66 shorter events, 7.8 us)
Async XLA Ops:
  0.0 7.6 %copy-start.3 = (f32[256,2048]{1,0:T(8,128)S(1)}, f32[256,2048]{1,0:T(8,128)}, u32[]{:S(2)}) copy-start(f32[256,2048]{1,0:T(8,128)} %left_ref.1) | copy-start | bytes 6291460
  0.0 7.6 %copy-start.6 = (s32[8]{0:T(128)S(1)}, s32[8]{0:T(128)}, u32[]{:S(2)}) copy-start(s32[8]{0:T(128)} %live.1) | copy-start | bytes 100
  2.8 38.6 %collective-permute-start.2 = (f32[256,1536]{1,0:T(8,128)}, f32[256,1536]{1,0:T(8,128)}, u32[]{:S(2)}, u32[]{:S(2)}) collective-permute-start(f32[256,1536]{1,0:T(8,128)} %slice.18), channel_id=1, source_target_pairs={{0,1},{1,0},{2,3},{3,2},{4,5},{5,4},{6,7},{7,6},{8,9},{9,8},{10,11... | collective-permute-start | bytes 4718600 | tf_op jit(solution)/shard_map/ppermute | solution.py:190
  5.8 37.4 %collective-permute-start = (f32[256,1536]{1,0:T(8,128)}, f32[256,1536]{1,0:T(8,128)}, u32[]{:S(2)}, u32[]{:S(2)}) collective-permute-start(f32[256,1536]{1,0:T(8,128)} %slice.18), channel_id=1, source_target_pairs={{1,2},{2,1},{5,6},{6,5},{9,10},{10,9},{13,14},{14,13},{17,18},{18,... | collective-permute-start | bytes 4718600 | tf_op jit(solution)/shard_map/ppermute | solution.py:190
  7.7 3.4 %copy-start.2 = (f32[2048,1024]{1,0:T(8,128)S(1)}, f32[2048,1024]{1,0:T(8,128)}, u32[]{:S(2)}) copy-start(f32[2048,1024]{1,0:T(8,128)} %param.5) | copy-start | bytes 25165828
  14.7 2.0 %copy-start = (bf16[8,256,1024]{2,1,0:T(8,128)(2,1)}, bf16[8,256,1024]{2,1,0:T(8,128)(2,1)S(1)}, u32[]{:S(2)}) copy-start(bf16[8,256,1024]{2,1,0:T(8,128)(2,1)S(1)} %get-tuple-element.37.refs_2_.refs_4_) | copy-start | bytes 12582916
  16.7 2.0 %copy-start.1 = (bf16[8,256,1024]{2,1,0:T(8,128)(2,1)}, bf16[8,256,1024]{2,1,0:T(8,128)(2,1)S(1)}, u32[]{:S(2)}) copy-start(bf16[8,256,1024]{2,1,0:T(8,128)(2,1)S(1)} %get-tuple-element.38.refs_3_.refs_5_) | copy-start | bytes 12582916
  19.6 24.9 %collective-permute-start.6 = (f32[4,32,1024]{2,1,0:T(8,128)}, f32[4,32,1024]{2,1,0:T(8,128)}, u32[]{:S(2)}, u32[]{:S(2)}) collective-permute-start(f32[4,32,1024]{2,1,0:T(8,128)} %dynamic-slice_bitcast_fusion.3), channel_id=1, source_target_pairs={{0,4},{4,0},{8,12},{12,8},{16,20},{20,16},{24,28},{28,24},{1,5},{5... | collective-permute-start | bytes 1572872 | tf_op jit(solution)/shard_map/ppermute | solution.py:162
  21.5 31.0 %collective-permute-start.4 = (f32[256,512]{1,0:T(8,128)}, f32[256,512]{1,0:T(8,128)S(1)}, u32[]{:S(2)}, u32[]{:S(2)}) collective-permute-start(f32[256,512]{1,0:T(8,128)} %slice.19), channel_id=1, source_target_pairs={{0,1},{1,0},{2,3},{3,2},{4,5},{5,4},{6,7},{7,6},{8,9},{9,8},{10,11... | collective-permute-start | bytes 1572872 | tf_op jit(solution)/shard_map/ppermute | solution.py:190
  24.5 28.0 %collective-permute-start.5 = (f32[256,512]{1,0:T(8,128)}, f32[256,512]{1,0:T(8,128)S(1)}, u32[]{:S(2)}, u32[]{:S(2)}) collective-permute-start(f32[256,512]{1,0:T(8,128)} %slice.19), channel_id=1, source_target_pairs={{1,2},{2,1},{5,6},{6,5},{9,10},{10,9},{13,14},{14,13},{17,18},{18,... | collective-permute-start | bytes 1572872 | tf_op jit(solution)/shard_map/ppermute | solution.py:190
  41.4 29.9 %collective-permute-start.3 = (f32[256,1536]{1,0:T(8,128)}, f32[256,1536]{1,0:T(8,128)}, u32[]{:S(2)}, u32[]{:S(2)}) collective-permute-start(f32[256,1536]{1,0:T(8,128)} %collective-permute-done.2.refs_0_), channel_id=1, source_target_pairs={{1,2},{2,1},{5,6},{6,5},{9,10},{10,9},{13,14},{14,13},{17,18},{18,... | collective-permute-start | bytes 4718600 | tf_op jit(solution)/shard_map/ppermute | solution.py:190
  43.2 43.1 %collective-permute-start.1 = (f32[256,1536]{1,0:T(8,128)}, f32[256,1536]{1,0:T(8,128)}, u32[]{:S(2)}, u32[]{:S(2)}) collective-permute-start(f32[256,1536]{1,0:T(8,128)} %collective-permute-done.refs_1_), channel_id=1, source_target_pairs={{1,0},{2,3},{5,4},{6,7},{9,8},{10,11},{13,12},{14,15},{17,16},{18,... | collective-permute-start | bytes 4718600 | tf_op jit(solution)/shard_map/ppermute | solution.py:190
  45.6 9.0 %copy-start.8 = (f32[4,32,1024]{2,1,0:T(8,128)}, f32[4,32,1024]{2,1,0:T(8,128)S(1)}, u32[]{:S(2)}) copy-start(f32[4,32,1024]{2,1,0:T(8,128)S(1)} %bitcast_add_fusion.3) | copy-start | bytes 1572868
  52.5 16.5 %copy-start.4 = (f32[256,512]{1,0:T(8,128)}, f32[256,512]{1,0:T(8,128)S(1)}, u32[]{:S(2)}) copy-start(f32[256,512]{1,0:T(8,128)S(1)} %collective-permute-done.5.refs_1_) | copy-start | bytes 1572868
  52.5 7.9 %collective-permute-start.7 = (f32[2,32,1024]{2,1,0:T(8,128)S(1)}, f32[2,32,1024]{2,1,0:T(8,128)}, u32[]{:S(2)}, u32[]{:S(2)}) collective-permute-start(f32[2,32,1024]{2,1,0:T(8,128)S(1)} %dynamic-slice_bitcast_fusion.5), channel_id=1, source_target_pairs={{0,8},{4,12},{8,0},{12,4},{16,24},{20,28},{24,16},{28,20},{1,9},{5... | collective-permute-start | bytes 786440 | tf_op jit(solution)/shard_map/ppermute | solution.py:162
  54.6 5.8 %copy-start.9 = (f32[4,32,1024]{2,1,0:T(8,128)S(1)}, f32[4,32,1024]{2,1,0:T(8,128)}, u32[]{:S(2)}) copy-start(f32[4,32,1024]{2,1,0:T(8,128)} %copy-done.8) | copy-start | bytes 1572868
  60.4 12.1 %collective-permute-start.9 = (f32[4,32,1024]{2,1,0:T(8,128)}, f32[4,32,1024]{2,1,0:T(8,128)}, u32[]{:S(2)}, u32[]{:S(2)}) collective-permute-start(f32[4,32,1024]{2,1,0:T(8,128)} %dynamic-slice_bitcast_fusion.2), channel_id=1, source_target_pairs={{0,4},{4,0},{8,12},{12,8},{16,20},{20,16},{24,28},{28,24},{1,5},{5... | collective-permute-start | bytes 1572872 | tf_op jit(solution)/shard_map/ppermute | solution.py:162
  61.5 7.6 %collective-permute-start.8 = (f32[1,32,1024]{2,1,0:T(8,128)S(1)}, f32[1,32,1024]{2,1,0:T(8,128)}, u32[]{:S(2)}, u32[]{:S(2)}) collective-permute-start(f32[1,32,1024]{2,1,0:T(8,128)S(1)} %constant_dynamic-slice_fusion.1), channel_id=1, source_target_pairs={{0,16},{4,20},{8,24},{12,28},{16,0},{20,4},{24,8},{28,12},{1,17},{... | collective-permute-start | bytes 393224 | tf_op jit(solution)/shard_map/ppermute | solution.py:162
  64.8 21.6 %collective-permute-start.12 = (f32[256,512]{1,0:T(8,128)S(1)}, f32[256,512]{1,0:T(8,128)S(1)}, u32[]{:S(2)}, u32[]{:S(2)}) collective-permute-start(f32[256,512]{1,0:T(8,128)S(1)} %collective-permute-done.4.refs_1_), channel_id=1, source_target_pairs={{1,2},{2,1},{5,6},{6,5},{9,10},{10,9},{13,14},{14,13},{17,18},{18,... | collective-permute-start | bytes 1572872 | tf_op jit(solution)/shard_map/ppermute | solution.py:190
  69.0 28.4 %collective-permute-start.11 = (f32[256,512]{1,0:T(8,128)S(1)}, f32[256,512]{1,0:T(8,128)S(1)}, u32[]{:S(2)}, u32[]{:S(2)}) collective-permute-start(f32[256,512]{1,0:T(8,128)S(1)} %collective-permute-done.5.refs_1_), channel_id=1, source_target_pairs={{1,0},{2,3},{5,4},{6,7},{9,8},{10,11},{13,12},{14,15},{17,16},{18,... | collective-permute-start | bytes 1572872 | tf_op jit(solution)/shard_map/ppermute | solution.py:190
  71.3 60.0 %collective-permute-start.10 = (f32[256,1536]{1,0:T(8,128)}, f32[256,1536]{1,0:T(8,128)}, u32[]{:S(2)}, u32[]{:S(2)}) collective-permute-start(f32[256,1536]{1,0:T(8,128)} %collective-permute-done.3.refs_1_), channel_id=1, source_target_pairs={{1,0},{2,3},{5,4},{6,7},{9,8},{10,11},{13,12},{14,15},{17,16},{18,... | collective-permute-start | bytes 4718600 | tf_op jit(solution)/shard_map/ppermute | solution.py:190
  97.5 9.9 %collective-permute-start.13 = (f32[2,32,1024]{2,1,0:T(8,128)S(1)}, f32[2,32,1024]{2,1,0:T(8,128)S(1)}, u32[]{:S(2)}, u32[]{:S(2)}) collective-permute-start(f32[2,32,1024]{2,1,0:T(8,128)S(1)} %dynamic-slice_bitcast_fusion.4), channel_id=1, source_target_pairs={{0,8},{4,12},{8,0},{12,4},{16,24},{20,28},{24,16},{28,20},{1,9},{5... | collective-permute-start | bytes 786440 | tf_op jit(solution)/shard_map/ppermute | solution.py:162
  107.3 10.0 %collective-permute-start.15 = (f32[4,32,1024]{2,1,0:T(8,128)}, f32[4,32,1024]{2,1,0:T(8,128)}, u32[]{:S(2)}, u32[]{:S(2)}) collective-permute-start(f32[4,32,1024]{2,1,0:T(8,128)} %dynamic-slice_bitcast_fusion.1), channel_id=1, source_target_pairs={{0,4},{4,0},{8,12},{12,8},{16,20},{20,16},{24,28},{28,24},{1,5},{5... | collective-permute-start | bytes 1572872 | tf_op jit(solution)/shard_map/ppermute | solution.py:162
  108.0 7.7 %collective-permute-start.14 = (f32[1,32,1024]{2,1,0:T(8,128)}, f32[1,32,1024]{2,1,0:T(8,128)}, u32[]{:S(2)}, u32[]{:S(2)}) collective-permute-start(f32[1,32,1024]{2,1,0:T(8,128)} %constant_dynamic-slice_fusion), channel_id=1, source_target_pairs={{0,16},{4,20},{8,24},{12,28},{16,0},{20,4},{24,8},{28,12},{1,17},{... | collective-permute-start | bytes 393224 | tf_op jit(solution)/shard_map/ppermute | solution.py:162
  114.1 28.5 %collective-permute-start.17 = (f32[256,512]{1,0:T(8,128)S(1)}, f32[256,512]{1,0:T(8,128)S(1)}, u32[]{:S(2)}, u32[]{:S(2)}) collective-permute-start(f32[256,512]{1,0:T(8,128)S(1)} %collective-permute-done.12.refs_3_), channel_id=1, source_target_pairs={{1,0},{2,3},{5,4},{6,7},{9,8},{10,11},{13,12},{14,15},{17,16},{18,... | collective-permute-start | bytes 1572872 | tf_op jit(solution)/shard_map/ppermute | solution.py:190
  118.6 16.9 %copy-start.7 = (f32[4,32,1024]{2,1,0:T(8,128)}, f32[4,32,1024]{2,1,0:T(8,128)S(1)}, u32[]{:S(2)}) copy-start(f32[4,32,1024]{2,1,0:T(8,128)S(1)} %bitcast_add_fusion.1) | copy-start | bytes 1572868
  132.0 9.4 %collective-permute-start.18 = (f32[32,1024]{1,0:T(8,128)}, f32[32,1024]{1,0:T(8,128)S(1)}, u32[]{:S(2)}, u32[]{:S(2)}) collective-permute-start(f32[32,1024]{1,0:T(8,128)} %get-tuple-element.66), channel_id=1, source_target_pairs={{0,8},{4,12},{8,0},{12,4},{16,24},{20,28},{24,16},{28,20},{1,9},{5... | collective-permute-start | bytes 393224 | tf_op jit(solution)/shard_map/ppermute | solution.py:185
  134.0 7.4 %collective-permute-start.19 = (f32[32,1024]{1,0:T(8,128)}, f32[32,1024]{1,0:T(8,128)}, u32[]{:S(2)}, u32[]{:S(2)}) collective-permute-start(f32[32,1024]{1,0:T(8,128)} %get-tuple-element.68), channel_id=1, source_target_pairs={{0,16},{4,20},{8,24},{12,28},{16,0},{20,4},{24,8},{28,12},{1,17},{... | collective-permute-start | bytes 393224 | tf_op jit(solution)/shard_map/ppermute | solution.py:185
  135.5 6.0 %collective-permute-start.20 = (f32[32,1024]{1,0:T(8,128)S(1)}, f32[32,1024]{1,0:T(8,128)}, u32[]{:S(2)}, u32[]{:S(2)}) collective-permute-start(f32[32,1024]{1,0:T(8,128)S(1)} %get-tuple-element.67), channel_id=1, source_target_pairs={{0,24},{4,28},{8,16},{12,20},{16,8},{20,12},{24,0},{28,4},{1,25},{... | collective-permute-start | bytes 393224 | tf_op jit(solution)/shard_map/ppermute | solution.py:185
  135.6 7.0 %copy-start.5 = (f32[256,512]{1,0:T(8,128)S(1)}, f32[256,512]{1,0:T(8,128)}, u32[]{:S(2)}) copy-start(f32[256,512]{1,0:T(8,128)} %copy-done.4) | copy-start | bytes 1572868
  143.4 7.6 %copy-start.11 = (f32[32,1024]{1,0:T(8,128)S(1)}, f32[32,1024]{1,0:T(8,128)}, u32[]{:S(2)}) copy-start(f32[32,1024]{1,0:T(8,128)} %add_bitcast_fusion) | copy-start | bytes 393220
  143.5 2.0 %collective-permute-start.22 = (f32[4,32,1024]{2,1,0:T(8,128)S(1)}, f32[4,32,1024]{2,1,0:T(8,128)S(1)}, u32[]{:S(2)}, u32[]{:S(2)}) collective-permute-start(f32[4,32,1024]{2,1,0:T(8,128)S(1)} %dynamic-slice_bitcast_fusion), channel_id=1, source_target_pairs={{0,4},{4,0},{8,12},{12,8},{16,20},{20,16},{24,28},{28,24},{1,5},{5... | collective-permute-start | bytes 1572872 | tf_op jit(solution)/shard_map/ppermute | solution.py:162
  145.6 22.4 %copy-start.10 = (f32[32,4096]{1,0:T(8,128)S(1)}, f32[32,4096]{1,0:T(8,128)}, u32[]{:S(2)}) copy-start(f32[32,4096]{1,0:T(8,128)} %param.7) | copy-start | bytes 1572868
  145.6 9.7 %collective-permute-start.23 = (f32[32,1024]{1,0:T(8,128)S(1)}, f32[32,1024]{1,0:T(8,128)S(1)}, u32[]{:S(2)}, u32[]{:S(2)}) collective-permute-start(f32[32,1024]{1,0:T(8,128)S(1)} %get-tuple-element.63), channel_id=1, source_target_pairs={{0,8},{4,12},{8,0},{12,4},{16,24},{20,28},{24,16},{28,20},{1,9},{5... | collective-permute-start | bytes 393224 | tf_op jit(solution)/shard_map/ppermute | solution.py:185
  149.5 8.1 %collective-permute-start.24 = (f32[32,1024]{1,0:T(8,128)S(1)}, f32[32,1024]{1,0:T(8,128)S(1)}, u32[]{:S(2)}, u32[]{:S(2)}) collective-permute-start(f32[32,1024]{1,0:T(8,128)S(1)} %get-tuple-element.65), channel_id=1, source_target_pairs={{0,16},{4,20},{8,24},{12,28},{16,0},{20,4},{24,8},{28,12},{1,17},{... | collective-permute-start | bytes 393224 | tf_op jit(solution)/shard_map/ppermute | solution.py:185
  151.0 6.6 %collective-permute-start.25 = (f32[32,1024]{1,0:T(8,128)S(1)}, f32[32,1024]{1,0:T(8,128)S(1)}, u32[]{:S(2)}, u32[]{:S(2)}) collective-permute-start(f32[32,1024]{1,0:T(8,128)S(1)} %get-tuple-element.64), channel_id=1, source_target_pairs={{0,24},{4,28},{8,16},{12,20},{16,8},{20,12},{24,0},{28,4},{1,25},{... | collective-permute-start | bytes 393224 | tf_op jit(solution)/shard_map/ppermute | solution.py:185
  151.1 6.9 %collective-permute-start.16 = (f32[32,1024]{1,0:T(8,128)S(1)}, f32[32,1024]{1,0:T(8,128)S(1)}, u32[]{:S(2)}, u32[]{:S(2)}) collective-permute-start(f32[32,1024]{1,0:T(8,128)S(1)} %copy-done.11), channel_id=1, source_target_pairs={{0,1},{1,0},{2,3},{3,2},{4,5},{5,4},{6,7},{7,6},{8,9},{9,8},{10,11... | collective-permute-start | bytes 393224 | tf_op jit(solution)/shard_map/ppermute | solution.py:190
  151.1 10.0 %collective-permute-start.21 = (f32[32,1024]{1,0:T(8,128)S(1)}, f32[32,1024]{1,0:T(8,128)S(1)}, u32[]{:S(2)}, u32[]{:S(2)}) collective-permute-start(f32[32,1024]{1,0:T(8,128)S(1)} %fusion.3), channel_id=1, source_target_pairs={{0,2},{2,0},{1,3},{3,1},{4,6},{6,4},{5,7},{7,5},{8,10},{10,8},{9,1... | collective-permute-start | bytes 393224 | tf_op jit(solution)/shard_map/ppermute | solution.py:190
  161.0 6.9 %collective-permute-start.26 = (f32[32,1024]{1,0:T(8,128)S(1)}, f32[32,1024]{1,0:T(8,128)S(1)}, u32[]{:S(2)}, u32[]{:S(2)}) collective-permute-start(f32[32,1024]{1,0:T(8,128)S(1)} %fusion.1), channel_id=1, source_target_pairs={{0,3},{3,0},{1,2},{2,1},{4,7},{7,4},{5,6},{6,5},{8,11},{11,8},{9,1... | collective-permute-start | bytes 393224 | tf_op jit(solution)/shard_map/ppermute | solution.py:190

commit v6 on v5

--- a/solution.py
+++ b/solution.py
@@ -152,6 +152,33 @@
     return [left[:, :kept], left[:, kept:]]
 
 
+def cut_kernel(left_ref, *refs):
+    *list_refs, sems = refs
+    copies, first = [], 0
+    for i, list_ref in enumerate(list_refs):
+        width = list_ref.shape[1]
+        source = left_ref.at[:, pl.ds(first, width)]
+        copies.append(pltpu.make_async_copy(source, list_ref, sems.at[i]))
+        copies[-1].start()
+        first += width
+    for copy in copies:
+        copy.wait()
+
+
+def cut_argument(left, tiles):
+    rows, columns = left.shape
+    kept = (tiles - tiles // 4) * TILE
+    widths = [kept, columns - kept]
+    return pl.pallas_call(
+        cut_kernel,
+        out_shape=[jax.ShapeDtypeStruct((rows, width), left.dtype) for width in widths],
+        in_specs=[pl.BlockSpec(memory_space=pl.ANY)],
+        out_specs=[pl.BlockSpec(memory_space=pltpu.VMEM)] * 2,
+        scratch_shapes=[pltpu.SemaphoreType.DMA((2,))],
+        compiler_params=pltpu.CompilerParams(vmem_limit_bytes=52 * MIB),
+    )(left)
+
+
 def take(blocks, at, axis):
     return lax.dynamic_index_in_dim(blocks, at, axis, keepdims=False)
 
@@ -213,7 +240,7 @@
     swap_2 = [(0, 2), (2, 0), (1, 3), (3, 1)]
     swap_3 = [(0, 3), (3, 0), (1, 2), (2, 1)]
     swap_inner, to_end = [(1, 2), (2, 1)], [(1, 0), (2, 3)]
-    lists = cut(amplitudes, live.shape[0])
+    lists = cut_argument(amplitudes, live.shape[0])
     kept = lists[0].shape[1] // TILE
 
     one = [send(x, swap_1) for x in lists]

time: 170 us -> 170 us (level)
  Pallas kernels: 21.1 us -> 31.6 us
  starting transfers between devices: 43.5 us -> 37.7 us
  local copies, waits for them, and re-layouts: 18.9 us -> 14.5 us
    pallas_call x4, Pallas kernels: 17.5 us -> 22.9 us  [product(): pl.pallas_call(functools.partial(product_kernel, [len(candidates) for can...]
    ppermute x8, starting transfers between devices: 11.8 us -> 6.61 us  [halve(): lax.ppermute(take(blocks, 1 - mine, axis), 'cd', pairs)]
    slice x2 -> x0, local copies, waits for them, and re-layouts: 3.65 us -> none  [cut(): return [left[:, :kept], left[:, kept:]]]
    pallas_call x0 -> x1, Pallas kernels: none -> 2.99 us  [cut_argument(): pl.pallas_call(cut_kernel, out_shape=[jax.ShapeDtypeStruct((rows, width),...]
    pallas_call x1, Pallas kernels: 3.66 us -> 5.75 us  [first_product(): pl.pallas_call(first_kernel, out_shape=(jax.ShapeDtypeStruct((rows, colum...]
    ppermute x6, starting transfers between devices: 8.98 us -> 7.07 us  [chip_sum_direct(): total += lax.ppermute(take(blocks, chip ^ flip, 0), 'cd', pairs)]
  transfers between devices with their start and end apart: 27 -> 27, of which waited for: 13 -> 11; matrix products, arithmetic and copies ran while one was open for 10% -> 8% of each run, Pallas kernels for 12% -> 16%
where the time goes in v6:
time: 170 us; the launch traced here: 169 us
  waiting for transfers between devices  76.8 us (45%)
  starting transfers between devices  37.7 us (22%)
  Pallas kernels  31.6 us (19%)
  local copies, waits for them, and re-layouts  14.5 us (9%)
  other arithmetic  8.25 us (5%)
    ppermute x13, waiting for transfers between devices, send(): return lax.ppermute(x, 'ab', pairs)  67.8 us
    ppermute x13, starting transfers between devices, send(): return lax.ppermute(x, 'ab', pairs)  24 us
    pallas_call x4, Pallas kernels, product(): pl.pallas_call(functools.partial(product_kernel, [len(candidates) for can...  22.9 us
    unnamed x24, local copies, waits for them, and re-layouts  7.41 us
    ppermute x8, waiting for transfers between devices, halve(): lax.ppermute(take(blocks, 1 - mine, axis), 'cd', pairs)  7.07 us
    ppermute x6, starting transfers between devices, chip_sum_direct(): total += lax.ppermute(take(blocks, chip ^ flip, 0), 'cd', pairs)  7.07 us
    ppermute x8, starting transfers between devices, halve(): lax.ppermute(take(blocks, 1 - mine, axis), 'cd', pairs)  6.61 us
    pallas_call x1, Pallas kernels, first_product(): pl.pallas_call(first_kernel, out_shape=(jax.ShapeDtypeStruct((rows, colum...  5.75 us
  transfers between devices with their start and end apart: 27, of which 11 were waited for; matrix products, arithmetic and copies ran while one was open for 8% of the time, Pallas kernels for 16%

profile of v6, /device:TPU:0, one launch (start us, length us, event | category | flops | bytes accessed | tf_op | source)
XLA Modules:
  0.0 169.2 jit_solution(13338821593301450282)
XLA Ops:
  0.0 3.0 %shard_map.46 = (f32[256,1536]{1,0:T(8,128)}, f32[256,512]{1,0:T(8,128)}) custom-call(f32[256,2048]{1,0:T(8,128)} %left_ref.3), custom_call_target="tpu_custom_call" | custom-call | tf_op jit(solution)/shard_map/pallas_call | solution.py:172
  3.0 3.1 %collective-permute-start.2 = (f32[256,1536]{1,0:T(8,128)}, f32[256,1536]{1,0:T(8,128)}, u32[]{:S(2)}, u32[]{:S(2)}) collective-permute-start(f32[256,1536]{1,0:T(8,128)} %get-tuple-element.34), channel_id=1, source_target_pairs={{0,1},{1,0},{2,3},{3,2},{4,5},{5,4},{6,7},{7,6},{8,9},{9,8},{10,11... | collective-permute-start | bytes 4718600 | tf_op jit(solution)/shard_map/ppermute | solution.py:217
  6.1 1.8 %collective-permute-start = (f32[256,1536]{1,0:T(8,128)}, f32[256,1536]{1,0:T(8,128)}, u32[]{:S(2)}, u32[]{:S(2)}) collective-permute-start(f32[256,1536]{1,0:T(8,128)} %get-tuple-element.34), channel_id=1, source_target_pairs={{1,2},{2,1},{5,6},{6,5},{9,10},{10,9},{13,14},{14,13},{17,18},{18,... | collective-permute-start | bytes 4718600 | tf_op jit(solution)/shard_map/ppermute | solution.py:217
  7.9 3.4 %copy-done.2 = f32[2048,1024]{1,0:T(8,128)S(1)} copy-done((f32[2048,1024]{1,0:T(8,128)S(1)}, f32[2048,1024]{1,0:T(8,128)}, u32[]{:S(2)}) %copy-start.2) | copy-done | bytes 8388632
  11.3 5.8 %shard_map.47 = (f32[256,1024]{1,0:T(8,128)S(1)}, bf16[8,256,1024]{2,1,0:T(8,128)(2,1)S(1)}, bf16[8,256,1024]{2,1,0:T(8,128)(2,1)S(1)}) custom-call(s32[8]{0:T(128)S(1)} %copy-done.6, f32[256,2048]{1,0:T(8,128)S(1)} %copy-done.3, f32[8,256,1024]{2,1,0:T(8,128)S(1)} %bitcast.73), custom_call_target="tpu_custom_call" | custom-call | flops 1073741824 | bytes 3145728 | tf_op jit(solution)/shard_map/pallas_call | solution.py:50
  17.1 2.0 %copy-done = bf16[8,256,1024]{2,1,0:T(8,128)(2,1)} copy-done((bf16[8,256,1024]{2,1,0:T(8,128)(2,1)}, bf16[8,256,1024]{2,1,0:T(8,128)(2,1)S(1)}, u32[]{:S(2)}) %copy-start) | copy-done | bytes 4194328
  19.0 2.0 %copy-done.1 = bf16[8,256,1024]{2,1,0:T(8,128)(2,1)} copy-done((bf16[8,256,1024]{2,1,0:T(8,128)(2,1)}, bf16[8,256,1024]{2,1,0:T(8,128)(2,1)S(1)}, u32[]{:S(2)}) %copy-start.1) | copy-done | bytes 4194328
  21.2 3.3 %collective-permute-start.4 = (f32[256,512]{1,0:T(8,128)}, f32[256,512]{1,0:T(8,128)S(1)}, u32[]{:S(2)}, u32[]{:S(2)}) collective-permute-start(f32[256,512]{1,0:T(8,128)} %get-tuple-element.35), channel_id=1, source_target_pairs={{0,1},{1,0},{2,3},{3,2},{4,5},{5,4},{6,7},{7,6},{8,9},{9,8},{10,11... | collective-permute-start | bytes 1572872 | tf_op jit(solution)/shard_map/ppermute | solution.py:217
  25.2 16.4 %collective-permute-done.2.refs_0_ = f32[256,1536]{1,0:T(8,128)} collective-permute-done((f32[256,1536]{1,0:T(8,128)}, f32[256,1536]{1,0:T(8,128)}, u32[]{:S(2)}, u32[]{:S(2)}) %collective-permute-start.2) | collective-permute-done | bytes 1572896 | tf_op jit(solution)/shard_map/ppermute | solution.py:217
  41.6 1.8 %collective-permute-start.3 = (f32[256,1536]{1,0:T(8,128)}, f32[256,1536]{1,0:T(8,128)}, u32[]{:S(2)}, u32[]{:S(2)}) collective-permute-start(f32[256,1536]{1,0:T(8,128)} %collective-permute-done.2.refs_0_), channel_id=1, source_target_pairs={{1,2},{2,1},{5,6},{6,5},{9,10},{10,9},{13,14},{14,13},{17,18},{18,... | collective-permute-start | bytes 4718600 | tf_op jit(solution)/shard_map/ppermute | solution.py:217
  43.5 1.3 collective-permute-start.1
  44.8 7.9 %collective-permute-done.4.refs_1_ = f32[256,512]{1,0:T(8,128)S(1)} collective-permute-done((f32[256,512]{1,0:T(8,128)}, f32[256,512]{1,0:T(8,128)S(1)}, u32[]{:S(2)}, u32[]{:S(2)}) %collective-permute-start.4) | collective-permute-done | bytes 524320 | tf_op jit(solution)/shard_map/ppermute | solution.py:217
  52.8 2.0 %collective-permute-start.7 = (f32[2,32,1024]{2,1,0:T(8,128)S(1)}, f32[2,32,1024]{2,1,0:T(8,128)}, u32[]{:S(2)}, u32[]{:S(2)}) collective-permute-start(f32[2,32,1024]{2,1,0:T(8,128)S(1)} %dynamic-slice_bitcast_fusion.5), channel_id=1, source_target_pairs={{0,8},{4,12},{8,0},{12,4},{16,24},{20,28},{24,16},{28,20},{1,9},{5... | collective-permute-start | bytes 786440 | tf_op jit(solution)/shard_map/ppermute | solution.py:189
  54.9 6.6 %shard_map.48 = f32[256,1024]{1,0:T(8,128)S(1)} custom-call(s32[9]{0:T(128)S(1)} %get-tuple-element.74.scalars, f32[256,1536]{1,0:T(8,128)} %collective-permute-done.2.refs_0_, f32[256,512]{1,0:T(8,128)S(1)} %collective-permute-done.4.refs_1_, bf16[8,256,1024]{2,1,0:T(8,128)(2,1)} %copy-done, bf16[8,256,1024]{2,1,0:T(8,128)(2,1)} %copy-done.1), custom_call_target="tpu_custom_call" | custom-call | flops 1073741824 | bytes 3145728 | tf_op jit(solution)/shard_map/pallas_call | solution.py:127
  61.5 0.9 dynamic-slice_bitcast_fusion.2
  62.4 1.0 bitcast_add_fusion.5
  63.4 1.2 collective-permute-start.8
  65.4 4.2 %collective-permute-done.8 = f32[1,32,1024]{2,1,0:T(8,128)} collective-permute-done((f32[1,32,1024]{2,1,0:T(8,128)S(1)}, f32[1,32,1024]{2,1,0:T(8,128)}, u32[]{:S(2)}, u32[]{:S(2)}) %collective-permute-start.8) | collective-permute-done | bytes 131104 | tf_op jit(solution)/shard_map/ppermute | solution.py:189
  69.5 1.3 collective-permute-start.11
  70.8 0.9 add_bitcast_fusion.1
  71.7 1.3 collective-permute-start.10
  73.1 1.1 bitcast_add_fusion.2
  74.2 12.4 %collective-permute-done.1.refs_0_ = f32[256,1536]{1,0:T(8,128)} collective-permute-done((f32[256,1536]{1,0:T(8,128)}, f32[256,1536]{1,0:T(8,128)}, u32[]{:S(2)}, u32[]{:S(2)}) %collective-permute-start.1) | collective-permute-done | bytes 1572896 | tf_op jit(solution)/shard_map/ppermute | solution.py:217
  86.6 11.1 %collective-permute-done.11.refs_2_ = f32[256,512]{1,0:T(8,128)S(1)} collective-permute-done((f32[256,512]{1,0:T(8,128)S(1)}, f32[256,512]{1,0:T(8,128)S(1)}, u32[]{:S(2)}, u32[]{:S(2)}) %collective-permute-start.11) | collective-permute-done | bytes 524320 | tf_op jit(solution)/shard_map/ppermute | solution.py:217
  97.7 2.0 %collective-permute-start.13 = (f32[2,32,1024]{2,1,0:T(8,128)S(1)}, f32[2,32,1024]{2,1,0:T(8,128)S(1)}, u32[]{:S(2)}, u32[]{:S(2)}) collective-permute-start(f32[2,32,1024]{2,1,0:T(8,128)S(1)} %dynamic-slice_bitcast_fusion.4), channel_id=1, source_target_pairs={{0,8},{4,12},{8,0},{12,4},{16,24},{20,28},{24,16},{28,20},{1,9},{5... | collective-permute-start | bytes 786440 | tf_op jit(solution)/shard_map/ppermute | solution.py:189
  99.8 7.7 %shard_map.49 = f32[256,1024]{1,0:T(8,128)} custom-call(s32[9]{0:T(128)S(1)} %get-tuple-element.73.scalars, f32[256,1536]{1,0:T(8,128)} %collective-permute-done.1.refs_0_, f32[256,1536]{1,0:T(8,128)} %collective-permute-done.3.refs_1_, f32[256,512]{1,0:T(8,128)S(1)} %collective-permute-done.11.refs_2_, f32[256,512]{1,0:T(8,128)S(1)} %collective-permute-done.12.refs_3_, ...), custom_call_target="tpu_custom_call" | custom-call | flops 1073741824 | bytes 3145728 | tf_op jit(solution)/shard_map/pallas_call | solution.py:127
  107.4 1.9 %dynamic-slice_bitcast_fusion.1 = f32[4,32,1024]{2,1,0:T(8,128)} fusion(f32[4,2,32,1024]{3,2,1,0:T(8,128)} %bitcast.81, s32[]{:T(128)S(6)} %select_n.67), kind=kLoop, calls=%fused_computation.7 | loop fusion | bytes 1048580 | tf_op jit(solution)/shard_map/jit(dynamic_index_in_dim)/squeeze | solution.py:183
  110.0 1.2 collective-permute-start.14
  111.2 1.3 slice.12.refs_2_
  112.5 1.3 slice.13.refs_3_
  114.0 1.3 collective-permute-start.17
  115.3 1.0 collective-permute-done.14
  116.3 1.6 add_bitcast_fusion
  117.9 1.3 bitcast_add_fusion.1
  119.1 12.4 %collective-permute-done.10.refs_0_ = f32[256,1536]{1,0:T(8,128)} collective-permute-done((f32[256,1536]{1,0:T(8,128)}, f32[256,1536]{1,0:T(8,128)}, u32[]{:S(2)}, u32[]{:S(2)}) %collective-permute-start.10) | collective-permute-done | bytes 1572896 | tf_op jit(solution)/shard_map/ppermute | solution.py:217
  132.2 2.0 %collective-permute-start.18 = (f32[32,1024]{1,0:T(8,128)}, f32[32,1024]{1,0:T(8,128)S(1)}, u32[]{:S(2)}, u32[]{:S(2)}) collective-permute-start(f32[32,1024]{1,0:T(8,128)} %get-tuple-element.70), channel_id=1, source_target_pairs={{0,8},{4,12},{8,0},{12,4},{16,24},{20,28},{24,16},{28,20},{1,9},{5... | collective-permute-start | bytes 393224 | tf_op jit(solution)/shard_map/ppermute | solution.py:212
  134.2 1.5 collective-permute-start.19
  135.8 6.8 %shard_map.50.refs_4_ = f32[256,1024]{1,0:T(8,128)S(1)} custom-call(s32[7]{0:T(128)S(1)} %pad_add_fusion.2.scalars, f32[256,1536]{1,0:T(8,128)} %collective-permute-done.10.refs_0_, f32[256,1536]{1,0:T(8,128)} %collective-permute-done.refs_1_, bf16[8,256,1024]{2,1,0:T(8,128)(2,1)} %copy-done, bf16[8,256,1024]{2,1,0:T(8,128)(2,1)} %copy-done.1), custom_call_target="tpu_custom_call" | custom-call | flops 805306368 | bytes 2621440 | tf_op jit(solution)/shard_map/pallas_call | solution.py:127
  142.6 1.1 fusion.3
  143.7 1.8 %shard_map.51 = f32[256,1024]{1,0:T(8,128)S(1)} custom-call(s32[3]{0:T(128)S(1)} %pad_add_fusion.3.scalars, f32[256,512]{1,0:T(8,128)S(1)} %collective-permute-done.17.refs_0_, f32[256,512]{1,0:T(8,128)S(1)} %copy-done.5, bf16[2,256,1024]{2,1,0:T(8,128)(2,1)S(1)} %slice.12.refs_2_, bf16[2,256,1024]{2,1,0:T(8,128)(2,1)S(1)} %slice.13.refs_3_, ...), custom_call_target="tpu_custom_call" | custom-call | flops 268435456 | bytes 1572864 | tf_op jit(solution)/shard_map/pallas_call | solution.py:127
  145.7 1.9 %collective-permute-done.22 = f32[4,32,1024]{2,1,0:T(8,128)S(1)} collective-permute-done((f32[4,32,1024]{2,1,0:T(8,128)S(1)}, f32[4,32,1024]{2,1,0:T(8,128)S(1)}, u32[]{:S(2)}, u32[]{:S(2)}) %collective-permute-start.22) | collective-permute-done | bytes 524320 | tf_op jit(solution)/shard_map/ppermute | solution.py:189
  147.7 2.0 %collective-permute-start.23 = (f32[32,1024]{1,0:T(8,128)S(1)}, f32[32,1024]{1,0:T(8,128)S(1)}, u32[]{:S(2)}, u32[]{:S(2)}) collective-permute-start(f32[32,1024]{1,0:T(8,128)S(1)} %get-tuple-element.67), channel_id=1, source_target_pairs={{0,8},{4,12},{8,0},{12,4},{16,24},{20,28},{24,16},{28,20},{1,9},{5... | collective-permute-start | bytes 393224 | tf_op jit(solution)/shard_map/ppermute | solution.py:212
  149.8 1.5 collective-permute-start.25
  151.3 4.6 %collective-permute-start.21 = (f32[32,1024]{1,0:T(8,128)S(1)}, f32[32,1024]{1,0:T(8,128)S(1)}, u32[]{:S(2)}, u32[]{:S(2)}) collective-permute-start(f32[32,1024]{1,0:T(8,128)S(1)} %fusion.3), channel_id=1, source_target_pairs={{0,2},{2,0},{1,3},{3,1},{4,6},{6,4},{5,7},{7,5},{8,10},{10,8},{9,1... | collective-permute-start | bytes 393224 | tf_op jit(solution)/shard_map/ppermute | solution.py:217
  155.9 1.9 %collective-permute-done.24 = f32[32,1024]{1,0:T(8,128)S(1)} collective-permute-done((f32[32,1024]{1,0:T(8,128)S(1)}, f32[32,1024]{1,0:T(8,128)S(1)}, u32[]{:S(2)}, u32[]{:S(2)}) %collective-permute-start.24) | collective-permute-done | bytes 131104 | tf_op jit(solution)/shard_map/ppermute | solution.py:212
  157.9 3.6 %collective-permute-done.21 = f32[32,1024]{1,0:T(8,128)S(1)} collective-permute-done((f32[32,1024]{1,0:T(8,128)S(1)}, f32[32,1024]{1,0:T(8,128)S(1)}, u32[]{:S(2)}, u32[]{:S(2)}) %collective-permute-start.21) | collective-permute-done | bytes 131104 | tf_op jit(solution)/shard_map/ppermute | solution.py:217
  161.5 2.8 %collective-permute-start.26 = (f32[32,1024]{1,0:T(8,128)S(1)}, f32[32,1024]{1,0:T(8,128)S(1)}, u32[]{:S(2)}, u32[]{:S(2)}) collective-permute-start(f32[32,1024]{1,0:T(8,128)S(1)} %fusion.1), channel_id=1, source_target_pairs={{0,3},{3,0},{1,2},{2,1},{4,7},{7,4},{5,6},{6,5},{8,11},{11,8},{9,1... | collective-permute-start | bytes 393224 | tf_op jit(solution)/shard_map/ppermute | solution.py:217
  164.3 3.9 %collective-permute-done.26 = f32[32,1024]{1,0:T(8,128)S(1)} collective-permute-done((f32[32,1024]{1,0:T(8,128)S(1)}, f32[32,1024]{1,0:T(8,128)S(1)}, u32[]{:S(2)}, u32[]{:S(2)}) %collective-permute-start.26) | collective-permute-done | bytes 131104 | tf_op jit(solution)/shard_map/ppermute | solution.py:217
  (65 shorter events, 4.6 us)
Async XLA Ops:
  0.0 7.9 %copy-start.3 = (f32[256,2048]{1,0:T(8,128)S(1)}, f32[256,2048]{1,0:T(8,128)}, u32[]{:S(2)}) copy-start(f32[256,2048]{1,0:T(8,128)} %left_ref.3) | copy-start | bytes 6291460
  0.0 7.9 %copy-start.6 = (s32[8]{0:T(128)S(1)}, s32[8]{0:T(128)}, u32[]{:S(2)}) copy-start(s32[8]{0:T(128)} %live.1) | copy-start | bytes 100
  3.0 38.6 %collective-permute-start.2 = (f32[256,1536]{1,0:T(8,128)}, f32[256,1536]{1,0:T(8,128)}, u32[]{:S(2)}, u32[]{:S(2)}) collective-permute-start(f32[256,1536]{1,0:T(8,128)} %get-tuple-element.34), channel_id=1, source_target_pairs={{0,1},{1,0},{2,3},{3,2},{4,5},{5,4},{6,7},{7,6},{8,9},{9,8},{10,11... | collective-permute-start | bytes 4718600 | tf_op jit(solution)/shard_map/ppermute | solution.py:217
  6.1 37.4 %collective-permute-start = (f32[256,1536]{1,0:T(8,128)}, f32[256,1536]{1,0:T(8,128)}, u32[]{:S(2)}, u32[]{:S(2)}) collective-permute-start(f32[256,1536]{1,0:T(8,128)} %get-tuple-element.34), channel_id=1, source_target_pairs={{1,2},{2,1},{5,6},{6,5},{9,10},{10,9},{13,14},{14,13},{17,18},{18,... | collective-permute-start | bytes 4718600 | tf_op jit(solution)/shard_map/ppermute | solution.py:217
  7.9 3.4 %copy-start.2 = (f32[2048,1024]{1,0:T(8,128)S(1)}, f32[2048,1024]{1,0:T(8,128)}, u32[]{:S(2)}) copy-start(f32[2048,1024]{1,0:T(8,128)} %param.5) | copy-start | bytes 25165828
  17.1 2.0 %copy-start = (bf16[8,256,1024]{2,1,0:T(8,128)(2,1)}, bf16[8,256,1024]{2,1,0:T(8,128)(2,1)S(1)}, u32[]{:S(2)}) copy-start(bf16[8,256,1024]{2,1,0:T(8,128)(2,1)S(1)} %get-tuple-element.41.refs_2_.refs_4_) | copy-start | bytes 12582916
  19.0 2.0 %copy-start.1 = (bf16[8,256,1024]{2,1,0:T(8,128)(2,1)}, bf16[8,256,1024]{2,1,0:T(8,128)(2,1)S(1)}, u32[]{:S(2)}) copy-start(bf16[8,256,1024]{2,1,0:T(8,128)(2,1)S(1)} %get-tuple-element.42.refs_3_.refs_5_) | copy-start | bytes 12582916
  21.1 23.6 %collective-permute-start.6 = (f32[4,32,1024]{2,1,0:T(8,128)S(1)}, f32[4,32,1024]{2,1,0:T(8,128)S(1)}, u32[]{:S(2)}, u32[]{:S(2)}) collective-permute-start(f32[4,32,1024]{2,1,0:T(8,128)S(1)} %dynamic-slice_bitcast_fusion.3), channel_id=1, source_target_pairs={{0,4},{4,0},{8,12},{12,8},{16,20},{20,16},{24,28},{28,24},{1,5},{5... | collective-permute-start | bytes 1572872 | tf_op jit(solution)/shard_map/ppermute | solution.py:189
  21.2 31.6 %collective-permute-start.4 = (f32[256,512]{1,0:T(8,128)}, f32[256,512]{1,0:T(8,128)S(1)}, u32[]{:S(2)}, u32[]{:S(2)}) collective-permute-start(f32[256,512]{1,0:T(8,128)} %get-tuple-element.35), channel_id=1, source_target_pairs={{0,1},{1,0},{2,3},{3,2},{4,5},{5,4},{6,7},{7,6},{8,9},{9,8},{10,11... | collective-permute-start | bytes 1572872 | tf_op jit(solution)/shard_map/ppermute | solution.py:217
  24.5 28.2 %collective-permute-start.5 = (f32[256,512]{1,0:T(8,128)}, f32[256,512]{1,0:T(8,128)S(1)}, u32[]{:S(2)}, u32[]{:S(2)}) collective-permute-start(f32[256,512]{1,0:T(8,128)} %get-tuple-element.35), channel_id=1, source_target_pairs={{1,2},{2,1},{5,6},{6,5},{9,10},{10,9},{13,14},{14,13},{17,18},{18,... | collective-permute-start | bytes 1572872 | tf_op jit(solution)/shard_map/ppermute | solution.py:217
  41.6 30.1 %collective-permute-start.3 = (f32[256,1536]{1,0:T(8,128)}, f32[256,1536]{1,0:T(8,128)}, u32[]{:S(2)}, u32[]{:S(2)}) collective-permute-start(f32[256,1536]{1,0:T(8,128)} %collective-permute-done.2.refs_0_), channel_id=1, source_target_pairs={{1,2},{2,1},{5,6},{6,5},{9,10},{10,9},{13,14},{14,13},{17,18},{18,... | collective-permute-start | bytes 4718600 | tf_op jit(solution)/shard_map/ppermute | solution.py:217
  43.5 43.1 %collective-permute-start.1 = (f32[256,1536]{1,0:T(8,128)}, f32[256,1536]{1,0:T(8,128)}, u32[]{:S(2)}, u32[]{:S(2)}) collective-permute-start(f32[256,1536]{1,0:T(8,128)} %collective-permute-done.refs_1_), channel_id=1, source_target_pairs={{1,0},{2,3},{5,4},{6,7},{9,8},{10,11},{13,12},{14,15},{17,16},{18,... | collective-permute-start | bytes 4718600 | tf_op jit(solution)/shard_map/ppermute | solution.py:217
  44.8 10.0 %copy-start.8 = (f32[4,32,1024]{2,1,0:T(8,128)}, f32[4,32,1024]{2,1,0:T(8,128)S(1)}, u32[]{:S(2)}) copy-start(f32[4,32,1024]{2,1,0:T(8,128)S(1)} %bitcast_add_fusion.3) | copy-start | bytes 1572868
  52.8 16.8 %copy-start.4 = (f32[256,512]{1,0:T(8,128)}, f32[256,512]{1,0:T(8,128)S(1)}, u32[]{:S(2)}) copy-start(f32[256,512]{1,0:T(8,128)S(1)} %collective-permute-done.5.refs_1_) | copy-start | bytes 1572868
  52.8 9.6 %collective-permute-start.7 = (f32[2,32,1024]{2,1,0:T(8,128)S(1)}, f32[2,32,1024]{2,1,0:T(8,128)}, u32[]{:S(2)}, u32[]{:S(2)}) collective-permute-start(f32[2,32,1024]{2,1,0:T(8,128)S(1)} %dynamic-slice_bitcast_fusion.5), channel_id=1, source_target_pairs={{0,8},{4,12},{8,0},{12,4},{16,24},{20,28},{24,16},{28,20},{1,9},{5... | collective-permute-start | bytes 786440 | tf_op jit(solution)/shard_map/ppermute | solution.py:189
  54.9 7.5 %copy-start.9 = (f32[4,32,1024]{2,1,0:T(8,128)S(1)}, f32[4,32,1024]{2,1,0:T(8,128)}, u32[]{:S(2)}) copy-start(f32[4,32,1024]{2,1,0:T(8,128)} %copy-done.8) | copy-start | bytes 1572868
  62.4 10.6 %collective-permute-start.9 = (f32[4,32,1024]{2,1,0:T(8,128)}, f32[4,32,1024]{2,1,0:T(8,128)}, u32[]{:S(2)}, u32[]{:S(2)}) collective-permute-start(f32[4,32,1024]{2,1,0:T(8,128)} %dynamic-slice_bitcast_fusion.2), channel_id=1, source_target_pairs={{0,4},{4,0},{8,12},{12,8},{16,20},{20,16},{24,28},{28,24},{1,5},{5... | collective-permute-start | bytes 1572872 | tf_op jit(solution)/shard_map/ppermute | solution.py:189
  63.4 6.1 %collective-permute-start.8 = (f32[1,32,1024]{2,1,0:T(8,128)S(1)}, f32[1,32,1024]{2,1,0:T(8,128)}, u32[]{:S(2)}, u32[]{:S(2)}) collective-permute-start(f32[1,32,1024]{2,1,0:T(8,128)S(1)} %constant_dynamic-slice_fusion.1), channel_id=1, source_target_pairs={{0,16},{4,20},{8,24},{12,28},{16,0},{20,4},{24,8},{28,12},{1,17},{... | collective-permute-start | bytes 393224 | tf_op jit(solution)/shard_map/ppermute | solution.py:189
  64.7 21.9 %collective-permute-start.12 = (f32[256,512]{1,0:T(8,128)S(1)}, f32[256,512]{1,0:T(8,128)S(1)}, u32[]{:S(2)}, u32[]{:S(2)}) collective-permute-start(f32[256,512]{1,0:T(8,128)S(1)} %collective-permute-done.4.refs_1_), channel_id=1, source_target_pairs={{1,2},{2,1},{5,6},{6,5},{9,10},{10,9},{13,14},{14,13},{17,18},{18,... | collective-permute-start | bytes 1572872 | tf_op jit(solution)/shard_map/ppermute | solution.py:217
  69.5 28.2 %collective-permute-start.11 = (f32[256,512]{1,0:T(8,128)S(1)}, f32[256,512]{1,0:T(8,128)S(1)}, u32[]{:S(2)}, u32[]{:S(2)}) collective-permute-start(f32[256,512]{1,0:T(8,128)S(1)} %collective-permute-done.5.refs_1_), channel_id=1, source_target_pairs={{1,0},{2,3},{5,4},{6,7},{9,8},{10,11},{13,12},{14,15},{17,16},{18,... | collective-permute-start | bytes 1572872 | tf_op jit(solution)/shard_map/ppermute | solution.py:217
  71.7 59.8 %collective-permute-start.10 = (f32[256,1536]{1,0:T(8,128)}, f32[256,1536]{1,0:T(8,128)}, u32[]{:S(2)}, u32[]{:S(2)}) collective-permute-start(f32[256,1536]{1,0:T(8,128)} %collective-permute-done.3.refs_1_), channel_id=1, source_target_pairs={{1,0},{2,3},{5,4},{6,7},{9,8},{10,11},{13,12},{14,15},{17,16},{18,... | collective-permute-start | bytes 4718600 | tf_op jit(solution)/shard_map/ppermute | solution.py:217
  97.7 11.6 %collective-permute-start.13 = (f32[2,32,1024]{2,1,0:T(8,128)S(1)}, f32[2,32,1024]{2,1,0:T(8,128)S(1)}, u32[]{:S(2)}, u32[]{:S(2)}) collective-permute-start(f32[2,32,1024]{2,1,0:T(8,128)S(1)} %dynamic-slice_bitcast_fusion.4), channel_id=1, source_target_pairs={{0,8},{4,12},{8,0},{12,4},{16,24},{20,28},{24,16},{28,20},{1,9},{5... | collective-permute-start | bytes 786440 | tf_op jit(solution)/shard_map/ppermute | solution.py:189
  109.3 8.5 %collective-permute-start.15 = (f32[4,32,1024]{2,1,0:T(8,128)}, f32[4,32,1024]{2,1,0:T(8,128)}, u32[]{:S(2)}, u32[]{:S(2)}) collective-permute-start(f32[4,32,1024]{2,1,0:T(8,128)} %dynamic-slice_bitcast_fusion.1), channel_id=1, source_target_pairs={{0,4},{4,0},{8,12},{12,8},{16,20},{20,16},{24,28},{28,24},{1,5},{5... | collective-permute-start | bytes 1572872 | tf_op jit(solution)/shard_map/ppermute | solution.py:189
  110.0 6.2 %collective-permute-start.14 = (f32[1,32,1024]{2,1,0:T(8,128)}, f32[1,32,1024]{2,1,0:T(8,128)}, u32[]{:S(2)}, u32[]{:S(2)}) collective-permute-start(f32[1,32,1024]{2,1,0:T(8,128)} %constant_dynamic-slice_fusion), channel_id=1, source_target_pairs={{0,16},{4,20},{8,24},{12,28},{16,0},{20,4},{24,8},{28,12},{1,17},{... | collective-permute-start | bytes 393224 | tf_op jit(solution)/shard_map/ppermute | solution.py:189
  114.0 29.7 %collective-permute-start.17 = (f32[256,512]{1,0:T(8,128)S(1)}, f32[256,512]{1,0:T(8,128)S(1)}, u32[]{:S(2)}, u32[]{:S(2)}) collective-permute-start(f32[256,512]{1,0:T(8,128)S(1)} %collective-permute-done.12.refs_3_), channel_id=1, source_target_pairs={{1,0},{2,3},{5,4},{6,7},{9,8},{10,11},{13,12},{14,15},{17,16},{18,... | collective-permute-start | bytes 1572872 | tf_op jit(solution)/shard_map/ppermute | solution.py:217
  119.1 16.6 %copy-start.7 = (f32[4,32,1024]{2,1,0:T(8,128)}, f32[4,32,1024]{2,1,0:T(8,128)S(1)}, u32[]{:S(2)}) copy-start(f32[4,32,1024]{2,1,0:T(8,128)S(1)} %bitcast_add_fusion.1) | copy-start | bytes 1572868
  132.2 10.4 %collective-permute-start.18 = (f32[32,1024]{1,0:T(8,128)}, f32[32,1024]{1,0:T(8,128)S(1)}, u32[]{:S(2)}, u32[]{:S(2)}) collective-permute-start(f32[32,1024]{1,0:T(8,128)} %get-tuple-element.70), channel_id=1, source_target_pairs={{0,8},{4,12},{8,0},{12,4},{16,24},{20,28},{24,16},{28,20},{1,9},{5... | collective-permute-start | bytes 393224 | tf_op jit(solution)/shard_map/ppermute | solution.py:212
  134.2 8.4 %collective-permute-start.19 = (f32[32,1024]{1,0:T(8,128)}, f32[32,1024]{1,0:T(8,128)}, u32[]{:S(2)}, u32[]{:S(2)}) collective-permute-start(f32[32,1024]{1,0:T(8,128)} %get-tuple-element.72), channel_id=1, source_target_pairs={{0,16},{4,20},{8,24},{12,28},{16,0},{20,4},{24,8},{28,12},{1,17},{... | collective-permute-start | bytes 393224 | tf_op jit(solution)/shard_map/ppermute | solution.py:212
  135.7 6.9 %collective-permute-start.20 = (f32[32,1024]{1,0:T(8,128)S(1)}, f32[32,1024]{1,0:T(8,128)}, u32[]{:S(2)}, u32[]{:S(2)}) collective-permute-start(f32[32,1024]{1,0:T(8,128)S(1)} %get-tuple-element.71), channel_id=1, source_target_pairs={{0,24},{4,28},{8,16},{12,20},{16,8},{20,12},{24,0},{28,4},{1,25},{... | collective-permute-start | bytes 393224 | tf_op jit(solution)/shard_map/ppermute | solution.py:212
  135.8 7.9 %copy-start.5 = (f32[256,512]{1,0:T(8,128)S(1)}, f32[256,512]{1,0:T(8,128)}, u32[]{:S(2)}) copy-start(f32[256,512]{1,0:T(8,128)} %copy-done.4) | copy-start | bytes 1572868
  145.6 5.7 %copy-start.11 = (f32[32,1024]{1,0:T(8,128)S(1)}, f32[32,1024]{1,0:T(8,128)}, u32[]{:S(2)}) copy-start(f32[32,1024]{1,0:T(8,128)} %add_bitcast_fusion) | copy-start | bytes 393220
  145.6 2.0 %collective-permute-start.22 = (f32[4,32,1024]{2,1,0:T(8,128)S(1)}, f32[4,32,1024]{2,1,0:T(8,128)S(1)}, u32[]{:S(2)}, u32[]{:S(2)}) collective-permute-start(f32[4,32,1024]{2,1,0:T(8,128)S(1)} %dynamic-slice_bitcast_fusion), channel_id=1, source_target_pairs={{0,4},{4,0},{8,12},{12,8},{16,20},{20,16},{24,28},{28,24},{1,5},{5... | collective-permute-start | bytes 1572872 | tf_op jit(solution)/shard_map/ppermute | solution.py:189
  147.7 20.6 %copy-start.10 = (f32[32,4096]{1,0:T(8,128)S(1)}, f32[32,4096]{1,0:T(8,128)}, u32[]{:S(2)}) copy-start(f32[32,4096]{1,0:T(8,128)} %param.7) | copy-start | bytes 1572868
  147.7 8.2 %collective-permute-start.23 = (f32[32,1024]{1,0:T(8,128)S(1)}, f32[32,1024]{1,0:T(8,128)S(1)}, u32[]{:S(2)}, u32[]{:S(2)}) collective-permute-start(f32[32,1024]{1,0:T(8,128)S(1)} %get-tuple-element.67), channel_id=1, source_target_pairs={{0,8},{4,12},{8,0},{12,4},{16,24},{20,28},{24,16},{28,20},{1,9},{5... | collective-permute-start | bytes 393224 | tf_op jit(solution)/shard_map/ppermute | solution.py:212
  149.8 8.1 %collective-permute-start.24 = (f32[32,1024]{1,0:T(8,128)S(1)}, f32[32,1024]{1,0:T(8,128)S(1)}, u32[]{:S(2)}, u32[]{:S(2)}) collective-permute-start(f32[32,1024]{1,0:T(8,128)S(1)} %get-tuple-element.69), channel_id=1, source_target_pairs={{0,16},{4,20},{8,24},{12,28},{16,0},{20,4},{24,8},{28,12},{1,17},{... | collective-permute-start | bytes 393224 | tf_op jit(solution)/shard_map/ppermute | solution.py:212
  149.8 8.1 %collective-permute-start.25 = (f32[32,1024]{1,0:T(8,128)S(1)}, f32[32,1024]{1,0:T(8,128)S(1)}, u32[]{:S(2)}, u32[]{:S(2)}) collective-permute-start(f32[32,1024]{1,0:T(8,128)S(1)} %get-tuple-element.68), channel_id=1, source_target_pairs={{0,24},{4,28},{8,16},{12,20},{16,8},{20,12},{24,0},{28,4},{1,25},{... | collective-permute-start | bytes 393224 | tf_op jit(solution)/shard_map/ppermute | solution.py:212
  151.3 6.6 %collective-permute-start.16 = (f32[32,1024]{1,0:T(8,128)S(1)}, f32[32,1024]{1,0:T(8,128)S(1)}, u32[]{:S(2)}, u32[]{:S(2)}) collective-permute-start(f32[32,1024]{1,0:T(8,128)S(1)} %copy-done.11), channel_id=1, source_target_pairs={{0,1},{1,0},{2,3},{3,2},{4,5},{5,4},{6,7},{7,6},{8,9},{9,8},{10,11... | collective-permute-start | bytes 393224 | tf_op jit(solution)/shard_map/ppermute | solution.py:217
  151.3 10.1 %collective-permute-start.21 = (f32[32,1024]{1,0:T(8,128)S(1)}, f32[32,1024]{1,0:T(8,128)S(1)}, u32[]{:S(2)}, u32[]{:S(2)}) collective-permute-start(f32[32,1024]{1,0:T(8,128)S(1)} %fusion.3), channel_id=1, source_target_pairs={{0,2},{2,0},{1,3},{3,1},{4,6},{6,4},{5,7},{7,5},{8,10},{10,8},{9,1... | collective-permute-start | bytes 393224 | tf_op jit(solution)/shard_map/ppermute | solution.py:217
  161.5 6.8 %collective-permute-start.26 = (f32[32,1024]{1,0:T(8,128)S(1)}, f32[32,1024]{1,0:T(8,128)S(1)}, u32[]{:S(2)}, u32[]{:S(2)}) collective-permute-start(f32[32,1024]{1,0:T(8,128)S(1)} %fusion.1), channel_id=1, source_target_pairs={{0,3},{3,0},{1,2},{2,1},{4,7},{7,4},{5,6},{6,5},{8,11},{11,8},{9,1... | collective-permute-start | bytes 393224 | tf_op jit(solution)/shard_map/ppermute | solution.py:217
